TPU v7x, 32 devices: a whole 2x2x4 slice. The times are simulated.
32 devices in a mesh: ctx: 8 (over z, x), ch: 4 (over y, core).
Axes of the slice: x: 2, y: 2, z: 4, core: 2. Of those that a mesh axis runs over, the one named last changes fastest.
Arguments:
- query_proj: bfloat16 [8192, 1024], P('ch', 'ctx'), may hold values from -6 to 6
- key_proj: bfloat16 [8192, 1024], P('ch', 'ctx'), may hold values from -6 to 6
- value_proj: bfloat16 [8192, 1024], P('ch', 'ctx'), may hold values from -6 to 6
- cotangent: bfloat16 [8192, 1024], P('ch', 'ctx'), may hold values from -0.046875 to 0.046875
- positions: int32 [1024], P('ctx'), may hold values from 0 to 1023, as said below
- group_of: int32 [8192], replicated, may hold values from 0 to 511, as said below
- decay_rates: float32 [512, 16], replicated, may hold values from 9.765625e-05 to 0.03
- residues: float32 [512, 16], replicated, may hold values from -1.5 to 1.5
Outputs:
- output: bfloat16 [8192, 1024], P('ch', 'ctx')
- filter_grad: float32 [512, 1024], P('ch', 'ctx')
Inputs may be any that keep to these rules, and one draw needn't show every extreme that they name: positions is a permutation of the sequence positions; every aligned run of 64 stored tokens holds consecutive positions that start at a multiple of 64. `group_of`: every group has exactly 16 channels; each aligned block of 2048 channels holds exactly 512 channels of the groups of each aligned block of 128 groups.
All inputs are finite; a program needn't handle non-finite values.
Results may differ from a plain program's by a relative error of at most 0.0058.
Values may be sent and summed in bfloat16 or wider, within the bound.
No kernel may reach another device: no remote copies, remote signals or barrier semaphores. Data moves between devices by JAX's collectives and lax.ppermute only.
A program may use at most 64 MiB of HBM per device.

v0:
```python
import functools
import math

import jax
import jax.numpy as jnp
from jax import lax
from jax.experimental import pallas as pl
from jax.experimental.pallas import tpu as pltpu
from jax.sharding import PartitionSpec as P

F32 = jnp.float32
BF16 = jnp.bfloat16
I32 = jnp.int32
LANES = 128
VMEM_LIMIT = 48 * 1024 * 1024


def product(form, left, right):
    return jnp.einsum(form, left, right, precision=lax.Precision.HIGHEST)


def split_rows(extent):
    chosen = 2
    for divisor in range(2, math.isqrt(extent) + 1, 2):
        if extent % divisor == 0:
            chosen = divisor
    return chosen


def dft_tables(row_count, col_count, extent):
    row_index = jnp.arange(row_count, dtype=jnp.int32)
    col_index = jnp.arange(col_count, dtype=jnp.int32)

    def angles(left_index, right_index, modulus):
        phase = left_index[:, None] * right_index[None, :] % modulus
        return phase.astype(jnp.float32) * (2.0 * math.pi / modulus)

    row_angle = angles(row_index, row_index, row_count)
    col_angle = angles(col_index, col_index, col_count)
    twist_angle = angles(row_index, col_index, extent)
    return (
        jnp.cos(row_angle),
        jnp.sin(row_angle),
        jnp.cos(col_angle),
        jnp.sin(col_angle),
        jnp.cos(twist_angle),
        jnp.sin(twist_angle),
    )


def forward_transform(signal, tables, row_count, col_count):
    row_cos, row_sin, col_cos, col_sin, twist_cos, twist_sin = tables
    folded = signal.reshape(signal.shape[0], row_count // 2, col_count)
    mid_real = product("ka,cab->ckb", row_cos[:, : row_count // 2], folded)
    mid_imag = -product("ka,cab->ckb", row_sin[:, : row_count // 2], folded)
    turned_real = mid_real * twist_cos + mid_imag * twist_sin
    turned_imag = mid_imag * twist_cos - mid_real * twist_sin
    spec_real = product("ckb,bm->ckm", turned_real, col_cos) + product(
        "ckb,bm->ckm", turned_imag, col_sin
    )
    spec_imag = product("ckb,bm->ckm", turned_imag, col_cos) - product(
        "ckb,bm->ckm", turned_real, col_sin
    )
    return (spec_real, spec_imag)


def inverse_transform(spec_real, spec_imag, tables, row_count, col_count):
    row_cos, row_sin, col_cos, col_sin, twist_cos, twist_sin = tables
    mid_real = product("ckm,bm->ckb", spec_real, col_cos) - product(
        "ckm,bm->ckb", spec_imag, col_sin
    )
    mid_imag = product("ckm,bm->ckb", spec_imag, col_cos) + product(
        "ckm,bm->ckb", spec_real, col_sin
    )
    turned_real = mid_real * twist_cos - mid_imag * twist_sin
    turned_imag = mid_imag * twist_cos + mid_real * twist_sin
    folded = product("ak,ckb->cab", row_cos[: row_count // 2, :], turned_real) - product(
        "ak,ckb->cab", row_sin[: row_count // 2, :], turned_imag
    )
    return folded.reshape(spec_real.shape[0], -1) / float(row_count * col_count)


def spectra(gated_seq, weighted_seq, chan_groups, decay_rates, residues, seq_length):
    extent = 2 * seq_length
    row_count = split_rows(extent)
    col_count = extent // row_count
    decay_rows = decay_rates[chan_groups]
    gain_rows = residues[chan_groups]
    tap_index = jnp.arange(seq_length, dtype=jnp.float32)
    coefs = gain_rows * jnp.sqrt(2.0 * decay_rows)
    filters = jnp.sum(coefs[:, :, None] * jnp.exp(-decay_rows[:, :, None] * tap_index), axis=1)
    tables = dft_tables(row_count, col_count, extent)
    gated_real, gated_imag = forward_transform(
        gated_seq.astype(jnp.float32), tables, row_count, col_count
    )
    filter_real, filter_imag = forward_transform(filters, tables, row_count, col_count)
    weight_real, weight_imag = forward_transform(
        weighted_seq.astype(jnp.float32), tables, row_count, col_count
    )
    convolved = inverse_transform(
        filter_real * gated_real - filter_imag * gated_imag,
        filter_real * gated_imag + filter_imag * gated_real,
        tables,
        row_count,
        col_count,
    )
    lagged = inverse_transform(
        weight_real * gated_real + weight_imag * gated_imag,
        weight_imag * gated_real - weight_real * gated_imag,
        tables,
        row_count,
        col_count,
    )
    return (convolved, lagged)


def general_way(
    query_proj, key_proj, value_proj, cotangent, positions, group_of, decay_rates, residues
):
    ctx_count = lax.axis_size("ctx")
    ch_count = lax.axis_size("ch")
    ctx_rank = lax.axis_index("ctx")
    ch_rank = lax.axis_index("ch")
    local_channels, local_tokens = query_proj.shape
    half_run = local_tokens // 2
    run_count = 2 * ctx_count
    seq_length = local_tokens * ctx_count
    per_device = local_channels // ctx_count
    groups_total = decay_rates.shape[0]
    gated = (key_proj.astype(jnp.float32) * value_proj.astype(jnp.float32)).astype(jnp.bfloat16)
    weighted = (cotangent.astype(jnp.float32) * query_proj.astype(jnp.float32)).astype(jnp.bfloat16)
    run_ids = jnp.stack([positions[0], positions[half_run]]) // half_run
    all_runs = lax.all_to_all(
        jnp.broadcast_to(run_ids[None, :], (ctx_count, 2)),
        "ctx",
        split_axis=0,
        concat_axis=0,
        tiled=True,
    ).reshape(run_count)
    source_run = (
        jnp.zeros((run_count,), jnp.int32).at[all_runs].set(jnp.arange(run_count, dtype=jnp.int32))
    )

    def to_sequence(stored):
        return stored.reshape(per_device, run_count, half_run)[:, source_run, :].reshape(
            per_device, seq_length
        )

    shard_groups = lax.dynamic_slice_in_dim(group_of, ch_rank * local_channels, local_channels)
    gated_cols, weighted_cols = (
        lax.all_to_all(gated, "ctx", split_axis=0, concat_axis=1, tiled=True),
        lax.all_to_all(weighted, "ctx", split_axis=0, concat_axis=1, tiled=True),
    )
    first_channel = ch_rank * local_channels + ctx_rank * per_device
    chan_groups = lax.dynamic_slice_in_dim(group_of, first_channel, per_device)
    convolved, lagged = spectra(
        to_sequence(gated_cols),
        to_sequence(weighted_cols),
        chan_groups,
        decay_rates,
        residues,
        seq_length,
    )
    ordered = convolved.astype(jnp.bfloat16).reshape(per_device, run_count, half_run)[
        :, all_runs, :
    ]
    conv_tokens = lax.all_to_all(
        ordered.reshape(per_device, seq_length), "ctx", split_axis=1, concat_axis=0, tiled=True
    )
    output = (query_proj.astype(jnp.float32) * conv_tokens.astype(jnp.float32)).astype(jnp.bfloat16)
    lag_rows = lax.all_to_all(lagged, "ctx", split_axis=1, concat_axis=0, tiled=True)
    select_all = (
        jnp.arange(groups_total, dtype=jnp.int32)[:, None] == shard_groups[None, :]
    ).astype(jnp.float32)
    partial = jnp.dot(
        select_all, lag_rows, precision=lax.Precision.HIGHEST, preferred_element_type=jnp.float32
    ).reshape(ch_count, groups_total // ch_count, local_tokens)
    filter_grad = jnp.sum(
        lax.all_to_all(partial, "ch", split_axis=0, concat_axis=0, tiled=True), axis=0
    )
    return (output, filter_grad)


def iota(shape, dim):
    return lax.broadcasted_iota(I32, shape, dim)


def hot(flags):
    return jnp.where(flags, 1.0, 0.0).astype(BF16)


def dot(left, right):
    return jnp.dot(left, right, preferred_element_type=F32)


def dot_lanes(left, right):
    return lax.dot_general(left, right, (((1,), (1,)), ((), ())), preferred_element_type=F32)


def two_terms(values):
    high = values.astype(BF16)
    return high, (values - high.astype(F32)).astype(BF16)


class Sizes:
    def __init__(self, ctx, ch, channels, tokens, groups):
        self.ctx, self.ch = ctx, ch
        self.peers = ctx * ch
        self.channels = channels
        self.tokens = tokens
        self.run = tokens // 2
        self.runs = 2 * ctx
        self.groups = groups
        self.block = groups // ch
        self.each = self.block // self.peers
        self.own = groups // self.peers
        self.size = channels * ch // groups
        self.cap = 96
        powers = [self.block, max(self.each, 1), self.own, self.size]
        self.fits = (
            tokens == LANES
            and self.runs == 16
            and self.own == 16
            and self.size == 16
            and self.each * self.peers == self.block
            and self.each * 8 * self.run == 16 * LANES
            and ch == 4
            and channels % 2048 == 0
            and channels // self.peers <= 64
            and all(p & (p - 1) == 0 for p in powers)
        )

    def owner(self, group):
        return lax.shift_right_logical(group & (self.block - 1), self.each.bit_length() - 1)

    def place(self, group):
        block = lax.shift_right_logical(group, self.block.bit_length() - 1)
        return block * self.each + (group & (self.each - 1))


def running_counts(marks, upper):
    width = upper.shape[0]
    before, counts = jnp.zeros((marks.shape[0], 1), F32), []
    for start in range(0, marks.shape[1], width):
        part = marks[:, start : start + width]
        counts.append(dot(part, upper) + before)
        before = before + jnp.sum(part.astype(F32), axis=1, keepdims=True)
    return jnp.concatenate(counts, axis=1), before


def upper_ones(width):
    return hot(iota((width, width), 0) < iota((width, width), 1))


def pack_kernel(
    sizes, runs_ref, group_ref, key_ref, value_ref, cot_ref, query_ref, out_ref, dest_ref, data
):
    part = out_ref.shape[0]

    @pl.when(pl.program_id(0) == 0)
    def _():
        owner = sizes.owner(group_ref[...])
        marks = iota((sizes.peers, sizes.channels), 0) == owner
        counts, _ = running_counts(hot(marks), upper_ones(256))
        slot = jnp.sum(jnp.where(marks, counts, 0.0), axis=0, keepdims=True).astype(I32)
        dest_ref[0:1, :] = jnp.where(slot < sizes.cap - 1, owner * sizes.cap + slot, -1)
        dest_ref[1:2, :] = owner
        dest_ref[2:3, :] = slot
        dest_ref[3:8, :] = jnp.zeros((5, sizes.channels), I32)
        data[:, :LANES] = (key_ref[...].astype(F32) * value_ref[...].astype(F32)).astype(BF16)
        data[:, LANES:] = (cot_ref[...].astype(F32) * query_ref[...].astype(F32)).astype(BF16)

    dest = dest_ref[0:1, :]
    lane = iota((1, 2 * LANES), 1)
    run_row = jnp.where(lane < LANES, runs_ref[0], runs_ref[1]).astype(F32)
    row = iota((sizes.cap, 1), 0)

    def one_peer(index, carry):
        base = (pl.program_id(0) * part + index) * sizes.cap
        chosen = hot(iota((sizes.cap, sizes.channels), 0) == dest - base)
        rows = dot(chosen, data[...])
        out_ref[index] = jnp.where(row == sizes.cap - 1, run_row, rows).astype(BF16)
        return carry

    lax.fori_loop(0, part, one_peer, 0)


def pack(sizes, run_ids, shard_groups, key_proj, value_proj, cotangent, query_proj):
    part = 8
    whole = lambda shape: pl.BlockSpec(shape, lambda step: (0, 0))
    rows = (sizes.channels, sizes.tokens)
    return pl.pallas_call(
        functools.partial(pack_kernel, sizes),
        grid=(sizes.peers // part,),
        in_specs=[
            pl.BlockSpec(memory_space=pltpu.SMEM),
            whole((1, sizes.channels)),
            whole(rows),
            whole(rows),
            whole(rows),
            whole(rows),
        ],
        out_specs=[
            pl.BlockSpec((part, sizes.cap, 2 * LANES), lambda step: (step, 0, 0)),
            whole((8, sizes.channels)),
        ],
        out_shape=[
            jax.ShapeDtypeStruct((sizes.peers, sizes.cap, 2 * LANES), BF16),
            jax.ShapeDtypeStruct((8, sizes.channels), I32),
        ],
        scratch_shapes=[pltpu.VMEM((sizes.channels, 2 * LANES), BF16)],
        compiler_params=pltpu.CompilerParams(vmem_limit_bytes=VMEM_LIMIT),
        name="pack_rows",
    )(run_ids, shard_groups, key_proj, value_proj, cotangent, query_proj)


def index_kernel(
    sizes, me_ref, group_ref, rate_ref, gain_ref, into_ref, back_ref, over_ref, table_ref
):
    me = me_ref[0]
    upper = upper_ones(256)
    group = group_ref[...]
    owner, place = sizes.owner(group), sizes.place(group)
    most = jnp.zeros((sizes.peers, 1), F32)
    for source in range(sizes.ch):
        marks = iota((sizes.peers, sizes.channels), 0) == owner[source : source + 1]
        most = jnp.maximum(most, jnp.sum(jnp.where(marks, 1.0, 0.0), axis=1, keepdims=True))
    over_ref[...] = jnp.broadcast_to(jnp.max(most, axis=0, keepdims=True), (8, LANES)).astype(I32)

    earlier = jnp.zeros((sizes.own, 1), F32)
    into = jnp.zeros((256, sizes.ch * sizes.cap), F32)
    for source in range(sizes.ch):
        mine = owner[source : source + 1] == me
        where = jnp.where(mine, place[source : source + 1], -1)
        marks = iota((sizes.own, sizes.channels), 0) == where
        counts, totals = running_counts(hot(marks), upper)
        slot = jnp.sum(counts, axis=0, keepdims=True).astype(I32)
        nth = jnp.sum(jnp.where(marks, counts + earlier, 0.0), axis=0, keepdims=True).astype(I32)
        earlier = earlier + totals
        row = jnp.where(mine, where * sizes.size + nth, -1)
        column = jnp.where(mine & (slot < sizes.cap - 1), slot, -1)
        to_row = hot(iota((256, sizes.channels), 0) == row)
        to_column = hot(iota((LANES, sizes.channels), 0) == column)
        found = dot_lanes(to_row, to_column).astype(BF16)
        back_ref[:, source * LANES : (source + 1) * LANES] = found
        shape = (LANES, sizes.ch * sizes.cap)
        moved = hot(
            (iota(shape, 1) == iota(shape, 0) + source * sizes.cap)
            & (iota(shape, 0) < sizes.cap)
        )
        into = into + dot(found, moved)
    into_ref[...] = into.astype(BF16)

    rate, gain = rate_ref[...], gain_ref[...]
    step = iota((256, sizes.run), 1).astype(F32)
    high, low = two_terms(gain * jnp.exp(-rate * step))
    table_ref[...] = jnp.concatenate([high, low], axis=1)


def index(sizes, me, all_groups, rate_col, gain_col):
    return pl.pallas_call(
        functools.partial(index_kernel, sizes),
        in_specs=[pl.BlockSpec(memory_space=pltpu.SMEM)]
        + [pl.BlockSpec(memory_space=pltpu.VMEM)] * 3,
        out_shape=[
            jax.ShapeDtypeStruct((256, sizes.ch * sizes.cap), BF16),
            jax.ShapeDtypeStruct((256, sizes.ch * LANES), BF16),
            jax.ShapeDtypeStruct((8, LANES), I32),
            jax.ShapeDtypeStruct((256, 2 * sizes.run), BF16),
        ],
        compiler_params=pltpu.CompilerParams(vmem_limit_bytes=VMEM_LIMIT),
        cost_estimate=pl.CostEstimate(flops=2 * 10**9, bytes_accessed=10**6, transcendentals=0),
        name="index_rows",
    )(me, all_groups, rate_col, gain_col)


def local_kernel(
    sizes, group_ref, param_ref, key_ref, value_ref, conv_ref, decay_ref, params, turned
):
    modes = param_ref.shape[0] // 2
    blocks = sizes.channels // LANES
    exact = param_ref[...]
    high, rest = two_terms(exact)
    low, last = two_terms(exact - high.astype(F32) - rest.astype(F32))
    stacked = jnp.concatenate([high, rest, low], axis=0)
    rows = 2 * modes
    for start in range(0, sizes.channels, 256):
        chosen = hot(iota((sizes.groups, 256), 0) == group_ref[:, start : start + 256])
        found = dot(stacked, chosen)
        found = found[:rows] + found[rows : 2 * rows] + found[2 * rows :]
        for half in range(2):
            block = start // LANES + half
            params[block * rows : (block + 1) * rows, :] = found[
                :, half * LANES : (half + 1) * LANES
            ]

    def turn(block, carry):
        at = pl.ds(pl.multiple_of(block * LANES, LANES), LANES)
        gated = (key_ref[at, :].astype(F32) * value_ref[at, :].astype(F32)).astype(BF16)
        turned[pl.ds(block, sizes.tokens, stride=blocks), :] = gated.astype(F32).T
        return carry

    lax.fori_loop(0, blocks, turn, 0)
    for first in range(0, blocks, 8):
        decays, gains = [], []
        for mode in range(modes):
            rate = params[pl.ds(first * rows + mode, 8, stride=rows), :]
            gains.append(params[pl.ds(first * rows + modes + mode, 8, stride=rows), :])
            decays.append(jnp.exp(-rate))
            decay_ref[mode * blocks + first : mode * blocks + first + 8, :] = decays[-1]
        for half in range(2):

            def step(token, states):
                at = (half * sizes.run + token) * blocks + first
                at = pl.ds(pl.multiple_of(at, 8), 8)
                value = turned[at, :]
                states = [a * s + c * value for a, c, s in zip(decays, gains, states)]
                conv_ref[at, :] = tree_sum(states)
                return states

            lax.fori_loop(0, sizes.run, step, [jnp.zeros((8, LANES), F32)] * modes)


def tree_sum(terms):
    while len(terms) > 1:
        terms = [
            terms[i] + terms[i + 1] if i + 1 < len(terms) else terms[i]
            for i in range(0, len(terms), 2)
        ]
    return terms[0]


def local(sizes, shard_groups, params, key_proj, value_proj):
    modes = params.shape[0] // 2
    blocks = sizes.channels // LANES
    return pl.pallas_call(
        functools.partial(local_kernel, sizes),
        in_specs=[pl.BlockSpec(memory_space=pltpu.VMEM)] * 4,
        out_shape=[
            jax.ShapeDtypeStruct((sizes.tokens * blocks, LANES), F32),
            jax.ShapeDtypeStruct((modes * blocks, LANES), F32),
        ],
        scratch_shapes=[
            pltpu.VMEM((blocks * 2 * modes, LANES), F32),
            pltpu.VMEM((sizes.tokens * blocks, LANES), F32),
        ],
        compiler_params=pltpu.CompilerParams(vmem_limit_bytes=VMEM_LIMIT),
        cost_estimate=pl.CostEstimate(flops=4 * 10**9, bytes_accessed=3 * 10**6, transcendentals=0),
        name="local_runs",
    )(shard_groups, params, key_proj, value_proj)


def owner_kernel(
    sizes,
    recv_ref,
    into_ref,
    back_ref,
    table_ref,
    leap_ref,
    out_ref,
    gated,
    weighted,
    states,
    sums,
    run_at,
):
    run, runs, own, size = sizes.run, sizes.runs, sizes.own, sizes.size
    rows = own * size
    lane = iota((rows, LANES), 1)
    mirror = hot(iota((LANES, LANES), 0) + iota((LANES, LANES), 1) == LANES - 1)
    weighted[runs : 2 * runs + 1] = jnp.zeros((runs + 1, rows, LANES), BF16)
    for source in range(sizes.ctx):
        tail = recv_ref[source * sizes.ch, sizes.cap - 16 : sizes.cap, :].astype(F32)
        ids = tail[15:16, :]
        first = jnp.max(ids[:, :LANES]).astype(I32)
        second = jnp.max(ids[:, LANES:]).astype(I32)
        run_at[2 * source] = first
        run_at[2 * source + 1] = second
        block = recv_ref[source * sizes.ch : (source + 1) * sizes.ch]
        block = block.reshape(sizes.ch * sizes.cap, 2 * LANES)
        found = dot(into_ref[...], block)
        mirrored = dot(found[:, :LANES].astype(BF16), mirror)
        swapped = pltpu.roll(mirrored, run, 1)
        gated[second] = jnp.where(lane < run, mirrored, swapped).astype(BF16)
        gated[first] = jnp.where(lane < run, swapped, mirrored).astype(BF16)
        value = found[:, LANES:]
        turned = pltpu.roll(value, run, 1).astype(BF16)
        value = value.astype(BF16)
        weighted[first + 1, :, :run] = value[:, :run]
        weighted[first, :, run:] = turned[:, run:]
        weighted[second + 1, :, :run] = turned[:, :run]
        weighted[second, :, run:] = value[:, run:]

    modes = states.shape[1]
    group_lane = lax.shift_right_logical(iota((modes, rows), 1), size.bit_length() - 1)
    carried = jnp.zeros((modes, rows), F32)
    leap = leap_ref[...]
    for at in range(runs):
        states[at] = carried
        if at + 1 < runs:
            ends = dot_lanes(table_ref[...], gated[at])
            total = jnp.zeros((modes, rows), F32)
            for group in range(own):
                piece = ends[group * modes : (group + 1) * modes]
                total = total + jnp.where(group_lane == group, piece, 0.0)
            carried = carried * leap + total

    seq = run * runs

    def one_group(group, carry):
        at = pl.ds(pl.multiple_of(group * size, size), size)
        left = gated[:, at, :].reshape(runs * size, LANES).T[:run]
        right = jnp.concatenate(
            [
                weighted[1 + lag : 1 + lag + runs, at, :].reshape(runs * size, LANES)
                for lag in range(0, runs, 2)
            ],
            axis=1,
        )
        gram = jnp.concatenate([dot(left, right), jnp.zeros((run, LANES), F32)], axis=1)
        skewed = pltpu.roll(gram, seq + LANES - (run - 1), 1, stride=1, stride_axis=0)
        sums[pl.ds(group, 1), :] = jnp.sum(skewed, axis=0, keepdims=True)[:, :seq]
        return carry

    lax.fori_loop(0, own, one_group, 0)

    each = sizes.each
    quarter = LANES // 4
    out_lane = iota((32, LANES), 1)
    for target in range(sizes.ctx):
        pair = jnp.concatenate(
            [states[run_at[2 * target]], states[run_at[2 * target + 1]]], axis=0
        )
        sent = dot(pair.astype(BF16), back_ref[...])
        lags = sums[:, target * LANES : (target + 1) * LANES]
        high = lags.astype(BF16).astype(F32)
        low = lags - high
        moved = [
            [pltpu.roll(term, (7 * quarter - q * quarter) % LANES, 1) for q in range(4)]
            for term in (high, low)
        ]
        for chan in range(sizes.ch):
            lag_rows = jnp.concatenate(
                [part[chan * each : (chan + 1) * each] for term in moved for part in term], axis=0
            )
            mine = sent[:, chan * LANES : (chan + 1) * LANES]
            out_ref[target * sizes.ch + chan] = jnp.where(
                out_lane < 3 * quarter, mine, lag_rows
            ).astype(BF16)


def owner(sizes, recv, into, back, table, leap):
    rows = sizes.own * sizes.size
    modes = leap.shape[0]
    return pl.pallas_call(
        functools.partial(owner_kernel, sizes),
        in_specs=[pl.BlockSpec(memory_space=pltpu.VMEM)] * 5,
        out_shape=jax.ShapeDtypeStruct((sizes.peers, 2 * modes, LANES), BF16),
        scratch_shapes=[
            pltpu.VMEM((sizes.runs, rows, LANES), BF16),
            pltpu.VMEM((2 * sizes.runs + 1, rows, LANES), BF16),
            pltpu.VMEM((sizes.runs, modes, rows), F32),
            pltpu.VMEM((sizes.own, sizes.run * sizes.runs), F32),
            pltpu.SMEM((sizes.runs,), I32),
        ],
        compiler_params=pltpu.CompilerParams(vmem_limit_bytes=VMEM_LIMIT),
        name="owner_sums",
    )(recv, into, back, table, leap)


def finish_kernel(
    sizes, recv_ref, dest_ref, conv_ref, decay_ref, query_ref, out_ref, grad_ref, found, total
):
    blocks = sizes.channels // LANES
    rows = recv_ref.shape[1]
    modes = rows // 2
    everything = recv_ref[...].reshape(sizes.peers * rows, LANES)

    def fetch(part, carry):
        at = pl.ds(pl.multiple_of(part * 256, 256), 256)
        owner, slot = dest_ref[1:2, at], dest_ref[2:3, at]
        chosen = hot(iota((LANES, 256), 0) == slot)
        picked = dot(everything, chosen)
        mine = jnp.zeros((rows, 256), F32)
        for peer in range(sizes.peers):
            mine = mine + jnp.where(owner == peer, picked[peer * rows : (peer + 1) * rows], 0.0)
        for half in range(2):
            start = pl.multiple_of((2 * part + half) * rows, rows)
            found[pl.ds(start, rows), :] = mine[:, half * LANES : (half + 1) * LANES]
        return carry

    lax.fori_loop(0, sizes.channels // 256, fetch, 0)
    for first in range(0, blocks, 8):
        decays = [
            decay_ref[mode * blocks + first : mode * blocks + first + 8, :]
            for mode in range(modes)
        ]
        for half in range(2):
            states = [
                found[pl.ds(first * rows + half * modes + mode, 8, stride=rows), :]
                for mode in range(modes)
            ]

            def step(token, states):
                at = (half * sizes.run + token) * blocks + first
                at = pl.ds(pl.multiple_of(at, 8), 8)
                states = [a * s for a, s in zip(decays, states)]
                total[at, :] = conv_ref[at, :] + tree_sum(states)
                return states

            lax.fori_loop(0, sizes.run, step, states)

    def turn(block, carry):
        at = pl.ds(pl.multiple_of(block * LANES, LANES), LANES)
        conv = total[pl.ds(block, sizes.tokens, stride=blocks), :].T.astype(BF16)
        out_ref[at, :] = (query_ref[at, :].astype(F32) * conv.astype(F32)).astype(BF16)
        return carry

    lax.fori_loop(0, blocks, turn, 0)

    each, quarter = sizes.each, LANES // 4
    high_low = recv_ref[...].astype(F32)
    terms = []
    lane_part = lax.shift_right_logical(iota((sizes.peers * 16, LANES), 1), 5)
    row = iota((sizes.peers * 16, LANES), 0)
    row_part = lax.shift_right_logical(row & 15, each.bit_length() - 1)
    for term in range(2):
        piece = high_low[:, term * 16 : (term + 1) * 16, :].reshape(sizes.peers * 16, LANES)
        placed = jnp.zeros((sizes.peers * 16, LANES), F32)
        for part in range(4):
            moved = pltpu.roll(piece, (part * quarter + quarter) % LANES, 1)
            placed = jnp.where((row_part == part) & (lane_part == part), moved, placed)
        terms.append(placed.astype(BF16))
    shape = (sizes.block, sizes.peers * 16)
    to, come = iota(shape, 0), iota(shape, 1)
    bits = each.bit_length() - 1
    chosen = hot(
        (lax.shift_right_logical(to, bits) == lax.shift_right_logical(come, 4))
        & ((to & (each - 1)) == (come & (each - 1)))
    )
    grad_ref[...] = dot(chosen, terms[0]) + dot(chosen, terms[1])


def finish(sizes, recv, dest, conv, decay, query_proj):
    blocks = sizes.channels // LANES
    return pl.pallas_call(
        functools.partial(finish_kernel, sizes),
        in_specs=[pl.BlockSpec(memory_space=pltpu.VMEM)] * 5,
        out_shape=[
            jax.ShapeDtypeStruct((sizes.channels, sizes.tokens), BF16),
            jax.ShapeDtypeStruct((sizes.block, LANES), F32),
        ],
        scratch_shapes=[
            pltpu.VMEM((blocks * recv.shape[1], LANES), F32),
            pltpu.VMEM((sizes.tokens * blocks, LANES), F32),
        ],
        compiler_params=pltpu.CompilerParams(vmem_limit_bytes=VMEM_LIMIT),
        name="finish_rows",
    )(recv, dest, conv, decay, query_proj)


def exchange(blocks):
    return lax.all_to_all(blocks, ("ctx", "ch"), split_axis=0, concat_axis=0, tiled=True)


def owners_way(sizes, args):
    query_proj, key_proj, value_proj, cotangent, positions, group_of, decay_rates, residues = args
    ch_rank = lax.axis_index("ch")
    me = lax.axis_index("ctx") * sizes.ch + ch_rank
    run_ids = jnp.stack([positions[0], positions[sizes.run]]) // sizes.run
    all_groups = group_of.reshape(sizes.ch, sizes.channels)
    shard_groups = lax.dynamic_slice_in_dim(all_groups, ch_rank, 1)
    sent, dest = pack(sizes, run_ids, shard_groups, key_proj, value_proj, cotangent, query_proj)
    recv = exchange(sent)

    gains = residues * jnp.sqrt(2.0 * decay_rates)
    params = jnp.concatenate([decay_rates, gains], axis=1).T
    conv, decay = local(sizes, shard_groups, params, key_proj, value_proj)
    modes = decay_rates.shape[1]

    def owned(values):
        split = values.reshape(sizes.ch, sizes.peers, sizes.each, modes)
        mine = lax.dynamic_index_in_dim(split, me, 1, keepdims=False)
        return mine.reshape(sizes.own, modes)

    own_rates, own_gains = owned(decay_rates), owned(gains)
    leap = jnp.repeat(jnp.exp(-float(sizes.run) * own_rates.T), sizes.size, axis=1)
    into, back, most, table = index(
        sizes,
        me.reshape(1).astype(I32),
        all_groups,
        own_rates.reshape(-1, 1),
        own_gains.reshape(-1, 1),
    )

    def fast(recv, into, back, table, leap, dest, conv, decay, *args):
        returned = exchange(owner(sizes, recv, into, back, table, leap))
        return tuple(finish(sizes, returned, dest, conv, decay, args[0]))

    def slow(recv, into, back, table, leap, dest, conv, decay, *args):
        return general_way(*args)

    return lax.cond(
        most[0, 0] <= sizes.cap - 1,
        fast,
        slow,
        recv,
        into,
        back,
        table,
        leap,
        dest,
        conv,
        decay,
        *args,
    )


def shards(*args):
    sizes = Sizes(
        lax.axis_size("ctx"), lax.axis_size("ch"), *args[0].shape, args[6].shape[0]
    )
    if not sizes.fits:
        return general_way(*args)
    return owners_way(sizes, args)


def solution(mesh):
    placed = (
        P("ch", "ctx"),
        P("ch", "ctx"),
        P("ch", "ctx"),
        P("ch", "ctx"),
        P("ctx"),
        P(),
        P(),
        P(),
    )
    return jax.shard_map(
        shards,
        mesh=mesh,
        in_specs=placed,
        out_specs=(P("ch", "ctx"), P("ch", "ctx")),
        check_vma=False,
    )
```

profile of v0, /device:TPU:1, one launch (start us, length us, event | category | flops | bytes accessed | tf_op | source)
XLA Modules:
  0.0 95.6 jit_solution(3531864820384831810)
XLA Ops:
  0.6 0.8 reshape.240.group_ref
  1.4 1.3 %fusion.267 = (s32[1]{0:T(128)}, s32[1]{0:T(128)}) fusion(s32[128]{0:T(128)} %param.14), kind=kLoop, calls=%fused_computation.289 | loop fusion | bytes 16 | tf_op jit(solution)/shard_map/slice | solution.py:670
  2.7 1.4 %and_select_fusion.1.runs_ref = s32[2]{0:T(128)S(1)} fusion(s32[1]{0:T(128)} %get-tuple-element.178, s32[1]{0:T(128)} %get-tuple-element.177), kind=kLoop, calls=%fused_computation.280 | loop fusion | flops 32 | bytes 16 | tf_op jit(solution)/shard_map/jit(floor_divide)/jit(_where)/select_n | solution.py:670
  4.1 13.2 %pack_rows.1 = (bf16[32,96,256]{2,1,0:T(8,128)(2,1)}, s32[8,2048]{1,0:T(8,128)}) custom-call(s32[2]{0:T(128)S(1)} %and_select_fusion.1.runs_ref, s32[1,2048]{1,0:T(1,128)S(1)} %constant_dynamic-slice_fusion.group_ref, bf16[2048,128]{1,0:T(8,128)(2,1)} %key_ref.3, bf16[2048,128]{1,0:T(8,128)(2,1)} %value_ref.3, bf16[2048,128]{1,0:T(8,128)(2,1)} %cot_ref.1, ...), custom_call_target="tpu_custom_call" | custom-call | tf_op jit(solution)/shard_map/pack_rows/pallas_call | solution.py:292
  17.3 7.1 %all-to-all-start.7 = ((bf16[32,96,256]{2,1,0:T(8,128)(2,1)}), bf16[32,96,256]{2,1,0:T(8,128)(2,1)S(1)}, u32[]{:S(2)}, u32[]{:S(2)}) async-start(bf16[32,96,256]{2,1,0:T(8,128)(2,1)} %get-tuple-element.68), calls=%async_computation.7 | async-start | bytes 3145728 | tf_op jit(solution)/shard_map/all_to_all | solution.py:663
  24.5 0.0 copy-done.10
  24.5 0.1 copy.266
  24.6 0.1 copy.267
  24.8 0.1 reshape_reshape.9.gain_ref
  24.9 0.1 reshape_reshape.8.rate_ref
  25.0 0.0 copy-start.6
  25.0 0.0 copy-start.7
  25.0 4.2 %index_rows.1 = (bf16[256,384]{1,0:T(8,128)(2,1)}, bf16[256,512]{1,0:T(8,128)(2,1)S(1)}, s32[8,128]{1,0:T(8,128)S(1)}, bf16[256,128]{1,0:T(8,128)(2,1)}) custom-call(s32[1]{0:T(128)} %bitcast.46.me_ref, s32[4,2048]{1,0:T(4,128)S(1)} %reshape.240.group_ref, f32[256,1]{1,0:T(8,128)S(1)} %reshape_reshape.8.rate_ref, f32[256,1]{1,0:T(8,128)S(1)} %reshape_reshape.9.gain_ref), custom_call_target="tpu_custom_call" | custom-call | flops 2000000000 | bytes 1000000 | tf_op jit(solution)/shard_map/index_rows/pallas_call | solution.py:361
  29.3 0.5 slice.45
  30.5 0.0 copy-start.3
  30.5 0.0 copy-start.13
  30.5 0.0 copy-start.15
  30.5 6.7 %local_runs.1 = (f32[2048,128]{1,0:T(8,128)}, f32[256,128]{1,0:T(8,128)}) custom-call(s32[1,2048]{1,0:T(1,128)S(1)} %constant_dynamic-slice_fusion.group_ref, f32[32,512]{1,0:T(8,128)S(1)} %maximum_bitcast_fusion.param_ref, bf16[2048,128]{1,0:T(8,128)(2,1)S(1)} %copy-done.6, bf16[2048,128]{1,0:T(8,128)(2,1)S(1)} %copy-done.7), custom_call_target="tpu_custom_call" | custom-call | flops 4000000000 | bytes 3000000 | tf_op jit(solution)/shard_map/local_runs/pallas_call | solution.py:436
  37.2 24.1 %all-to-all-done.7 = bf16[32,96,256]{2,1,0:T(8,128)(2,1)S(1)} async-done(((bf16[32,96,256]{2,1,0:T(8,128)(2,1)}), bf16[32,96,256]{2,1,0:T(8,128)(2,1)S(1)}, u32[]{:S(2)}, u32[]{:S(2)}) %all-to-all-start.7) | async-done | bytes 1572896 | tf_op jit(solution)/shard_map/all_to_all | solution.py:663
  61.4 0.0 copy-done.3
  61.4 34.2 %conditional.1 = ((bf16[2048,128]{1,0:T(8,128)(2,1)}, f32[128,128]{1,0:T(8,128)})) conditional(s32[]{:T(128)} %bitcast.49, (bf16[2048,128]{1,0:T(8,128)(2,1)S(1)}, s32[8192]{0:T(1024)}, f32[512,16]{0,1:T(8,128)S(1)}, f32[512,16]{0,1:T(8,128)S(1)}, bf16[2048,128]{1,0:T(8,128)(2,1)S(1)}, /*index=5*/bf16[2048,128]{1,0:T(8,128)(2,1)S(1)}, ...), branch_computations={%region_0.4_spmd, %region_4.5_spmd} | conditional | flops 10720338944 | bytes 259373696 | solution.py:703
  61.6 0.0 copy-start.5
  61.6 0.0 copy-start.9
  61.6 0.1 copy.272
  61.7 1.1 %copy-done.5 = bf16[32,96,256]{2,1,0:T(8,128)(2,1)} copy-done((bf16[32,96,256]{2,1,0:T(8,128)(2,1)}, bf16[32,96,256]{2,1,0:T(8,128)(2,1)S(1)}, u32[]{:S(2)}) %copy-start.5) | copy-done | bytes 1572888 | tf_op jit(solution)/shard_map/cond
  62.8 0.1 broadcast_in_dim.8
  62.9 0.1 reshape.233.leap_ref
  63.0 10.4 %owner_sums.1 = bf16[32,32,128]{2,1,0:T(8,128)(2,1)S(1)} custom-call(bf16[32,96,256]{2,1,0:T(8,128)(2,1)} %copy-done.5, bf16[256,384]{1,0:T(8,128)(2,1)} %get-tuple-element.49.into_ref, bf16[256,512]{1,0:T(8,128)(2,1)S(1)} %get-tuple-element.50.back_ref, bf16[256,128]{1,0:T(8,128)(2,1)} %get-tuple-element.51.table_ref, f32[16,256]{1,0:T(8,128)S(1)} %reshape.233.leap_ref), custom_call_target="tpu_custom_call" | custom-call | tf_op jit(solution)/shard_map/cond/branch_1_fun/owner_sums/pallas_call | solution.py:555
  73.5 14.3 %all_to_all.68.recv_ref = bf16[32,32,128]{2,1,0:T(8,128)(2,1)S(1)} all-to-all(bf16[32,32,128]{2,1,0:T(8,128)(2,1)S(1)} %owner_sums.1), channel_id=1, replica_groups=mesh['ctx'=8,'ch'=4] {'ctx','ch'}, dimensions={0} | all-to-all | bytes 524288 | tf_op jit(solution)/shard_map/cond/branch_1_fun/all_to_all | solution.py:663
  87.8 0.0 copy-done.9
  87.8 0.0 copy-done.14
  87.8 7.7 %finish_rows.1 = (bf16[2048,128]{1,0:T(8,128)(2,1)}, f32[128,128]{1,0:T(8,128)}) custom-call(bf16[32,32,128]{2,1,0:T(8,128)(2,1)S(1)} %all_to_all.68.recv_ref, s32[8,2048]{1,0:T(8,128)S(1)} %copy-done.14, f32[2048,128]{1,0:T(8,128)S(1)} %copy-done.9, f32[256,128]{1,0:T(8,128)S(1)} %copy-done.11, bf16[2048,128]{1,0:T(8,128)(2,1)S(1)} %get-tuple-element.56.query_ref), custom_call_target="tpu_custom_call" | custom-call | tf_op jit(solution)/shard_map/cond/branch_1_fun/finish_rows/pallas_call | solution.py:646
  (16 shorter events, 0.1 us)
Async XLA Ops:
  17.3 7.1 %copy-start.10 = (f32[512,16]{0,1:T(8,128)S(1)}, f32[512,16]{0,1:T(8,128)}, u32[]{:S(2)}) copy-start(f32[512,16]{0,1:T(8,128)} %param.16) | copy-start | bytes 98308
  17.3 7.3 %copy-start.12 = (f32[512,16]{0,1:T(8,128)S(1)}, f32[512,16]{0,1:T(8,128)}, u32[]{:S(2)}) copy-start(f32[512,16]{0,1:T(8,128)} %param.17) | copy-start | bytes 98308
  17.3 44.0 %all-to-all-start.7 = ((bf16[32,96,256]{2,1,0:T(8,128)(2,1)}), bf16[32,96,256]{2,1,0:T(8,128)(2,1)S(1)}, u32[]{:S(2)}, u32[]{:S(2)}) async-start(bf16[32,96,256]{2,1,0:T(8,128)(2,1)} %get-tuple-element.68), calls=%async_computation.7 | async-start | bytes 3145728 | tf_op jit(solution)/shard_map/all_to_all | solution.py:663
  25.0 5.4 %copy-start.6 = (bf16[2048,128]{1,0:T(8,128)(2,1)S(1)}, bf16[2048,128]{1,0:T(8,128)(2,1)}, u32[]{:S(2)}) copy-start(bf16[2048,128]{1,0:T(8,128)(2,1)} %key_ref.3) | copy-start | bytes 1572868
  25.0 5.4 %copy-start.7 = (bf16[2048,128]{1,0:T(8,128)(2,1)S(1)}, bf16[2048,128]{1,0:T(8,128)(2,1)}, u32[]{:S(2)}) copy-start(bf16[2048,128]{1,0:T(8,128)(2,1)} %value_ref.3) | copy-start | bytes 1572868
  30.5 30.9 %copy-start.3 = (bf16[2048,128]{1,0:T(8,128)(2,1)S(1)}, bf16[2048,128]{1,0:T(8,128)(2,1)}, u32[]{:S(2)}) copy-start(bf16[2048,128]{1,0:T(8,128)(2,1)} %query_ref.1) | copy-start | bytes 1572868
  30.5 30.9 %copy-start.13 = (f32[512,16]{0,1:T(8,128)S(1)}, f32[512,16]{0,1:T(8,128)}, u32[]{:S(2)}) copy-start(f32[512,16]{0,1:T(8,128)} %param.17) | copy-start | bytes 98308
  30.5 30.9 %copy-start.15 = (s32[128]{0:T(128)S(1)}, s32[128]{0:T(128)}, u32[]{:S(2)}) copy-start(s32[128]{0:T(128)} %param.14) | copy-start | bytes 1540
  61.6 1.2 %copy-start.5 = (bf16[32,96,256]{2,1,0:T(8,128)(2,1)}, bf16[32,96,256]{2,1,0:T(8,128)(2,1)S(1)}, u32[]{:S(2)}) copy-start(bf16[32,96,256]{2,1,0:T(8,128)(2,1)S(1)} %get-tuple-element.48.recv_ref) | copy-start | bytes 4718596 | tf_op jit(solution)/shard_map/cond
  61.6 26.2 %copy-start.9 = (f32[2048,128]{1,0:T(8,128)S(1)}, f32[2048,128]{1,0:T(8,128)}, u32[]{:S(2)}) copy-start(f32[2048,128]{1,0:T(8,128)} %get-tuple-element.54.conv_ref) | copy-start | bytes 3145732 | tf_op jit(solution)/shard_map/cond
  62.9 24.9 %copy-start.11 = (f32[256,128]{1,0:T(8,128)S(1)}, f32[256,128]{1,0:T(8,128)}, u32[]{:S(2)}) copy-start(f32[256,128]{1,0:T(8,128)} %get-tuple-element.55.decay_ref) | copy-start | bytes 393220 | tf_op jit(solution)/shard_map/cond
  62.9 24.9 %copy-start.14 = (s32[8,2048]{1,0:T(8,128)S(1)}, s32[8,2048]{1,0:T(8,128)}, u32[]{:S(2)}) copy-start(s32[8,2048]{1,0:T(8,128)} %get-tuple-element.53.dest_ref) | copy-start | bytes 196612 | tf_op jit(solution)/shard_map/cond
where the time goes:
time: 96.6 us; the launch traced here: 95.6 us
  Pallas kernels  42.3 us (44%)
  waiting for transfers between devices  24.1 us (25%)
  blocking collectives  14.3 us (15%)
  starting transfers between devices  7.1 us (7%)
  local copies, waits for them, and re-layouts  4.49 us (5%)
  between operations  1.45 us (2%)
  other arithmetic  1.41 us (1%)
    all_to_all x1, waiting for transfers between devices, exchange(): lax.all_to_all(blocks, ('ctx', 'ch'), split_axis=0, concat_axis=0, tiled=...  24.1 us
    all_to_all x1, blocking collectives, exchange(): lax.all_to_all(blocks, ('ctx', 'ch'), split_axis=0, concat_axis=0, tiled=...  14.3 us
    pallas_call x1, Pallas kernels, pack(): pl.pallas_call(functools.partial(pack_kernel, sizes), grid=(sizes.peers /...  13.2 us
    pallas_call x1, Pallas kernels, owner(): pl.pallas_call(functools.partial(owner_kernel, sizes), in_specs=[pl.Block...  10.4 us
    pallas_call x1, Pallas kernels, finish(): pl.pallas_call(functools.partial(finish_kernel, sizes), in_specs=[pl.Bloc...  7.74 us
    all_to_all x1, starting transfers between devices, exchange(): lax.all_to_all(blocks, ('ctx', 'ch'), split_axis=0, concat_axis=0, tiled=...  7.1 us
    pallas_call x1, Pallas kernels, local(): pl.pallas_call(functools.partial(local_kernel, sizes), in_specs=[pl.Block...  6.71 us
    pallas_call x1, Pallas kernels, index(): pl.pallas_call(functools.partial(index_kernel, sizes), in_specs=[pl.Block...  4.21 us
  transfers between devices with their start and end apart: 1, of which 1 were waited for; matrix products, arithmetic and copies ran while one was open for 1% of the time, Pallas kernels for 11%

commit v1 on v0

--- a/solution.py
+++ b/solution.py
@@ -3,6 +3,7 @@
 
 import jax
 import jax.numpy as jnp
+import numpy as np
 from jax import lax
 from jax.experimental import pallas as pl
 from jax.experimental.pallas import tpu as pltpu
@@ -215,10 +216,11 @@
         self.each = self.block // self.peers
         self.own = groups // self.peers
         self.size = channels * ch // groups
-        self.cap = 96
+        self.cap = 80
         powers = [self.block, max(self.each, 1), self.own, self.size]
         self.fits = (
             tokens == LANES
+            and self.block == LANES
             and self.runs == 16
             and self.own == 16
             and self.size == 16
@@ -230,12 +232,40 @@
             and all(p & (p - 1) == 0 for p in powers)
         )
 
-    def owner(self, group):
-        return lax.shift_right_logical(group & (self.block - 1), self.each.bit_length() - 1)
-
-    def place(self, group):
-        block = lax.shift_right_logical(group, self.block.bit_length() - 1)
-        return block * self.each + (group & (self.each - 1))
+    def deal(self):
+        ways = np.zeros((8, 64), np.int32)
+        for way in range(64):
+            step = 2 * (way // 2) + 1
+            ways[:3, way] = (pow(step, -1, self.block), self.each // 2 * (way % 2), step)
+        return ways
+
+    def seat(self, group, way):
+        turn, start, _ = way
+        return (turn * (group & (self.block - 1)) + start) & (self.block - 1)
+
+    def owner(self, group, way):
+        return lax.shift_right_logical(self.seat(group, way), bits(self.each))
+
+    def place(self, group, way):
+        block = lax.shift_right_logical(group, bits(self.block))
+        return block * self.each + (self.seat(group, way) & (self.each - 1))
+
+    def group_at(self, seat, way):
+        _, start, step = way
+        return (step * (seat - start)) & (self.block - 1)
+
+    def group_here(self, place, me, way):
+        block = lax.shift_right_logical(place, bits(self.each))
+        seat = me * self.each + (place & (self.each - 1))
+        return block * self.block + self.group_at(seat, way)
+
+
+def bits(power):
+    return power.bit_length() - 1
+
+
+def way_of(dest_ref):
+    return tuple(dest_ref[row : row + 1, 0:1] for row in (3, 4, 5))
 
 
 def running_counts(marks, upper):
@@ -252,40 +282,82 @@
     return hot(iota((width, width), 0) < iota((width, width), 1))
 
 
+def choose_way(sizes, group, ways):
+    count = ways.shape[1]
+    low = 16
+    group = group & (sizes.block - 1)
+    loads = []
+    for source in range(sizes.ch):
+        row = group[source : source + 1]
+        high_hot = hot(iota((sizes.block // low, sizes.channels), 0) == lax.shift_right_logical(row, 4))
+        low_hot = hot(iota((low, sizes.channels), 0) == (row & (low - 1)))
+        table = dot_lanes(high_hot, low_hot)
+        spread = hot((iota((low, sizes.block), 1) & (low - 1)) == iota((low, sizes.block), 0))
+        wide = dot(table.astype(BF16), spread)
+        own = lax.shift_right_logical(iota(wide.shape, 1), 4) == iota(wide.shape, 0)
+        loads.append(jnp.sum(jnp.where(own, wide, 0.0), axis=0, keepdims=True))
+    loads = jnp.concatenate(loads + [jnp.zeros((8 - sizes.ch, sizes.block), F32)], axis=0)
+    lanes = sizes.peers * count
+    spread_ways = jnp.concatenate([ways] * sizes.peers, axis=1)
+    seat = sizes.seat(iota((sizes.block, lanes), 0), (spread_ways[0:1], spread_ways[1:2], None))
+    peer = lax.shift_right_logical(iota((1, lanes), 1), bits(count))
+    dealt = hot(lax.shift_right_logical(seat, bits(sizes.each)) == peer)
+    sums = dot(loads.astype(BF16), dealt)
+    fullest = sums[:, :LANES]
+    for start in range(LANES, lanes, LANES):
+        fullest = jnp.maximum(fullest, sums[:, start : start + LANES])
+    fullest = jnp.max(jnp.maximum(fullest, pltpu.roll(fullest, count, 1)), axis=0, keepdims=True)
+    score = fullest[:, :count] * float(count) + iota((1, count), 1).astype(F32)
+    best = jnp.min(score, axis=1, keepdims=True)
+    mine = jnp.where(score == best, ways[0:3].astype(F32), 0.0)
+    chosen = jnp.sum(mine, axis=1, keepdims=True).astype(I32)
+    return chosen[0:1], chosen[1:2], chosen[2:3]
+
+
 def pack_kernel(
-    sizes, runs_ref, group_ref, key_ref, value_ref, cot_ref, query_ref, out_ref, dest_ref, data
+    sizes,
+    place_ref,
+    ways_ref,
+    all_ref,
+    group_ref,
+    key_ref,
+    value_ref,
+    cot_ref,
+    query_ref,
+    out_ref,
+    dest_ref,
+    data,
 ):
     part = out_ref.shape[0]
 
     @pl.when(pl.program_id(0) == 0)
     def _():
-        owner = sizes.owner(group_ref[...])
+        way = choose_way(sizes, all_ref[...], ways_ref[...])
+        owner = sizes.owner(group_ref[...], way)
         marks = iota((sizes.peers, sizes.channels), 0) == owner
         counts, _ = running_counts(hot(marks), upper_ones(256))
         slot = jnp.sum(jnp.where(marks, counts, 0.0), axis=0, keepdims=True).astype(I32)
         dest_ref[0:1, :] = jnp.where(slot < sizes.cap - 1, owner * sizes.cap + slot, -1)
         dest_ref[1:2, :] = owner
         dest_ref[2:3, :] = slot
-        dest_ref[3:8, :] = jnp.zeros((5, sizes.channels), I32)
+        for row in range(3):
+            dest_ref[3 + row : 4 + row, :] = jnp.broadcast_to(way[row], (1, sizes.channels))
+        dest_ref[6:8, :] = jnp.zeros((2, sizes.channels), I32)
         data[:, :LANES] = (key_ref[...].astype(F32) * value_ref[...].astype(F32)).astype(BF16)
         data[:, LANES:] = (cot_ref[...].astype(F32) * query_ref[...].astype(F32)).astype(BF16)
 
-    dest = dest_ref[0:1, :]
-    lane = iota((1, 2 * LANES), 1)
-    run_row = jnp.where(lane < LANES, runs_ref[0], runs_ref[1]).astype(F32)
-    row = iota((sizes.cap, 1), 0)
-
-    def one_peer(index, carry):
-        base = (pl.program_id(0) * part + index) * sizes.cap
-        chosen = hot(iota((sizes.cap, sizes.channels), 0) == dest - base)
-        rows = dot(chosen, data[...])
-        out_ref[index] = jnp.where(row == sizes.cap - 1, run_row, rows).astype(BF16)
-        return carry
-
-    lax.fori_loop(0, part, one_peer, 0)
-
-
-def pack(sizes, run_ids, shard_groups, key_proj, value_proj, cotangent, query_proj):
+    shift = bits(sizes.run)
+    first = lax.shift_right_logical(place_ref[0], shift)
+    second = lax.shift_right_logical(place_ref[sizes.run], shift)
+    run_row = jnp.where(iota((1, 1, 2 * LANES), 2) < LANES, first, second).astype(F32)
+    base = pl.program_id(0) * part * sizes.cap
+    chosen = hot(iota((part * sizes.cap, sizes.channels), 0) == dest_ref[0:1, :] - base)
+    rows = dot(chosen, data[...]).reshape(part, sizes.cap, 2 * LANES)
+    spare = iota((part, sizes.cap, 1), 1) == sizes.cap - 1
+    out_ref[...] = jnp.where(spare, run_row, rows).astype(BF16)
+
+
+def pack(sizes, positions, ways, all_groups, shard_groups, key_proj, value_proj, cotangent, query_proj):
     part = 8
     whole = lambda shape: pl.BlockSpec(shape, lambda step: (0, 0))
     rows = (sizes.channels, sizes.tokens)
@@ -294,6 +366,8 @@
         grid=(sizes.peers // part,),
         in_specs=[
             pl.BlockSpec(memory_space=pltpu.SMEM),
+            whole(ways.shape),
+            whole((sizes.ch, sizes.channels)),
             whole((1, sizes.channels)),
             whole(rows),
             whole(rows),
@@ -311,16 +385,26 @@
         scratch_shapes=[pltpu.VMEM((sizes.channels, 2 * LANES), BF16)],
         compiler_params=pltpu.CompilerParams(vmem_limit_bytes=VMEM_LIMIT),
         name="pack_rows",
-    )(run_ids, shard_groups, key_proj, value_proj, cotangent, query_proj)
+    )(positions, ways, all_groups, shard_groups, key_proj, value_proj, cotangent, query_proj)
 
 
 def index_kernel(
-    sizes, me_ref, group_ref, rate_ref, gain_ref, into_ref, back_ref, over_ref, table_ref
+    sizes,
+    me_ref,
+    group_ref,
+    dest_ref,
+    param_ref,
+    into_ref,
+    back_ref,
+    over_ref,
+    table_ref,
+    leap_ref,
 ):
     me = me_ref[0]
+    way = way_of(dest_ref)
     upper = upper_ones(256)
     group = group_ref[...]
-    owner, place = sizes.owner(group), sizes.place(group)
+    owner, place = sizes.owner(group, way), sizes.place(group, way)
     most = jnp.zeros((sizes.peers, 1), F32)
     for source in range(sizes.ch):
         marks = iota((sizes.peers, sizes.channels), 0) == owner[source : source + 1]
@@ -351,13 +435,38 @@
         into = into + dot(found, moved)
     into_ref[...] = into.astype(BF16)
 
-    rate, gain = rate_ref[...], gain_ref[...]
+    modes = leap_ref.shape[0]
+    terms = three_terms(param_ref[...])
+    shape = (256, sizes.groups)
+    wanted = sizes.group_here(lax.shift_right_logical(iota((256, 1), 0), bits(modes)), me, way)
+    found = dot_lanes(hot(iota(shape, 1) == wanted), terms)
+    found = three_sum(found, 1)
+    mode = iota((256, 2 * modes), 0) & (modes - 1)
+    lane = iota((256, 2 * modes), 1)
+    rate = jnp.sum(jnp.where(lane == mode, found, 0.0), axis=1, keepdims=True)
+    gain = jnp.sum(jnp.where(lane == mode + modes, found, 0.0), axis=1, keepdims=True)
     step = iota((256, sizes.run), 1).astype(F32)
     high, low = two_terms(gain * jnp.exp(-rate * step))
     table_ref[...] = jnp.concatenate([high, low], axis=1)
-
-
-def index(sizes, me, all_groups, rate_col, gain_col):
+    shape = (sizes.groups, 256)
+    wanted = sizes.group_here(lax.shift_right_logical(iota((1, 256), 1), bits(sizes.size)), me, way)
+    found = three_sum(dot(terms, hot(iota(shape, 0) == wanted)), 0)
+    leap_ref[...] = jnp.exp(found[:modes] * -float(sizes.run))
+
+
+def three_terms(exact):
+    high, rest = two_terms(exact)
+    low, _ = two_terms(exact - high.astype(F32) - rest.astype(F32))
+    return jnp.concatenate([high, rest, low], axis=0)
+
+
+def three_sum(found, dim):
+    high, rest, low = jnp.split(found, 3, axis=dim)
+    return high + rest + low
+
+
+def index(sizes, me, all_groups, dest, params):
+    modes = params.shape[0] // 2
     return pl.pallas_call(
         functools.partial(index_kernel, sizes),
         in_specs=[pl.BlockSpec(memory_space=pltpu.SMEM)]
@@ -367,11 +476,12 @@
             jax.ShapeDtypeStruct((256, sizes.ch * LANES), BF16),
             jax.ShapeDtypeStruct((8, LANES), I32),
             jax.ShapeDtypeStruct((256, 2 * sizes.run), BF16),
+            jax.ShapeDtypeStruct((modes, 256), F32),
         ],
         compiler_params=pltpu.CompilerParams(vmem_limit_bytes=VMEM_LIMIT),
         cost_estimate=pl.CostEstimate(flops=2 * 10**9, bytes_accessed=10**6, transcendentals=0),
         name="index_rows",
-    )(me, all_groups, rate_col, gain_col)
+    )(me, all_groups, dest, params)
 
 
 def local_kernel(
@@ -379,15 +489,11 @@
 ):
     modes = param_ref.shape[0] // 2
     blocks = sizes.channels // LANES
-    exact = param_ref[...]
-    high, rest = two_terms(exact)
-    low, last = two_terms(exact - high.astype(F32) - rest.astype(F32))
-    stacked = jnp.concatenate([high, rest, low], axis=0)
+    stacked = three_terms(param_ref[...])
     rows = 2 * modes
     for start in range(0, sizes.channels, 256):
         chosen = hot(iota((sizes.groups, 256), 0) == group_ref[:, start : start + 256])
-        found = dot(stacked, chosen)
-        found = found[:rows] + found[rows : 2 * rows] + found[2 * rows :]
+        found = three_sum(dot(stacked, chosen), 0)
         for half in range(2):
             block = start // LANES + half
             params[block * rows : (block + 1) * rows, :] = found[
@@ -492,7 +598,7 @@
         weighted[second, :, run:] = value[:, run:]
 
     modes = states.shape[1]
-    group_lane = lax.shift_right_logical(iota((modes, rows), 1), size.bit_length() - 1)
+    group_lane = lax.shift_right_logical(iota((modes, rows), 1), bits(size))
     carried = jnp.zeros((modes, rows), F32)
     leap = leap_ref[...]
     for at in range(runs):
@@ -522,7 +628,7 @@
         sums[pl.ds(group, 1), :] = jnp.sum(skewed, axis=0, keepdims=True)[:, :seq]
         return carry
 
-    lax.fori_loop(0, own, one_group, 0)
+    lax.fori_loop(0, own, one_group, 0, unroll=True)
 
     each = sizes.each
     quarter = LANES // 4
@@ -589,7 +695,7 @@
             found[pl.ds(start, rows), :] = mine[:, half * LANES : (half + 1) * LANES]
         return carry
 
-    lax.fori_loop(0, sizes.channels // 256, fetch, 0)
+    lax.fori_loop(0, sizes.channels // 256, fetch, 0, unroll=True)
     for first in range(0, blocks, 8):
         decays = [
             decay_ref[mode * blocks + first : mode * blocks + first + 8, :]
@@ -608,7 +714,7 @@
                 total[at, :] = conv_ref[at, :] + tree_sum(states)
                 return states
 
-            lax.fori_loop(0, sizes.run, step, states)
+            lax.fori_loop(0, sizes.run, step, states, unroll=8)
 
     def turn(block, carry):
         at = pl.ds(pl.multiple_of(block * LANES, LANES), LANES)
@@ -616,14 +722,14 @@
         out_ref[at, :] = (query_ref[at, :].astype(F32) * conv.astype(F32)).astype(BF16)
         return carry
 
-    lax.fori_loop(0, blocks, turn, 0)
+    lax.fori_loop(0, blocks, turn, 0, unroll=True)
 
     each, quarter = sizes.each, LANES // 4
     high_low = recv_ref[...].astype(F32)
     terms = []
     lane_part = lax.shift_right_logical(iota((sizes.peers * 16, LANES), 1), 5)
     row = iota((sizes.peers * 16, LANES), 0)
-    row_part = lax.shift_right_logical(row & 15, each.bit_length() - 1)
+    row_part = lax.shift_right_logical(row & 15, bits(each))
     for term in range(2):
         piece = high_low[:, term * 16 : (term + 1) * 16, :].reshape(sizes.peers * 16, LANES)
         placed = jnp.zeros((sizes.peers * 16, LANES), F32)
@@ -631,13 +737,10 @@
             moved = pltpu.roll(piece, (part * quarter + quarter) % LANES, 1)
             placed = jnp.where((row_part == part) & (lane_part == part), moved, placed)
         terms.append(placed.astype(BF16))
-    shape = (sizes.block, sizes.peers * 16)
-    to, come = iota(shape, 0), iota(shape, 1)
-    bits = each.bit_length() - 1
-    chosen = hot(
-        (lax.shift_right_logical(to, bits) == lax.shift_right_logical(come, 4))
-        & ((to & (each - 1)) == (come & (each - 1)))
-    )
+    come = iota((1, sizes.peers * 16), 1)
+    seat = lax.shift_right_logical(come, 4) * each + (come & (each - 1))
+    wanted = sizes.group_at(seat, way_of(dest_ref))
+    chosen = hot(iota((sizes.block, sizes.peers * 16), 0) == wanted)
     grad_ref[...] = dot(chosen, terms[0]) + dot(chosen, terms[1])
 
 
@@ -667,30 +770,26 @@
     query_proj, key_proj, value_proj, cotangent, positions, group_of, decay_rates, residues = args
     ch_rank = lax.axis_index("ch")
     me = lax.axis_index("ctx") * sizes.ch + ch_rank
-    run_ids = jnp.stack([positions[0], positions[sizes.run]]) // sizes.run
     all_groups = group_of.reshape(sizes.ch, sizes.channels)
     shard_groups = lax.dynamic_slice_in_dim(all_groups, ch_rank, 1)
-    sent, dest = pack(sizes, run_ids, shard_groups, key_proj, value_proj, cotangent, query_proj)
+    sent, dest = pack(
+        sizes,
+        positions,
+        jnp.asarray(sizes.deal()),
+        all_groups,
+        shard_groups,
+        key_proj,
+        value_proj,
+        cotangent,
+        query_proj,
+    )
     recv = exchange(sent)
 
     gains = residues * jnp.sqrt(2.0 * decay_rates)
     params = jnp.concatenate([decay_rates, gains], axis=1).T
     conv, decay = local(sizes, shard_groups, params, key_proj, value_proj)
-    modes = decay_rates.shape[1]
-
-    def owned(values):
-        split = values.reshape(sizes.ch, sizes.peers, sizes.each, modes)
-        mine = lax.dynamic_index_in_dim(split, me, 1, keepdims=False)
-        return mine.reshape(sizes.own, modes)
-
-    own_rates, own_gains = owned(decay_rates), owned(gains)
-    leap = jnp.repeat(jnp.exp(-float(sizes.run) * own_rates.T), sizes.size, axis=1)
-    into, back, most, table = index(
-        sizes,
-        me.reshape(1).astype(I32),
-        all_groups,
-        own_rates.reshape(-1, 1),
-        own_gains.reshape(-1, 1),
+    into, back, most, table, leap = index(
+        sizes, me.reshape(1).astype(I32), all_groups, dest, params
     )
 
     def fast(recv, into, back, table, leap, dest, conv, decay, *args):

time: 96.6 us -> 73.6 us (0.76)
  Pallas kernels: 42.3 us -> 29.1 us
  waiting for transfers between devices: 24.1 us -> 18.2 us
  local copies, waits for them, and re-layouts: 4.49 us -> 2.04 us
  other arithmetic: 1.41 us -> 0.02 us
    all_to_all x1, waiting for transfers between devices: 24.1 us -> 18.2 us  [exchange(): lax.all_to_all(blocks, ('ctx', 'ch'), split_axis=0, concat_axis=0, tiled=...]
    pallas_call x1, Pallas kernels: 13.2 us -> 7.63 us  [pack(): pl.pallas_call(functools.partial(pack_kernel, sizes), grid=(sizes.peers /...]
    pallas_call x1, Pallas kernels: 10.4 us -> 5.96 us  [owner(): pl.pallas_call(functools.partial(owner_kernel, sizes), in_specs=[pl.Block...]
    pallas_call x1, Pallas kernels: 7.74 us -> 4.04 us  [finish(): pl.pallas_call(functools.partial(finish_kernel, sizes), in_specs=[pl.Bloc...]
    select_n x1 -> x0, other arithmetic: 1.38 us -> none  [owners_way(): run_ids = jnp.stack([positions[0], positions[sizes.run]]) // sizes.run]
    slice x1 -> x0, local copies, waits for them, and re-layouts: 1.31 us -> none  [owners_way(): run_ids = jnp.stack([positions[0], positions[sizes.run]]) // sizes.run]
    cond x8 -> x6, local copies, waits for them, and re-layouts: 1.11 us -> 0.01 us
  transfers between devices with their start and end apart: 1 -> 1, of which waited for: 1 -> 1; matrix products, arithmetic and copies ran while one was open for 1% -> 1% of each run, Pallas kernels for 11% -> 16%
where the time goes in v1:
time: 73.6 us; the launch traced here: 72.7 us
  Pallas kernels  29.1 us (40%)
  waiting for transfers between devices  18.2 us (25%)
  blocking collectives  14.5 us (20%)
  starting transfers between devices  7.09 us (10%)
  local copies, waits for them, and re-layouts  2.04 us (3%)
  between operations  1.41 us (2%)
    all_to_all x1, waiting for transfers between devices, exchange(): lax.all_to_all(blocks, ('ctx', 'ch'), split_axis=0, concat_axis=0, tiled=...  18.2 us
    all_to_all x1, blocking collectives, exchange(): lax.all_to_all(blocks, ('ctx', 'ch'), split_axis=0, concat_axis=0, tiled=...  14.5 us
    pallas_call x1, Pallas kernels, pack(): pl.pallas_call(functools.partial(pack_kernel, sizes), grid=(sizes.peers /...  7.63 us
    all_to_all x1, starting transfers between devices, exchange(): lax.all_to_all(blocks, ('ctx', 'ch'), split_axis=0, concat_axis=0, tiled=...  7.09 us
    pallas_call x1, Pallas kernels, local(): pl.pallas_call(functools.partial(local_kernel, sizes), in_specs=[pl.Block...  6.72 us
    pallas_call x1, Pallas kernels, owner(): pl.pallas_call(functools.partial(owner_kernel, sizes), in_specs=[pl.Block...  5.96 us
    pallas_call x1, Pallas kernels, index(): pl.pallas_call(functools.partial(index_kernel, sizes), in_specs=[pl.Block...  4.77 us
    pallas_call x1, Pallas kernels, finish(): pl.pallas_call(functools.partial(finish_kernel, sizes), in_specs=[pl.Bloc...  4.04 us
  transfers between devices with their start and end apart: 1, of which 1 were waited for; matrix products, arithmetic and copies ran while one was open for 1% of the time, Pallas kernels for 16%

profile of v1, /device:TPU:1, one launch (start us, length us, event | category | flops | bytes accessed | tf_op | source)
XLA Modules:
  0.0 72.7 jit_solution(8081202721146811137)
XLA Ops:
  0.6 0.8 %reshape.224.all_ref.group_ref = s32[4,2048]{1,0:T(4,128)S(1)} reshape(s32[8192]{0:T(1024)} %param.16) | data formatting | bytes 65536 | tf_op jit(solution)/shard_map/reshape | solution.py:773
  1.4 0.0 copy-start
  1.4 0.7 copy-done
  2.1 7.6 %pack_rows.1 = (bf16[32,80,256]{2,1,0:T(8,128)(2,1)}, s32[8,2048]{1,0:T(8,128)S(1)}) custom-call(s32[128]{0:T(128)} %place_ref.1, s32[8,64]{1,0:T(8,128)S(1)} %copy-done, s32[4,2048]{1,0:T(4,128)S(1)} %reshape.224.all_ref.group_ref, s32[1,2048]{1,0:T(1,128)S(1)} %constant_dynamic-slice_fusion.group_ref, bf16[2048,128]{1,0:T(8,128)(2,1)} %key_ref.3, ...), custom_call_target="tpu_custom_call" | custom-call | tf_op jit(solution)/shard_map/pack_rows/pallas_call | solution.py:364
  9.8 7.1 %all-to-all-start.7 = ((bf16[32,80,256]{2,1,0:T(8,128)(2,1)}), bf16[32,80,256]{2,1,0:T(8,128)(2,1)S(1)}, u32[]{:S(2)}, u32[]{:S(2)}) async-start(bf16[32,80,256]{2,1,0:T(8,128)(2,1)} %get-tuple-element.64), calls=%async_computation.7 | async-start | bytes 2621440 | tf_op jit(solution)/shard_map/all_to_all | solution.py:766
  16.9 0.0 copy-done.10
  16.9 0.0 copy-done.12
  16.9 0.0 copy-start.6
  16.9 0.0 copy-start.7
  16.9 4.8 %index_rows.1 = (bf16[256,320]{1,0:T(8,128)(2,1)}, bf16[256,512]{1,0:T(8,128)(2,1)}, s32[8,128]{1,0:T(8,128)S(1)}, bf16[256,128]{1,0:T(8,128)(2,1)}, f32[16,256]{1,0:T(8,128)}) custom-call(s32[1]{0:T(128)} %bitcast.46.me_ref, s32[4,2048]{1,0:T(4,128)S(1)} %reshape.224.all_ref.group_ref, s32[8,2048]{1,0:T(8,128)S(1)} %get-tuple-element.62.dest_ref, ...), custom_call_target="tpu_custom_call" | custom-call | flops 2000000000 | bytes 1000000 | tf_op jit(solution)/shard_map/index_rows/pallas_call | solution.py:470
  21.7 0.0 copy-done.13
  21.7 0.5 slice.39
  22.9 0.0 copy-done.6
  22.9 0.0 copy-done.7
  22.9 0.0 copy-start.4
  22.9 0.0 copy-start.8
  22.9 0.0 copy-start.15
  22.9 6.7 %local_runs.1 = (f32[2048,128]{1,0:T(8,128)}, f32[256,128]{1,0:T(8,128)}) custom-call(s32[1,2048]{1,0:T(1,128)S(1)} %constant_dynamic-slice_fusion.group_ref, f32[32,512]{1,0:T(8,128)S(1)} %maximum_bitcast_fusion.param_ref, bf16[2048,128]{1,0:T(8,128)(2,1)S(1)} %copy-done.6, bf16[2048,128]{1,0:T(8,128)(2,1)S(1)} %copy-done.7), custom_call_target="tpu_custom_call" | custom-call | flops 4000000000 | bytes 3000000 | tf_op jit(solution)/shard_map/local_runs/pallas_call | solution.py:542
  29.7 18.2 %all-to-all-done.7 = bf16[32,80,256]{2,1,0:T(8,128)(2,1)S(1)} async-done(((bf16[32,80,256]{2,1,0:T(8,128)(2,1)}), bf16[32,80,256]{2,1,0:T(8,128)(2,1)S(1)}, u32[]{:S(2)}, u32[]{:S(2)}) %all-to-all-start.7) | async-done | bytes 1310752 | tf_op jit(solution)/shard_map/all_to_all | solution.py:766
  47.8 0.0 copy-done.4
  47.9 0.0 copy-done.8
  47.9 0.0 copy-done.15
  47.9 24.8 %conditional.1 = ((bf16[2048,128]{1,0:T(8,128)(2,1)}, f32[128,128]{1,0:T(8,128)})) conditional(s32[]{:T(128)} %bitcast.48, (bf16[2048,128]{1,0:T(8,128)(2,1)S(1)}, s32[8192]{0:T(1024)}, f32[512,16]{0,1:T(8,128)S(1)}, f32[512,16]{0,1:T(8,128)S(1)}, bf16[2048,128]{1,0:T(8,128)(2,1)S(1)}, /*index=5*/bf16[2048,128]{1,0:T(8,128)(2,1)S(1)}, ...), branch_computations={%region_0.4_spmd, %region_4.5_spmd} | conditional | flops 10720338944 | bytes 257276512 | solution.py:802
  48.1 0.0 copy-start.9
  48.1 0.0 copy-start.11
  48.1 0.0 copy-start.14
  48.1 6.0 %owner_sums.1 = bf16[32,32,128]{2,1,0:T(8,128)(2,1)S(1)} custom-call(bf16[32,80,256]{2,1,0:T(8,128)(2,1)S(1)} %get-tuple-element.42.recv_ref, bf16[256,320]{1,0:T(8,128)(2,1)} %get-tuple-element.43.into_ref, bf16[256,512]{1,0:T(8,128)(2,1)} %get-tuple-element.44.back_ref, bf16[256,128]{1,0:T(8,128)(2,1)} %get-tuple-element.45.table_ref, ...), custom_call_target="tpu_custom_call" | custom-call | tf_op jit(solution)/shard_map/cond/branch_1_fun/owner_sums/pallas_call | solution.py:661
  54.1 14.5 %all_to_all.68.recv_ref = bf16[32,32,128]{2,1,0:T(8,128)(2,1)S(1)} all-to-all(bf16[32,32,128]{2,1,0:T(8,128)(2,1)S(1)} %owner_sums.1), channel_id=1, replica_groups=mesh['ctx'=8,'ch'=4] {'ctx','ch'}, dimensions={0} | all-to-all | bytes 524288 | tf_op jit(solution)/shard_map/cond/branch_1_fun/all_to_all | solution.py:766
  68.6 0.0 copy-done.9
  68.6 0.0 copy-done.11
  68.7 0.0 copy-done.14
  68.7 4.0 %finish_rows.1 = (bf16[2048,128]{1,0:T(8,128)(2,1)}, f32[128,128]{1,0:T(8,128)}) custom-call(bf16[32,32,128]{2,1,0:T(8,128)(2,1)S(1)} %all_to_all.68.recv_ref, s32[8,2048]{1,0:T(8,128)S(1)} %copy-done.14, f32[2048,128]{1,0:T(8,128)S(1)} %copy-done.9, f32[256,128]{1,0:T(8,128)S(1)} %copy-done.11, bf16[2048,128]{1,0:T(8,128)(2,1)S(1)} %get-tuple-element.50.query_ref), custom_call_target="tpu_custom_call" | custom-call | tf_op jit(solution)/shard_map/cond/branch_1_fun/finish_rows/pallas_call | solution.py:749
  (6 shorter events, 0.0 us)
Async XLA Ops:
  1.4 0.7 copy-start
  2.1 14.7 %copy-start.10 = (f32[512,16]{0,1:T(8,128)S(1)}, f32[512,16]{0,1:T(8,128)}, u32[]{:S(2)}) copy-start(f32[512,16]{0,1:T(8,128)} %param.17) | copy-start | bytes 98308
  2.1 14.8 %copy-start.12 = (f32[512,16]{0,1:T(8,128)S(1)}, f32[512,16]{0,1:T(8,128)}, u32[]{:S(2)}) copy-start(f32[512,16]{0,1:T(8,128)} %param.18) | copy-start | bytes 98308
  9.8 12.0 %copy-start.13 = (s32[8,2048]{1,0:T(8,128)}, s32[8,2048]{1,0:T(8,128)S(1)}, u32[]{:S(2)}) copy-start(s32[8,2048]{1,0:T(8,128)S(1)} %get-tuple-element.62.dest_ref) | copy-start | bytes 196612
  9.8 38.1 %all-to-all-start.7 = ((bf16[32,80,256]{2,1,0:T(8,128)(2,1)}), bf16[32,80,256]{2,1,0:T(8,128)(2,1)S(1)}, u32[]{:S(2)}, u32[]{:S(2)}) async-start(bf16[32,80,256]{2,1,0:T(8,128)(2,1)} %get-tuple-element.64), calls=%async_computation.7 | async-start | bytes 2621440 | tf_op jit(solution)/shard_map/all_to_all | solution.py:766
  16.9 6.0 %copy-start.6 = (bf16[2048,128]{1,0:T(8,128)(2,1)S(1)}, bf16[2048,128]{1,0:T(8,128)(2,1)}, u32[]{:S(2)}) copy-start(bf16[2048,128]{1,0:T(8,128)(2,1)} %key_ref.3) | copy-start | bytes 1572868
  16.9 6.0 %copy-start.7 = (bf16[2048,128]{1,0:T(8,128)(2,1)S(1)}, bf16[2048,128]{1,0:T(8,128)(2,1)}, u32[]{:S(2)}) copy-start(bf16[2048,128]{1,0:T(8,128)(2,1)} %value_ref.3) | copy-start | bytes 1572868
  22.9 24.9 %copy-start.4 = (bf16[2048,128]{1,0:T(8,128)(2,1)S(1)}, bf16[2048,128]{1,0:T(8,128)(2,1)}, u32[]{:S(2)}) copy-start(bf16[2048,128]{1,0:T(8,128)(2,1)} %query_ref.1) | copy-start | bytes 1572868
  22.9 24.9 %copy-start.8 = (bf16[2048,128]{1,0:T(8,128)(2,1)S(1)}, bf16[2048,128]{1,0:T(8,128)(2,1)}, u32[]{:S(2)}) copy-start(bf16[2048,128]{1,0:T(8,128)(2,1)} %cot_ref.1) | copy-start | bytes 1572868
  22.9 24.9 %copy-start.15 = (s32[128]{0:T(128)S(1)}, s32[128]{0:T(128)}, u32[]{:S(2)}) copy-start(s32[128]{0:T(128)} %place_ref.1) | copy-start | bytes 1540
  48.1 20.5 %copy-start.9 = (f32[2048,128]{1,0:T(8,128)S(1)}, f32[2048,128]{1,0:T(8,128)}, u32[]{:S(2)}) copy-start(f32[2048,128]{1,0:T(8,128)} %get-tuple-element.48.conv_ref) | copy-start | bytes 3145732 | tf_op jit(solution)/shard_map/cond
  48.1 20.5 %copy-start.11 = (f32[256,128]{1,0:T(8,128)S(1)}, f32[256,128]{1,0:T(8,128)}, u32[]{:S(2)}) copy-start(f32[256,128]{1,0:T(8,128)} %get-tuple-element.49.decay_ref) | copy-start | bytes 393220 | tf_op jit(solution)/shard_map/cond
  48.1 20.5 %copy-start.14 = (s32[8,2048]{1,0:T(8,128)S(1)}, s32[8,2048]{1,0:T(8,128)}, u32[]{:S(2)}) copy-start(s32[8,2048]{1,0:T(8,128)} %get-tuple-element.47.dest_ref) | copy-start | bytes 196612 | tf_op jit(solution)/shard_map/cond

commit v2 on v1

--- a/solution.py
+++ b/solution.py
@@ -3,7 +3,6 @@
 
 import jax
 import jax.numpy as jnp
-import numpy as np
 from jax import lax
 from jax.experimental import pallas as pl
 from jax.experimental.pallas import tpu as pltpu
@@ -232,12 +231,13 @@
             and all(p & (p - 1) == 0 for p in powers)
         )
 
-    def deal(self):
-        ways = np.zeros((8, 64), np.int32)
-        for way in range(64):
-            step = 2 * (way // 2) + 1
-            ways[:3, way] = (pow(step, -1, self.block), self.each // 2 * (way % 2), step)
-        return ways
+    def deal(self, count):
+        way = iota((1, count), 1)
+        step = 2 * lax.shift_right_logical(way, 1) + 1
+        turn = step
+        for _ in range(3):
+            turn = (turn * (2 - step * turn)) & (self.block - 1)
+        return turn, (self.each // 2) * (way & 1), step
 
     def seat(self, group, way):
         turn, start, _ = way
@@ -282,13 +282,14 @@
     return hot(iota((width, width), 0) < iota((width, width), 1))
 
 
-def choose_way(sizes, group, ways):
-    count = ways.shape[1]
+def choose_way(sizes, group):
+    count = 64
+    ways = sizes.deal(count)
     low = 16
     group = group & (sizes.block - 1)
     loads = []
     for source in range(sizes.ch):
-        row = group[source : source + 1]
+        row = group[:, source * sizes.channels : (source + 1) * sizes.channels]
         high_hot = hot(iota((sizes.block // low, sizes.channels), 0) == lax.shift_right_logical(row, 4))
         low_hot = hot(iota((low, sizes.channels), 0) == (row & (low - 1)))
         table = dot_lanes(high_hot, low_hot)
@@ -298,8 +299,8 @@
         loads.append(jnp.sum(jnp.where(own, wide, 0.0), axis=0, keepdims=True))
     loads = jnp.concatenate(loads + [jnp.zeros((8 - sizes.ch, sizes.block), F32)], axis=0)
     lanes = sizes.peers * count
-    spread_ways = jnp.concatenate([ways] * sizes.peers, axis=1)
-    seat = sizes.seat(iota((sizes.block, lanes), 0), (spread_ways[0:1], spread_ways[1:2], None))
+    spread = [jnp.concatenate([part] * sizes.peers, axis=1) for part in ways]
+    seat = sizes.seat(iota((sizes.block, lanes), 0), spread)
     peer = lax.shift_right_logical(iota((1, lanes), 1), bits(count))
     dealt = hot(lax.shift_right_logical(seat, bits(sizes.each)) == peer)
     sums = dot(loads.astype(BF16), dealt)
@@ -309,31 +310,45 @@
     fullest = jnp.max(jnp.maximum(fullest, pltpu.roll(fullest, count, 1)), axis=0, keepdims=True)
     score = fullest[:, :count] * float(count) + iota((1, count), 1).astype(F32)
     best = jnp.min(score, axis=1, keepdims=True)
-    mine = jnp.where(score == best, ways[0:3].astype(F32), 0.0)
-    chosen = jnp.sum(mine, axis=1, keepdims=True).astype(I32)
-    return chosen[0:1], chosen[1:2], chosen[2:3]
+    return tuple(
+        jnp.sum(jnp.where(score == best, part.astype(F32), 0.0), axis=1, keepdims=True).astype(I32)
+        for part in ways
+    )
 
 
 def pack_kernel(
     sizes,
-    place_ref,
-    ways_ref,
-    all_ref,
-    group_ref,
-    key_ref,
-    value_ref,
-    cot_ref,
-    query_ref,
+    place_hbm,
+    group_hbm,
+    key_hbm,
+    value_hbm,
+    cot_hbm,
+    query_hbm,
     out_ref,
     dest_ref,
+    place_ref,
+    group_ref,
+    inputs,
     data,
+    arrived,
 ):
     part = out_ref.shape[0]
 
     @pl.when(pl.program_id(0) == 0)
     def _():
-        way = choose_way(sizes, all_ref[...], ways_ref[...])
-        owner = sizes.owner(group_ref[...], way)
+        moves = [(group_hbm, group_ref), (place_hbm, place_ref)]
+        for at, source in enumerate((key_hbm, value_hbm, cot_hbm, query_hbm)):
+            moves.append((source, inputs.at[at]))
+        copies = [
+            pltpu.make_async_copy(source, target, arrived.at[at])
+            for at, (source, target) in enumerate(moves)
+        ]
+        for copy in copies:
+            copy.start()
+        copies[0].wait()
+        way = choose_way(sizes, group_ref[...])
+        first = pl.multiple_of(lax.axis_index("ch") * sizes.channels, LANES)
+        owner = sizes.owner(group_ref[:, pl.ds(first, sizes.channels)], way)
         marks = iota((sizes.peers, sizes.channels), 0) == owner
         counts, _ = running_counts(hot(marks), upper_ones(256))
         slot = jnp.sum(jnp.where(marks, counts, 0.0), axis=0, keepdims=True).astype(I32)
@@ -343,8 +358,12 @@
         for row in range(3):
             dest_ref[3 + row : 4 + row, :] = jnp.broadcast_to(way[row], (1, sizes.channels))
         dest_ref[6:8, :] = jnp.zeros((2, sizes.channels), I32)
-        data[:, :LANES] = (key_ref[...].astype(F32) * value_ref[...].astype(F32)).astype(BF16)
-        data[:, LANES:] = (cot_ref[...].astype(F32) * query_ref[...].astype(F32)).astype(BF16)
+        for copy in copies[1:]:
+            copy.wait()
+        across = iota((LANES, LANES), 0) ^ iota((LANES, LANES), 1)
+        gated = (inputs[0].astype(F32) * inputs[1].astype(F32)).astype(BF16)
+        data[:, :LANES] = dot(gated, hot(across == sizes.run - 1)).astype(BF16)
+        data[:, LANES:] = (inputs[2].astype(F32) * inputs[3].astype(F32)).astype(BF16)
 
     shift = bits(sizes.run)
     first = lax.shift_right_logical(place_ref[0], shift)
@@ -357,35 +376,30 @@
     out_ref[...] = jnp.where(spare, run_row, rows).astype(BF16)
 
 
-def pack(sizes, positions, ways, all_groups, shard_groups, key_proj, value_proj, cotangent, query_proj):
-    part = 8
-    whole = lambda shape: pl.BlockSpec(shape, lambda step: (0, 0))
-    rows = (sizes.channels, sizes.tokens)
+def pack(sizes, positions, groups, key_proj, value_proj, cotangent, query_proj):
+    part = 16
     return pl.pallas_call(
         functools.partial(pack_kernel, sizes),
         grid=(sizes.peers // part,),
-        in_specs=[
-            pl.BlockSpec(memory_space=pltpu.SMEM),
-            whole(ways.shape),
-            whole((sizes.ch, sizes.channels)),
-            whole((1, sizes.channels)),
-            whole(rows),
-            whole(rows),
-            whole(rows),
-            whole(rows),
-        ],
+        in_specs=[pl.BlockSpec(memory_space=pl.ANY)] * 6,
         out_specs=[
             pl.BlockSpec((part, sizes.cap, 2 * LANES), lambda step: (step, 0, 0)),
-            whole((8, sizes.channels)),
+            pl.BlockSpec((8, sizes.channels), lambda step: (0, 0)),
         ],
         out_shape=[
             jax.ShapeDtypeStruct((sizes.peers, sizes.cap, 2 * LANES), BF16),
             jax.ShapeDtypeStruct((8, sizes.channels), I32),
         ],
-        scratch_shapes=[pltpu.VMEM((sizes.channels, 2 * LANES), BF16)],
+        scratch_shapes=[
+            pltpu.SMEM(positions.shape, I32),
+            pltpu.VMEM(groups.shape, I32),
+            pltpu.VMEM((4, sizes.channels, sizes.tokens), BF16),
+            pltpu.VMEM((sizes.channels, 2 * LANES), BF16),
+            pltpu.SemaphoreType.DMA((6,)),
+        ],
         compiler_params=pltpu.CompilerParams(vmem_limit_bytes=VMEM_LIMIT),
         name="pack_rows",
-    )(positions, ways, all_groups, shard_groups, key_proj, value_proj, cotangent, query_proj)
+    )(positions, groups, key_proj, value_proj, cotangent, query_proj)
 
 
 def index_kernel(
@@ -405,17 +419,18 @@
     upper = upper_ones(256)
     group = group_ref[...]
     owner, place = sizes.owner(group, way), sizes.place(group, way)
+    owner, place = jnp.split(owner, sizes.ch, axis=1), jnp.split(place, sizes.ch, axis=1)
     most = jnp.zeros((sizes.peers, 1), F32)
     for source in range(sizes.ch):
-        marks = iota((sizes.peers, sizes.channels), 0) == owner[source : source + 1]
+        marks = iota((sizes.peers, sizes.channels), 0) == owner[source]
         most = jnp.maximum(most, jnp.sum(jnp.where(marks, 1.0, 0.0), axis=1, keepdims=True))
     over_ref[...] = jnp.broadcast_to(jnp.max(most, axis=0, keepdims=True), (8, LANES)).astype(I32)
 
     earlier = jnp.zeros((sizes.own, 1), F32)
     into = jnp.zeros((256, sizes.ch * sizes.cap), F32)
     for source in range(sizes.ch):
-        mine = owner[source : source + 1] == me
-        where = jnp.where(mine, place[source : source + 1], -1)
+        mine = owner[source] == me
+        where = jnp.where(mine, place[source], -1)
         marks = iota((sizes.own, sizes.channels), 0) == where
         counts, totals = running_counts(hot(marks), upper)
         slot = jnp.sum(counts, axis=0, keepdims=True).astype(I32)
@@ -465,7 +480,7 @@
     return high + rest + low
 
 
-def index(sizes, me, all_groups, dest, params):
+def index(sizes, me, groups, dest, params):
     modes = params.shape[0] // 2
     return pl.pallas_call(
         functools.partial(index_kernel, sizes),
@@ -481,18 +496,20 @@
         compiler_params=pltpu.CompilerParams(vmem_limit_bytes=VMEM_LIMIT),
         cost_estimate=pl.CostEstimate(flops=2 * 10**9, bytes_accessed=10**6, transcendentals=0),
         name="index_rows",
-    )(me, all_groups, dest, params)
+    )(me, groups, dest, params)
 
 
 def local_kernel(
-    sizes, group_ref, param_ref, key_ref, value_ref, conv_ref, decay_ref, params, turned
+    sizes, me_ref, group_ref, param_ref, key_ref, value_ref, conv_ref, decay_ref, params, turned
 ):
     modes = param_ref.shape[0] // 2
     blocks = sizes.channels // LANES
     stacked = three_terms(param_ref[...])
     rows = 2 * modes
+    first_lane = pl.multiple_of((me_ref[0] & (sizes.ch - 1)) * sizes.channels, LANES)
+    groups = group_ref[:, pl.ds(first_lane, sizes.channels)]
     for start in range(0, sizes.channels, 256):
-        chosen = hot(iota((sizes.groups, 256), 0) == group_ref[:, start : start + 256])
+        chosen = hot(iota((sizes.groups, 256), 0) == groups[:, start : start + 256])
         found = three_sum(dot(stacked, chosen), 0)
         for half in range(2):
             block = start // LANES + half
@@ -536,12 +553,13 @@
     return terms[0]
 
 
-def local(sizes, shard_groups, params, key_proj, value_proj):
+def local(sizes, me, groups, params, key_proj, value_proj):
     modes = params.shape[0] // 2
     blocks = sizes.channels // LANES
     return pl.pallas_call(
         functools.partial(local_kernel, sizes),
-        in_specs=[pl.BlockSpec(memory_space=pltpu.VMEM)] * 4,
+        in_specs=[pl.BlockSpec(memory_space=pltpu.SMEM)]
+        + [pl.BlockSpec(memory_space=pltpu.VMEM)] * 4,
         out_shape=[
             jax.ShapeDtypeStruct((sizes.tokens * blocks, LANES), F32),
             jax.ShapeDtypeStruct((modes * blocks, LANES), F32),
@@ -553,7 +571,7 @@
         compiler_params=pltpu.CompilerParams(vmem_limit_bytes=VMEM_LIMIT),
         cost_estimate=pl.CostEstimate(flops=4 * 10**9, bytes_accessed=3 * 10**6, transcendentals=0),
         name="local_runs",
-    )(shard_groups, params, key_proj, value_proj)
+    )(me, groups, params, key_proj, value_proj)
 
 
 def owner_kernel(
@@ -564,6 +582,7 @@
     table_ref,
     leap_ref,
     out_ref,
+    merged,
     gated,
     weighted,
     states,
@@ -572,30 +591,29 @@
 ):
     run, runs, own, size = sizes.run, sizes.runs, sizes.own, sizes.size
     rows = own * size
-    lane = iota((rows, LANES), 1)
-    mirror = hot(iota((LANES, LANES), 0) + iota((LANES, LANES), 1) == LANES - 1)
     weighted[runs : 2 * runs + 1] = jnp.zeros((runs + 1, rows, LANES), BF16)
     for source in range(sizes.ctx):
         tail = recv_ref[source * sizes.ch, sizes.cap - 16 : sizes.cap, :].astype(F32)
-        ids = tail[15:16, :]
-        first = jnp.max(ids[:, :LANES]).astype(I32)
-        second = jnp.max(ids[:, LANES:]).astype(I32)
-        run_at[2 * source] = first
-        run_at[2 * source + 1] = second
+        run_at[2 * source] = tail[15, 0].astype(I32)
+        run_at[2 * source + 1] = tail[15, LANES].astype(I32)
+    lane = iota((rows, LANES), 1)
+    for source in range(sizes.ctx):
         block = recv_ref[source * sizes.ch : (source + 1) * sizes.ch]
-        block = block.reshape(sizes.ch * sizes.cap, 2 * LANES)
-        found = dot(into_ref[...], block)
-        mirrored = dot(found[:, :LANES].astype(BF16), mirror)
-        swapped = pltpu.roll(mirrored, run, 1)
-        gated[second] = jnp.where(lane < run, mirrored, swapped).astype(BF16)
-        gated[first] = jnp.where(lane < run, swapped, mirrored).astype(BF16)
-        value = found[:, LANES:]
-        turned = pltpu.roll(value, run, 1).astype(BF16)
-        value = value.astype(BF16)
-        weighted[first + 1, :, :run] = value[:, :run]
-        weighted[first, :, run:] = turned[:, run:]
-        weighted[second + 1, :, :run] = turned[:, :run]
-        weighted[second, :, run:] = value[:, run:]
+        found = dot(into_ref[...], block.reshape(sizes.ch * sizes.cap, 2 * LANES))
+        value = found[:, :LANES]
+        turned = pltpu.roll(value, run, 1)
+        merged[source, 0] = jnp.where(lane < run, value, turned).astype(BF16)
+        merged[source, 1] = jnp.where(lane < run, turned, value).astype(BF16)
+        merged[source, 2] = found[:, LANES:].astype(BF16)
+        merged[source, 3] = pltpu.roll(found[:, LANES:], run, 1).astype(BF16)
+    for source in range(sizes.ctx):
+        first, second = run_at[2 * source], run_at[2 * source + 1]
+        gated[first] = merged[source, 0]
+        gated[second] = merged[source, 1]
+        weighted[first + 1, :, :run] = merged[source, 2, :, :run]
+        weighted[first, :, run:] = merged[source, 3, :, run:]
+        weighted[second + 1, :, :run] = merged[source, 3, :, :run]
+        weighted[second, :, run:] = merged[source, 2, :, run:]
 
     modes = states.shape[1]
     group_lane = lax.shift_right_logical(iota((modes, rows), 1), bits(size))
@@ -663,6 +681,7 @@
         in_specs=[pl.BlockSpec(memory_space=pltpu.VMEM)] * 5,
         out_shape=jax.ShapeDtypeStruct((sizes.peers, 2 * modes, LANES), BF16),
         scratch_shapes=[
+            pltpu.VMEM((sizes.ctx, 4, rows, LANES), BF16),
             pltpu.VMEM((sizes.runs, rows, LANES), BF16),
             pltpu.VMEM((2 * sizes.runs + 1, rows, LANES), BF16),
             pltpu.VMEM((sizes.runs, modes, rows), F32),
@@ -768,29 +787,15 @@
 
 def owners_way(sizes, args):
     query_proj, key_proj, value_proj, cotangent, positions, group_of, decay_rates, residues = args
-    ch_rank = lax.axis_index("ch")
-    me = lax.axis_index("ctx") * sizes.ch + ch_rank
-    all_groups = group_of.reshape(sizes.ch, sizes.channels)
-    shard_groups = lax.dynamic_slice_in_dim(all_groups, ch_rank, 1)
-    sent, dest = pack(
-        sizes,
-        positions,
-        jnp.asarray(sizes.deal()),
-        all_groups,
-        shard_groups,
-        key_proj,
-        value_proj,
-        cotangent,
-        query_proj,
-    )
+    me = (lax.axis_index("ctx") * sizes.ch + lax.axis_index("ch")).reshape(1).astype(I32)
+    groups = group_of.reshape(1, -1)
+    sent, dest = pack(sizes, positions, groups, key_proj, value_proj, cotangent, query_proj)
     recv = exchange(sent)
 
     gains = residues * jnp.sqrt(2.0 * decay_rates)
     params = jnp.concatenate([decay_rates, gains], axis=1).T
-    conv, decay = local(sizes, shard_groups, params, key_proj, value_proj)
-    into, back, most, table, leap = index(
-        sizes, me.reshape(1).astype(I32), all_groups, dest, params
-    )
+    conv, decay = local(sizes, me, groups, params, key_proj, value_proj)
+    into, back, most, table, leap = index(sizes, me, groups, dest, params)
 
     def fast(recv, into, back, table, leap, dest, conv, decay, *args):
         returned = exchange(owner(sizes, recv, into, back, table, leap))

time: 73.6 us -> 69.9 us (0.950)
  Pallas kernels: 29.1 us -> 27.1 us
  local copies, waits for them, and re-layouts: 2.04 us -> 0.57 us
    pallas_call x1, Pallas kernels: 5.96 us -> 4.84 us  [owner(): pl.pallas_call(functools.partial(owner_kernel, sizes), in_specs=[pl.Block...]
    pallas_call x1, Pallas kernels: 7.63 us -> 6.63 us  [pack(): pl.pallas_call(functools.partial(pack_kernel, sizes), grid=(sizes.peers /...]
    reshape x1 -> x0, local copies, waits for them, and re-layouts: 0.78 us -> none  [owners_way(): all_groups = group_of.reshape(sizes.ch, sizes.channels)]
  transfers between devices with their start and end apart: 1 -> 1, of which waited for: 1 -> 1; matrix products, arithmetic and copies ran while one was open for 1% -> 1% of each run, Pallas kernels for 16% -> 17%
where the time goes in v2:
time: 69.9 us; the launch traced here: 69.1 us
  Pallas kernels  27.1 us (39%)
  waiting for transfers between devices  18.1 us (26%)
  blocking collectives  14.6 us (21%)
  starting transfers between devices  7.1 us (10%)
  between operations  1.44 us (2%)
    all_to_all x1, waiting for transfers between devices, exchange(): lax.all_to_all(blocks, ('ctx', 'ch'), split_axis=0, concat_axis=0, tiled=...  18.1 us
    all_to_all x1, blocking collectives, exchange(): lax.all_to_all(blocks, ('ctx', 'ch'), split_axis=0, concat_axis=0, tiled=...  14.6 us
    all_to_all x1, starting transfers between devices, exchange(): lax.all_to_all(blocks, ('ctx', 'ch'), split_axis=0, concat_axis=0, tiled=...  7.1 us
    pallas_call x1, Pallas kernels, local(): pl.pallas_call(functools.partial(local_kernel, sizes), in_specs=[pl.Block...  6.72 us
    pallas_call x1, Pallas kernels, pack(): pl.pallas_call(functools.partial(pack_kernel, sizes), grid=(sizes.peers /...  6.63 us
    pallas_call x1, Pallas kernels, index(): pl.pallas_call(functools.partial(index_kernel, sizes), in_specs=[pl.Block...  4.89 us
    pallas_call x1, Pallas kernels, owner(): pl.pallas_call(functools.partial(owner_kernel, sizes), in_specs=[pl.Block...  4.84 us
    pallas_call x1, Pallas kernels, finish(): pl.pallas_call(functools.partial(finish_kernel, sizes), in_specs=[pl.Bloc...  4.03 us
  transfers between devices with their start and end apart: 1, of which 1 were waited for; matrix products, arithmetic and copies ran while one was open for 1% of the time, Pallas kernels for 17%

profile of v2, /device:TPU:1, one launch (start us, length us, event | category | flops | bytes accessed | tf_op | source)
XLA Modules:
  0.0 69.1 jit_solution(11203500554339817242)
XLA Ops:
  0.6 0.0 copy-start.9
  0.6 0.0 copy-start.11
  0.7 0.0 copy-start.14
  0.7 6.6 %pack_rows.1 = (bf16[32,80,256]{2,1,0:T(8,128)(2,1)}, s32[8,2048]{1,0:T(8,128)S(1)}) custom-call(s32[128]{0:T(128)} %place_hbm.1, s32[1,8192]{1,0:T(1,128)} %bitcast.172, bf16[2048,128]{1,0:T(8,128)(2,1)} %key_ref.1, bf16[2048,128]{1,0:T(8,128)(2,1)} %value_ref.1, bf16[2048,128]{1,0:T(8,128)(2,1)} %cot_hbm.1, bf16[2048,128]{1,0:T(8,128)(2,1)} %query_hbm.1), custom_call_target="tpu_custom_call" | custom-call | tf_op jit(solution)/shard_map/pack_rows/pallas_call | solution.py:381
  7.3 0.0 copy-start.12
  7.3 7.1 %all-to-all-start.7 = ((bf16[32,80,256]{2,1,0:T(8,128)(2,1)}), bf16[32,80,256]{2,1,0:T(8,128)(2,1)S(1)}, u32[]{:S(2)}, u32[]{:S(2)}) async-start(bf16[32,80,256]{2,1,0:T(8,128)(2,1)} %get-tuple-element.64), calls=%async_computation.7 | async-start | bytes 2621440 | tf_op jit(solution)/shard_map/all_to_all | solution.py:785
  14.4 0.0 copy-done.9
  14.4 0.0 copy-done.11
  14.5 0.0 copy-done.14
  14.5 0.0 copy-start.5
  14.5 0.0 copy-start.6
  14.5 4.9 %index_rows.1 = (bf16[256,320]{1,0:T(8,128)(2,1)}, bf16[256,512]{1,0:T(8,128)(2,1)}, s32[8,128]{1,0:T(8,128)S(1)}, bf16[256,128]{1,0:T(8,128)(2,1)}, f32[16,256]{1,0:T(8,128)S(1)}) custom-call(s32[1]{0:T(128)} %bitcast.46.me_ref, s32[1,8192]{1,0:T(1,128)S(1)} %bitcast.173, s32[8,2048]{1,0:T(8,128)S(1)} %get-tuple-element.62.dest_ref, ...), custom_call_target="tpu_custom_call" | custom-call | flops 2000000000 | bytes 1000000 | tf_op jit(solution)/shard_map/index_rows/pallas_call | solution.py:485
  19.4 0.0 copy-done.12
  19.4 0.5 slice.39
  20.6 0.0 copy-done.5
  20.6 0.0 copy-done.6
  20.6 0.0 copy-start.3
  20.6 0.0 copy-start.7
  20.6 0.0 copy-start.16
  20.6 6.7 %local_runs.1 = (f32[2048,128]{1,0:T(8,128)}, f32[256,128]{1,0:T(8,128)}) custom-call(s32[1]{0:T(128)} %bitcast.46.me_ref, s32[1,8192]{1,0:T(1,128)S(1)} %bitcast.174, f32[32,512]{1,0:T(8,128)S(1)} %maximum_bitcast_fusion.param_ref, bf16[2048,128]{1,0:T(8,128)(2,1)S(1)} %copy-done.5, bf16[2048,128]{1,0:T(8,128)(2,1)S(1)} %copy-done.6), custom_call_target="tpu_custom_call" | custom-call | flops 4000000000 | bytes 3000000 | tf_op jit(solution)/shard_map/local_runs/pallas_call | solution.py:559
  27.3 18.1 %all-to-all-done.7 = bf16[32,80,256]{2,1,0:T(8,128)(2,1)S(1)} async-done(((bf16[32,80,256]{2,1,0:T(8,128)(2,1)}), bf16[32,80,256]{2,1,0:T(8,128)(2,1)S(1)}, u32[]{:S(2)}, u32[]{:S(2)}) %all-to-all-start.7) | async-done | bytes 1310752 | tf_op jit(solution)/shard_map/all_to_all | solution.py:785
  45.4 0.0 copy-done.3
  45.4 0.0 copy-done.7
  45.4 0.0 copy-done.16
  45.4 23.7 %conditional.1 = ((bf16[2048,128]{1,0:T(8,128)(2,1)}, f32[128,128]{1,0:T(8,128)})) conditional(s32[]{:T(128)} %bitcast.49, (bf16[2048,128]{1,0:T(8,128)(2,1)S(1)}, s32[8192]{0:T(1024)S(1)}, f32[512,16]{0,1:T(8,128)S(1)}, f32[512,16]{0,1:T(8,128)S(1)}, bf16[2048,128]{1,0:T(8,128)(2,1)S(1)}, /*index=5*/bf16[2048,128]{1,0:T(8,128)(2,1)S(1)}, ...), branch_computations={%region_0.4_spmd, %region_4.5_spmd} | conditional | flops 10720338944 | bytes 257407616 | solution.py:807
  45.7 0.0 copy-start.8
  45.7 0.0 copy-start.10
  45.7 0.0 copy-start.13
  45.7 4.8 %owner_sums.1 = bf16[32,32,128]{2,1,0:T(8,128)(2,1)S(1)} custom-call(bf16[32,80,256]{2,1,0:T(8,128)(2,1)S(1)} %get-tuple-element.42.recv_ref, bf16[256,320]{1,0:T(8,128)(2,1)} %get-tuple-element.43.into_ref, bf16[256,512]{1,0:T(8,128)(2,1)} %get-tuple-element.44.back_ref, bf16[256,128]{1,0:T(8,128)(2,1)} %get-tuple-element.45.table_ref, ...), custom_call_target="tpu_custom_call" | custom-call | tf_op jit(solution)/shard_map/cond/branch_1_fun/owner_sums/pallas_call | solution.py:679
  50.5 14.6 %all_to_all.68.recv_ref = bf16[32,32,128]{2,1,0:T(8,128)(2,1)S(1)} all-to-all(bf16[32,32,128]{2,1,0:T(8,128)(2,1)S(1)} %owner_sums.1), channel_id=1, replica_groups=mesh['ctx'=8,'ch'=4] {'ctx','ch'}, dimensions={0} | all-to-all | bytes 524288 | tf_op jit(solution)/shard_map/cond/branch_1_fun/all_to_all | solution.py:785
  65.1 0.0 copy-done.10
  65.1 4.0 %finish_rows.1 = (bf16[2048,128]{1,0:T(8,128)(2,1)}, f32[128,128]{1,0:T(8,128)}) custom-call(bf16[32,32,128]{2,1,0:T(8,128)(2,1)S(1)} %all_to_all.68.recv_ref, s32[8,2048]{1,0:T(8,128)S(1)} %copy-done.13, f32[2048,128]{1,0:T(8,128)S(1)} %copy-done.8, f32[256,128]{1,0:T(8,128)S(1)} %copy-done.10, bf16[2048,128]{1,0:T(8,128)(2,1)S(1)} %get-tuple-element.50.query_ref), custom_call_target="tpu_custom_call" | custom-call | tf_op jit(solution)/shard_map/cond/branch_1_fun/finish_rows/pallas_call | solution.py:768
  (4 shorter events, 0.0 us)
Async XLA Ops:
  0.6 13.8 %copy-start.9 = (f32[512,16]{0,1:T(8,128)S(1)}, f32[512,16]{0,1:T(8,128)}, u32[]{:S(2)}) copy-start(f32[512,16]{0,1:T(8,128)} %param.16) | copy-start | bytes 98308
  0.6 13.8 %copy-start.11 = (f32[512,16]{0,1:T(8,128)S(1)}, f32[512,16]{0,1:T(8,128)}, u32[]{:S(2)}) copy-start(f32[512,16]{0,1:T(8,128)} %param.17) | copy-start | bytes 98308
  0.7 13.8 %copy-start.14 = (s32[8192]{0:T(1024)S(1)}, s32[8192]{0:T(1024)}, u32[]{:S(2)}) copy-start(s32[8192]{0:T(1024)} %param.15) | copy-start | bytes 98308
  7.3 12.1 %copy-start.12 = (s32[8,2048]{1,0:T(8,128)}, s32[8,2048]{1,0:T(8,128)S(1)}, u32[]{:S(2)}) copy-start(s32[8,2048]{1,0:T(8,128)S(1)} %get-tuple-element.62.dest_ref) | copy-start | bytes 196612
  7.3 38.1 %all-to-all-start.7 = ((bf16[32,80,256]{2,1,0:T(8,128)(2,1)}), bf16[32,80,256]{2,1,0:T(8,128)(2,1)S(1)}, u32[]{:S(2)}, u32[]{:S(2)}) async-start(bf16[32,80,256]{2,1,0:T(8,128)(2,1)} %get-tuple-element.64), calls=%async_computation.7 | async-start | bytes 2621440 | tf_op jit(solution)/shard_map/all_to_all | solution.py:785
  14.5 6.1 %copy-start.5 = (bf16[2048,128]{1,0:T(8,128)(2,1)S(1)}, bf16[2048,128]{1,0:T(8,128)(2,1)}, u32[]{:S(2)}) copy-start(bf16[2048,128]{1,0:T(8,128)(2,1)} %key_ref.1) | copy-start | bytes 1572868
  14.5 6.1 %copy-start.6 = (bf16[2048,128]{1,0:T(8,128)(2,1)S(1)}, bf16[2048,128]{1,0:T(8,128)(2,1)}, u32[]{:S(2)}) copy-start(bf16[2048,128]{1,0:T(8,128)(2,1)} %value_ref.1) | copy-start | bytes 1572868
  20.6 24.8 %copy-start.3 = (bf16[2048,128]{1,0:T(8,128)(2,1)S(1)}, bf16[2048,128]{1,0:T(8,128)(2,1)}, u32[]{:S(2)}) copy-start(bf16[2048,128]{1,0:T(8,128)(2,1)} %query_hbm.1) | copy-start | bytes 1572868
  20.6 24.8 %copy-start.7 = (bf16[2048,128]{1,0:T(8,128)(2,1)S(1)}, bf16[2048,128]{1,0:T(8,128)(2,1)}, u32[]{:S(2)}) copy-start(bf16[2048,128]{1,0:T(8,128)(2,1)} %cot_hbm.1) | copy-start | bytes 1572868
  20.6 24.8 %copy-start.16 = (s32[128]{0:T(128)S(1)}, s32[128]{0:T(128)}, u32[]{:S(2)}) copy-start(s32[128]{0:T(128)} %place_hbm.1) | copy-start | bytes 1540
  45.7 19.4 %copy-start.8 = (f32[2048,128]{1,0:T(8,128)S(1)}, f32[2048,128]{1,0:T(8,128)}, u32[]{:S(2)}) copy-start(f32[2048,128]{1,0:T(8,128)} %get-tuple-element.48.conv_ref) | copy-start | bytes 3145732 | tf_op jit(solution)/shard_map/cond
  45.7 19.4 %copy-start.10 = (f32[256,128]{1,0:T(8,128)S(1)}, f32[256,128]{1,0:T(8,128)}, u32[]{:S(2)}) copy-start(f32[256,128]{1,0:T(8,128)} %get-tuple-element.49.decay_ref) | copy-start | bytes 393220 | tf_op jit(solution)/shard_map/cond
  45.7 19.4 %copy-start.13 = (s32[8,2048]{1,0:T(8,128)S(1)}, s32[8,2048]{1,0:T(8,128)}, u32[]{:S(2)}) copy-start(s32[8,2048]{1,0:T(8,128)} %get-tuple-element.47.dest_ref) | copy-start | bytes 196612 | tf_op jit(solution)/shard_map/cond

commit v3 on v2

--- a/solution.py
+++ b/solution.py
@@ -216,6 +216,7 @@
         self.own = groups // self.peers
         self.size = channels * ch // groups
         self.cap = 80
+        self.rest = LANES - self.cap
         powers = [self.block, max(self.each, 1), self.own, self.size]
         self.fits = (
             tokens == LANES
@@ -332,60 +333,53 @@
     data,
     arrived,
 ):
-    part = out_ref.shape[0]
-
-    @pl.when(pl.program_id(0) == 0)
-    def _():
-        moves = [(group_hbm, group_ref), (place_hbm, place_ref)]
-        for at, source in enumerate((key_hbm, value_hbm, cot_hbm, query_hbm)):
-            moves.append((source, inputs.at[at]))
-        copies = [
-            pltpu.make_async_copy(source, target, arrived.at[at])
-            for at, (source, target) in enumerate(moves)
-        ]
-        for copy in copies:
-            copy.start()
-        copies[0].wait()
-        way = choose_way(sizes, group_ref[...])
-        first = pl.multiple_of(lax.axis_index("ch") * sizes.channels, LANES)
-        owner = sizes.owner(group_ref[:, pl.ds(first, sizes.channels)], way)
-        marks = iota((sizes.peers, sizes.channels), 0) == owner
-        counts, _ = running_counts(hot(marks), upper_ones(256))
-        slot = jnp.sum(jnp.where(marks, counts, 0.0), axis=0, keepdims=True).astype(I32)
-        dest_ref[0:1, :] = jnp.where(slot < sizes.cap - 1, owner * sizes.cap + slot, -1)
-        dest_ref[1:2, :] = owner
-        dest_ref[2:3, :] = slot
-        for row in range(3):
-            dest_ref[3 + row : 4 + row, :] = jnp.broadcast_to(way[row], (1, sizes.channels))
-        dest_ref[6:8, :] = jnp.zeros((2, sizes.channels), I32)
-        for copy in copies[1:]:
-            copy.wait()
-        across = iota((LANES, LANES), 0) ^ iota((LANES, LANES), 1)
-        gated = (inputs[0].astype(F32) * inputs[1].astype(F32)).astype(BF16)
-        data[:, :LANES] = dot(gated, hot(across == sizes.run - 1)).astype(BF16)
-        data[:, LANES:] = (inputs[2].astype(F32) * inputs[3].astype(F32)).astype(BF16)
+    moves = [(group_hbm, group_ref), (place_hbm, place_ref)]
+    for at, source in enumerate((key_hbm, value_hbm, cot_hbm, query_hbm)):
+        moves.append((source, inputs.at[at]))
+    copies = [
+        pltpu.make_async_copy(source, target, arrived.at[at])
+        for at, (source, target) in enumerate(moves)
+    ]
+    for copy in copies:
+        copy.start()
+    copies[0].wait()
+    way = choose_way(sizes, group_ref[...])
+    first = pl.multiple_of(lax.axis_index("ch") * sizes.channels, LANES)
+    owner = sizes.owner(group_ref[:, pl.ds(first, sizes.channels)], way)
+    marks = iota((sizes.peers, sizes.channels), 0) == owner
+    counts, _ = running_counts(hot(marks), upper_ones(256))
+    slot = jnp.sum(jnp.where(marks, counts, 0.0), axis=0, keepdims=True).astype(I32)
+    dest_ref[0:1, :] = jnp.where(slot < sizes.cap - 1, owner * sizes.cap + slot, -1)
+    dest_ref[1:2, :] = owner
+    dest_ref[2:3, :] = slot
+    for row in range(3):
+        dest_ref[3 + row : 4 + row, :] = jnp.broadcast_to(way[row], (1, sizes.channels))
+    dest_ref[6:8, :] = jnp.zeros((2, sizes.channels), I32)
+    for copy in copies[1:]:
+        copy.wait()
+    across = iota((LANES, LANES), 0) ^ iota((LANES, LANES), 1)
+    gated = (inputs[0].astype(F32) * inputs[1].astype(F32)).astype(BF16)
+    data[:, :LANES] = dot(gated, hot(across == sizes.run - 1)).astype(BF16)
+    data[:, LANES:] = (inputs[2].astype(F32) * inputs[3].astype(F32)).astype(BF16)
 
     shift = bits(sizes.run)
     first = lax.shift_right_logical(place_ref[0], shift)
     second = lax.shift_right_logical(place_ref[sizes.run], shift)
     run_row = jnp.where(iota((1, 1, 2 * LANES), 2) < LANES, first, second).astype(F32)
-    base = pl.program_id(0) * part * sizes.cap
-    chosen = hot(iota((part * sizes.cap, sizes.channels), 0) == dest_ref[0:1, :] - base)
-    rows = dot(chosen, data[...]).reshape(part, sizes.cap, 2 * LANES)
+    part = 16
     spare = iota((part, sizes.cap, 1), 1) == sizes.cap - 1
-    out_ref[...] = jnp.where(spare, run_row, rows).astype(BF16)
+    for start in range(0, sizes.peers, part):
+        base = start * sizes.cap
+        chosen = hot(iota((part * sizes.cap, sizes.channels), 0) == dest_ref[0:1, :] - base)
+        rows = dot(chosen, data[...]).reshape(part, sizes.cap, 2 * LANES)
+        out_ref[start : start + part] = jnp.where(spare, run_row, rows).astype(BF16)
 
 
 def pack(sizes, positions, groups, key_proj, value_proj, cotangent, query_proj):
-    part = 16
     return pl.pallas_call(
         functools.partial(pack_kernel, sizes),
-        grid=(sizes.peers // part,),
         in_specs=[pl.BlockSpec(memory_space=pl.ANY)] * 6,
-        out_specs=[
-            pl.BlockSpec((part, sizes.cap, 2 * LANES), lambda step: (step, 0, 0)),
-            pl.BlockSpec((8, sizes.channels), lambda step: (0, 0)),
-        ],
+        out_specs=[pl.BlockSpec(memory_space=pltpu.VMEM)] * 2,
         out_shape=[
             jax.ShapeDtypeStruct((sizes.peers, sizes.cap, 2 * LANES), BF16),
             jax.ShapeDtypeStruct((8, sizes.channels), I32),
@@ -439,9 +433,18 @@
         row = jnp.where(mine, where * sizes.size + nth, -1)
         column = jnp.where(mine & (slot < sizes.cap - 1), slot, -1)
         to_row = hot(iota((256, sizes.channels), 0) == row)
-        to_column = hot(iota((LANES, sizes.channels), 0) == column)
-        found = dot_lanes(to_row, to_column).astype(BF16)
-        back_ref[:, source * LANES : (source + 1) * LANES] = found
+        in_front = (column >= 0) & (column < sizes.rest)
+        columns = (
+            column,
+            jnp.where(in_front, column + sizes.cap, -1),
+            jnp.where(column >= sizes.rest, column + sizes.cap - sizes.rest, -1),
+        )
+        for at, wanted in enumerate(columns):
+            to_column = hot(iota((LANES, sizes.channels), 0) == wanted)
+            back_ref[at, :, source * LANES : (source + 1) * LANES] = dot_lanes(
+                to_row, to_column
+            ).astype(BF16)
+        found = back_ref[0, :, source * LANES : (source + 1) * LANES]
         shape = (LANES, sizes.ch * sizes.cap)
         moved = hot(
             (iota(shape, 1) == iota(shape, 0) + source * sizes.cap)
@@ -488,7 +491,7 @@
         + [pl.BlockSpec(memory_space=pltpu.VMEM)] * 3,
         out_shape=[
             jax.ShapeDtypeStruct((256, sizes.ch * sizes.cap), BF16),
-            jax.ShapeDtypeStruct((256, sizes.ch * LANES), BF16),
+            jax.ShapeDtypeStruct((3, 256, sizes.ch * LANES), BF16),
             jax.ShapeDtypeStruct((8, LANES), I32),
             jax.ShapeDtypeStruct((256, 2 * sizes.run), BF16),
             jax.ShapeDtypeStruct((modes, 256), F32),
@@ -648,28 +651,38 @@
 
     lax.fori_loop(0, own, one_group, 0, unroll=True)
 
-    each = sizes.each
-    quarter = LANES // 4
-    out_lane = iota((32, LANES), 1)
+    each, cap, rest = sizes.each, sizes.cap, sizes.rest
+    wide = 2 * modes - 8
+    few_lags = LANES // 2 - rest
+    pairs = [
+        jnp.concatenate([states[run_at[2 * target]], states[run_at[2 * target + 1]]], axis=0)
+        for target in range(sizes.ctx)
+    ]
+    front = dot(jnp.concatenate(pairs, axis=0).astype(BF16), back_ref[0])
+    last = jnp.concatenate([pair[wide:] for pair in pairs], axis=0).astype(BF16)
+    second, third = dot(last, back_ref[1]), dot(last, back_ref[2])
+    out_lane = iota((8, LANES), 1)
     for target in range(sizes.ctx):
-        pair = jnp.concatenate(
-            [states[run_at[2 * target]], states[run_at[2 * target + 1]]], axis=0
-        )
-        sent = dot(pair.astype(BF16), back_ref[...])
         lags = sums[:, target * LANES : (target + 1) * LANES]
-        high = lags.astype(BF16).astype(F32)
-        low = lags - high
-        moved = [
-            [pltpu.roll(term, (7 * quarter - q * quarter) % LANES, 1) for q in range(4)]
-            for term in (high, low)
-        ]
+        moves = [(cap, cap - rest), (LANES - few_lags - 2 * rest, LANES - 2 * few_lags - 2 * rest)]
+        moved = [[pltpu.roll(lags, shift % LANES, 1) for shift in pair] for pair in moves]
         for chan in range(sizes.ch):
-            lag_rows = jnp.concatenate(
-                [part[chan * each : (chan + 1) * each] for term in moved for part in term], axis=0
-            )
-            mine = sent[:, chan * LANES : (chan + 1) * LANES]
-            out_ref[target * sizes.ch + chan] = jnp.where(
-                out_lane < 3 * quarter, mine, lag_rows
+            at = slice(chan * LANES, (chan + 1) * LANES)
+            mine = slice(chan * each, (chan + 1) * each)
+            most, few = [jnp.concatenate([part[mine] for part in pair], axis=0) for pair in moved]
+            head = front[target * 2 * modes : target * 2 * modes + wide, at]
+            tail = slice(target * 8, (target + 1) * 8)
+            beside = [
+                second[tail, at],
+                jnp.where(out_lane < LANES - few_lags, third[tail, at], few),
+                most,
+            ]
+            out_ref[target * sizes.ch + chan] = jnp.concatenate(
+                [
+                    jnp.where(out_lane < cap, head[8 * row : 8 * row + 8], beside[row])
+                    for row in range(3)
+                ],
+                axis=0,
             ).astype(BF16)
 
 
@@ -679,7 +692,7 @@
     return pl.pallas_call(
         functools.partial(owner_kernel, sizes),
         in_specs=[pl.BlockSpec(memory_space=pltpu.VMEM)] * 5,
-        out_shape=jax.ShapeDtypeStruct((sizes.peers, 2 * modes, LANES), BF16),
+        out_shape=jax.ShapeDtypeStruct((sizes.peers, 2 * modes - 8, LANES), BF16),
         scratch_shapes=[
             pltpu.VMEM((sizes.ctx, 4, rows, LANES), BF16),
             pltpu.VMEM((sizes.runs, rows, LANES), BF16),
@@ -697,25 +710,45 @@
     sizes, recv_ref, dest_ref, conv_ref, decay_ref, query_ref, out_ref, grad_ref, found, total
 ):
     blocks = sizes.channels // LANES
-    rows = recv_ref.shape[1]
+    wide = recv_ref.shape[1]
+    rows = wide + 8
     modes = rows // 2
-    everything = recv_ref[...].reshape(sizes.peers * rows, LANES)
-
-    def fetch(part, carry):
-        at = pl.ds(pl.multiple_of(part * 256, 256), 256)
+    cap, rest = sizes.cap, sizes.rest
+    halves = sizes.peers // 2
+    both = recv_ref[...].reshape(halves, 2, wide, LANES)
+    both = jnp.concatenate([both[:, 0], both[:, 1]], axis=2)
+    front = both.reshape(halves * wide, 2 * LANES)
+    second = both[:, :8].astype(F32).reshape(halves * 8, 2 * LANES).astype(BF16)
+    third = both[:, 8:16].astype(F32).reshape(halves * 8, 2 * LANES).astype(BF16)
+
+    def fetch(part):
+        at = pl.ds(part * 256, 256)
         owner, slot = dest_ref[1:2, at], dest_ref[2:3, at]
-        chosen = hot(iota((LANES, 256), 0) == slot)
-        picked = dot(everything, chosen)
-        mine = jnp.zeros((rows, 256), F32)
-        for peer in range(sizes.peers):
-            mine = mine + jnp.where(owner == peer, picked[peer * rows : (peer + 1) * rows], 0.0)
-        for half in range(2):
-            start = pl.multiple_of((2 * part + half) * rows, rows)
-            found[pl.ds(start, rows), :] = mine[:, half * LANES : (half + 1) * LANES]
-        return carry
-
-    lax.fori_loop(0, sizes.channels // 256, fetch, 0, unroll=True)
+        half, offset = lax.shift_right_logical(owner, 1), (owner & 1) * LANES
+        lane = iota((2 * LANES, 256), 0)
+        in_second = jnp.where(slot < rest, slot + cap + offset, -1)
+        in_third = jnp.where(slot >= rest, slot + cap - rest + offset, -1)
+        most = dot(front, hot(lane == slot + offset))
+        few = dot(second, hot(lane == in_second)) + dot(third, hot(lane == in_third))
+        mine = [jnp.zeros((wide, 256), F32), jnp.zeros((8, 256), F32)]
+        for peer in range(halves):
+            mine[0] = mine[0] + jnp.where(half == peer, most[peer * wide : (peer + 1) * wide], 0.0)
+            mine[1] = mine[1] + jnp.where(half == peer, few[peer * 8 : (peer + 1) * 8], 0.0)
+        for side in range(2):
+            start = (2 * part + side) * rows
+            for piece, first in zip(mine, (0, wide)):
+                found[pl.ds(start + first, piece.shape[0]), :] = piece[
+                    :, side * LANES : (side + 1) * LANES
+                ]
+
+    def turn(block):
+        at = pl.ds(block * LANES, LANES)
+        conv = total[pl.ds(block, sizes.tokens, stride=blocks), :].astype(BF16).T
+        out_ref[at, :] = (query_ref[at, :].astype(F32) * conv.astype(F32)).astype(BF16)
+
     for first in range(0, blocks, 8):
+        for part in range(first // 2, first // 2 + 4):
+            fetch(part)
         decays = [
             decay_ref[mode * blocks + first : mode * blocks + first + 8, :]
             for mode in range(modes)
@@ -733,34 +766,27 @@
                 total[at, :] = conv_ref[at, :] + tree_sum(states)
                 return states
 
-            lax.fori_loop(0, sizes.run, step, states, unroll=8)
-
-    def turn(block, carry):
-        at = pl.ds(pl.multiple_of(block * LANES, LANES), LANES)
-        conv = total[pl.ds(block, sizes.tokens, stride=blocks), :].T.astype(BF16)
-        out_ref[at, :] = (query_ref[at, :].astype(F32) * conv.astype(F32)).astype(BF16)
-        return carry
-
-    lax.fori_loop(0, blocks, turn, 0, unroll=True)
-
-    each, quarter = sizes.each, LANES // 4
-    high_low = recv_ref[...].astype(F32)
-    terms = []
-    lane_part = lax.shift_right_logical(iota((sizes.peers * 16, LANES), 1), 5)
-    row = iota((sizes.peers * 16, LANES), 0)
-    row_part = lax.shift_right_logical(row & 15, bits(each))
-    for term in range(2):
-        piece = high_low[:, term * 16 : (term + 1) * 16, :].reshape(sizes.peers * 16, LANES)
-        placed = jnp.zeros((sizes.peers * 16, LANES), F32)
-        for part in range(4):
-            moved = pltpu.roll(piece, (part * quarter + quarter) % LANES, 1)
-            placed = jnp.where((row_part == part) & (lane_part == part), moved, placed)
-        terms.append(placed.astype(BF16))
-    come = iota((1, sizes.peers * 16), 1)
-    seat = lax.shift_right_logical(come, 4) * each + (come & (each - 1))
+            lax.fori_loop(0, sizes.run, step, states, unroll=True)
+        for block in range(first, first + 8):
+            turn(block)
+
+    each, few_lags = sizes.each, LANES // 2 - rest
+    shape = (sizes.peers * 8, LANES)
+    upper = lax.shift_right_logical(iota(shape, 0) & 7, bits(each)) == 1
+    lane = iota(shape, 1)
+    placed = jnp.zeros(shape, F32)
+    for rows_at, count, come, go in ((16, rest, cap, 0), (8, few_lags, LANES - few_lags, 2 * rest)):
+        piece = recv_ref[:, rows_at : rows_at + 8, :].astype(F32).reshape(shape)
+        for part in range(2):
+            start = go + part * count
+            moved = pltpu.roll(piece, (start - come) % LANES, 1)
+            here = (upper == (part == 1)) & (lane >= start) & (lane < start + count)
+            placed = jnp.where(here, moved, placed)
+    come = iota((1, sizes.peers * 8), 1)
+    seat = lax.shift_right_logical(come, 3) * each + (come & (each - 1))
     wanted = sizes.group_at(seat, way_of(dest_ref))
-    chosen = hot(iota((sizes.block, sizes.peers * 16), 0) == wanted)
-    grad_ref[...] = dot(chosen, terms[0]) + dot(chosen, terms[1])
+    chosen = hot(iota((sizes.block, sizes.peers * 8), 0) == wanted)
+    grad_ref[...] = dot(chosen, placed.astype(BF16))
 
 
 def finish(sizes, recv, dest, conv, decay, query_proj):
@@ -773,7 +799,7 @@
             jax.ShapeDtypeStruct((sizes.block, LANES), F32),
         ],
         scratch_shapes=[
-            pltpu.VMEM((blocks * recv.shape[1], LANES), F32),
+            pltpu.VMEM((blocks * (recv.shape[1] + 8), LANES), F32),
             pltpu.VMEM((sizes.tokens * blocks, LANES), F32),
         ],
         compiler_params=pltpu.CompilerParams(vmem_limit_bytes=VMEM_LIMIT),

time: 69.9 us -> 67.6 us (0.967)
  blocking collectives: 14.6 us -> 13.5 us
  waiting for transfers between devices: 18.1 us -> 17.2 us
    all_to_all x1, blocking collectives: 14.6 us -> 13.5 us  [exchange(): lax.all_to_all(blocks, ('ctx', 'ch'), split_axis=0, concat_axis=0, tiled=...]
    all_to_all x1, waiting for transfers between devices: 18.1 us -> 17.2 us  [exchange(): lax.all_to_all(blocks, ('ctx', 'ch'), split_axis=0, concat_axis=0, tiled=...]
    pallas_call x1, Pallas kernels: 4.89 us -> 5.78 us  [index(): pl.pallas_call(functools.partial(index_kernel, sizes), in_specs=[pl.Block...]
  transfers between devices with their start and end apart: 1 -> 1, of which waited for: 1 -> 1; matrix products, arithmetic and copies ran while one was open for 1% -> 1% of each run, Pallas kernels for 17% -> 19%
where the time goes in v3:
time: 67.6 us; the launch traced here: 67.4 us
  Pallas kernels  27.3 us (40%)
  waiting for transfers between devices  17.2 us (25%)
  blocking collectives  13.5 us (20%)
  starting transfers between devices  7.1 us (11%)
  between operations  1.44 us (2%)
    all_to_all x1, waiting for transfers between devices, exchange(): lax.all_to_all(blocks, ('ctx', 'ch'), split_axis=0, concat_axis=0, tiled=...  17.2 us
    all_to_all x1, blocking collectives, exchange(): lax.all_to_all(blocks, ('ctx', 'ch'), split_axis=0, concat_axis=0, tiled=...  13.5 us
    all_to_all x1, starting transfers between devices, exchange(): lax.all_to_all(blocks, ('ctx', 'ch'), split_axis=0, concat_axis=0, tiled=...  7.1 us
    pallas_call x1, Pallas kernels, local(): pl.pallas_call(functools.partial(local_kernel, sizes), in_specs=[pl.Block...  6.72 us
    pallas_call x1, Pallas kernels, pack(): pl.pallas_call(functools.partial(pack_kernel, sizes), in_specs=[pl.BlockS...  6.3 us
    pallas_call x1, Pallas kernels, index(): pl.pallas_call(functools.partial(index_kernel, sizes), in_specs=[pl.Block...  5.78 us
    pallas_call x1, Pallas kernels, owner(): pl.pallas_call(functools.partial(owner_kernel, sizes), in_specs=[pl.Block...  4.9 us
    pallas_call x1, Pallas kernels, finish(): pl.pallas_call(functools.partial(finish_kernel, sizes), in_specs=[pl.Bloc...  3.56 us
  transfers between devices with their start and end apart: 1, of which 1 were waited for; matrix products, arithmetic and copies ran while one was open for 1% of the time, Pallas kernels for 19%

profile of v3, /device:TPU:1, one launch (start us, length us, event | category | flops | bytes accessed | tf_op | source)
XLA Modules:
  0.0 67.4 jit_solution(4221580073522563770)
XLA Ops:
  0.6 0.0 copy-start.9
  0.6 0.0 copy-start.10
  0.7 0.0 copy-start.14
  0.7 6.3 %pack_rows.1 = (bf16[32,80,256]{2,1,0:T(8,128)(2,1)}, s32[8,2048]{1,0:T(8,128)S(1)}) custom-call(s32[128]{0:T(128)} %place_hbm.1, s32[1,8192]{1,0:T(1,128)} %bitcast.172, bf16[2048,128]{1,0:T(8,128)(2,1)} %key_ref.1, bf16[2048,128]{1,0:T(8,128)(2,1)} %value_ref.1, bf16[2048,128]{1,0:T(8,128)(2,1)} %cot_hbm.1, bf16[2048,128]{1,0:T(8,128)(2,1)} %query_hbm.1), custom_call_target="tpu_custom_call" | custom-call | tf_op jit(solution)/shard_map/pack_rows/pallas_call | solution.py:379
  7.0 0.0 copy-start.12
  7.0 7.1 %all-to-all-start.7 = ((bf16[32,80,256]{2,1,0:T(8,128)(2,1)}), bf16[32,80,256]{2,1,0:T(8,128)(2,1)S(1)}, u32[]{:S(2)}, u32[]{:S(2)}) async-start(bf16[32,80,256]{2,1,0:T(8,128)(2,1)} %get-tuple-element.64), calls=%async_computation.7 | async-start | bytes 2621440 | tf_op jit(solution)/shard_map/all_to_all | solution.py:811
  14.1 0.0 copy-done.9
  14.1 0.0 copy-done.10
  14.1 0.0 copy-done.14
  14.2 0.0 copy-start.5
  14.2 0.0 copy-start.6
  14.2 5.8 %index_rows.1 = (bf16[256,320]{1,0:T(8,128)(2,1)}, bf16[3,256,512]{2,1,0:T(8,128)(2,1)}, s32[8,128]{1,0:T(8,128)S(1)}, bf16[256,128]{1,0:T(8,128)(2,1)}, f32[16,256]{1,0:T(8,128)S(1)}) custom-call(s32[1]{0:T(128)} %bitcast.46.me_ref, s32[1,8192]{1,0:T(1,128)S(1)} %bitcast.173, s32[8,2048]{1,0:T(8,128)S(1)} %get-tuple-element.62.dest_ref, ...), custom_call_target="tpu_custom_call" | custom-call | flops 2000000000 | bytes 1000000 | tf_op jit(solution)/shard_map/index_rows/pallas_call | solution.py:488
  20.0 0.0 copy-done.12
  20.0 0.5 slice.39
  21.1 0.0 copy-done.5
  21.1 0.0 copy-done.6
  21.1 0.0 copy-start.3
  21.2 0.0 copy-start.7
  21.2 0.0 copy-start.16
  21.2 6.7 %local_runs.1 = (f32[2048,128]{1,0:T(8,128)}, f32[256,128]{1,0:T(8,128)}) custom-call(s32[1]{0:T(128)} %bitcast.46.me_ref, s32[1,8192]{1,0:T(1,128)S(1)} %bitcast.174, f32[32,512]{1,0:T(8,128)S(1)} %maximum_bitcast_fusion.param_ref, bf16[2048,128]{1,0:T(8,128)(2,1)S(1)} %copy-done.5, bf16[2048,128]{1,0:T(8,128)(2,1)S(1)} %copy-done.6), custom_call_target="tpu_custom_call" | custom-call | flops 4000000000 | bytes 3000000 | tf_op jit(solution)/shard_map/local_runs/pallas_call | solution.py:562
  27.9 17.2 %all-to-all-done.7 = bf16[32,80,256]{2,1,0:T(8,128)(2,1)S(1)} async-done(((bf16[32,80,256]{2,1,0:T(8,128)(2,1)}), bf16[32,80,256]{2,1,0:T(8,128)(2,1)S(1)}, u32[]{:S(2)}, u32[]{:S(2)}) %all-to-all-start.7) | async-done | bytes 1310752 | tf_op jit(solution)/shard_map/all_to_all | solution.py:811
  45.1 0.0 copy-done.3
  45.1 0.0 copy-done.7
  45.1 0.0 copy-done.16
  45.1 22.3 %conditional.1 = ((bf16[2048,128]{1,0:T(8,128)(2,1)}, f32[128,128]{1,0:T(8,128)})) conditional(s32[]{:T(128)} %bitcast.49, (bf16[2048,128]{1,0:T(8,128)(2,1)S(1)}, s32[8192]{0:T(1024)S(1)}, f32[512,16]{0,1:T(8,128)S(1)}, f32[512,16]{0,1:T(8,128)S(1)}, bf16[2048,128]{1,0:T(8,128)(2,1)S(1)}, /*index=5*/bf16[2048,128]{1,0:T(8,128)(2,1)S(1)}, ...), branch_computations={%region_0.4_spmd, %region_4.5_spmd} | conditional | flops 10720338944 | bytes 257407616 | solution.py:833
  45.3 0.0 copy-start.8
  45.3 0.0 copy-start.11
  45.3 0.0 copy-start.13
  45.4 4.9 %owner_sums.1 = bf16[32,24,128]{2,1,0:T(8,128)(2,1)S(1)} custom-call(bf16[32,80,256]{2,1,0:T(8,128)(2,1)S(1)} %get-tuple-element.42.recv_ref, bf16[256,320]{1,0:T(8,128)(2,1)} %get-tuple-element.43.into_ref, bf16[3,256,512]{2,1,0:T(8,128)(2,1)} %get-tuple-element.44.back_ref, bf16[256,128]{1,0:T(8,128)(2,1)} %get-tuple-element.45.table_ref, ...), custom_call_target="tpu_custom_call" | custom-call | tf_op jit(solution)/shard_map/cond/branch_1_fun/owner_sums/pallas_call | solution.py:692
  50.3 13.5 %all_to_all.68.recv_ref = bf16[32,24,128]{2,1,0:T(8,128)(2,1)S(1)} all-to-all(bf16[32,24,128]{2,1,0:T(8,128)(2,1)S(1)} %owner_sums.1), channel_id=1, replica_groups=mesh['ctx'=8,'ch'=4] {'ctx','ch'}, dimensions={0} | all-to-all | bytes 393216 | tf_op jit(solution)/shard_map/cond/branch_1_fun/all_to_all | solution.py:811
  63.8 0.0 copy-done.8
  63.8 3.6 %finish_rows.1 = (bf16[2048,128]{1,0:T(8,128)(2,1)}, f32[128,128]{1,0:T(8,128)}) custom-call(bf16[32,24,128]{2,1,0:T(8,128)(2,1)S(1)} %all_to_all.68.recv_ref, s32[8,2048]{1,0:T(8,128)S(1)} %copy-done.13, f32[2048,128]{1,0:T(8,128)S(1)} %copy-done.8, f32[256,128]{1,0:T(8,128)S(1)} %copy-done.11, bf16[2048,128]{1,0:T(8,128)(2,1)S(1)} %get-tuple-element.50.query_ref), custom_call_target="tpu_custom_call" | custom-call | tf_op jit(solution)/shard_map/cond/branch_1_fun/finish_rows/pallas_call | solution.py:794
  (4 shorter events, 0.0 us)
Async XLA Ops:
  0.6 13.5 %copy-start.9 = (f32[512,16]{0,1:T(8,128)S(1)}, f32[512,16]{0,1:T(8,128)}, u32[]{:S(2)}) copy-start(f32[512,16]{0,1:T(8,128)} %param.16) | copy-start | bytes 98308
  0.6 13.5 %copy-start.10 = (f32[512,16]{0,1:T(8,128)S(1)}, f32[512,16]{0,1:T(8,128)}, u32[]{:S(2)}) copy-start(f32[512,16]{0,1:T(8,128)} %param.17) | copy-start | bytes 98308
  0.7 13.5 %copy-start.14 = (s32[8192]{0:T(1024)S(1)}, s32[8192]{0:T(1024)}, u32[]{:S(2)}) copy-start(s32[8192]{0:T(1024)} %param.15) | copy-start | bytes 98308
  7.0 13.0 %copy-start.12 = (s32[8,2048]{1,0:T(8,128)}, s32[8,2048]{1,0:T(8,128)S(1)}, u32[]{:S(2)}) copy-start(s32[8,2048]{1,0:T(8,128)S(1)} %get-tuple-element.62.dest_ref) | copy-start | bytes 196612
  7.0 38.1 %all-to-all-start.7 = ((bf16[32,80,256]{2,1,0:T(8,128)(2,1)}), bf16[32,80,256]{2,1,0:T(8,128)(2,1)S(1)}, u32[]{:S(2)}, u32[]{:S(2)}) async-start(bf16[32,80,256]{2,1,0:T(8,128)(2,1)} %get-tuple-element.64), calls=%async_computation.7 | async-start | bytes 2621440 | tf_op jit(solution)/shard_map/all_to_all | solution.py:811
  14.2 7.0 %copy-start.5 = (bf16[2048,128]{1,0:T(8,128)(2,1)S(1)}, bf16[2048,128]{1,0:T(8,128)(2,1)}, u32[]{:S(2)}) copy-start(bf16[2048,128]{1,0:T(8,128)(2,1)} %key_ref.1) | copy-start | bytes 1572868
  14.2 7.0 %copy-start.6 = (bf16[2048,128]{1,0:T(8,128)(2,1)S(1)}, bf16[2048,128]{1,0:T(8,128)(2,1)}, u32[]{:S(2)}) copy-start(bf16[2048,128]{1,0:T(8,128)(2,1)} %value_ref.1) | copy-start | bytes 1572868
  21.1 23.9 %copy-start.3 = (bf16[2048,128]{1,0:T(8,128)(2,1)S(1)}, bf16[2048,128]{1,0:T(8,128)(2,1)}, u32[]{:S(2)}) copy-start(bf16[2048,128]{1,0:T(8,128)(2,1)} %query_hbm.1) | copy-start | bytes 1572868
  21.2 23.9 %copy-start.7 = (bf16[2048,128]{1,0:T(8,128)(2,1)S(1)}, bf16[2048,128]{1,0:T(8,128)(2,1)}, u32[]{:S(2)}) copy-start(bf16[2048,128]{1,0:T(8,128)(2,1)} %cot_hbm.1) | copy-start | bytes 1572868
  21.2 23.9 %copy-start.16 = (s32[128]{0:T(128)S(1)}, s32[128]{0:T(128)}, u32[]{:S(2)}) copy-start(s32[128]{0:T(128)} %place_hbm.1) | copy-start | bytes 1540
  45.3 18.5 %copy-start.8 = (f32[2048,128]{1,0:T(8,128)S(1)}, f32[2048,128]{1,0:T(8,128)}, u32[]{:S(2)}) copy-start(f32[2048,128]{1,0:T(8,128)} %get-tuple-element.48.conv_ref) | copy-start | bytes 3145732 | tf_op jit(solution)/shard_map/cond
  45.3 18.5 %copy-start.11 = (f32[256,128]{1,0:T(8,128)S(1)}, f32[256,128]{1,0:T(8,128)}, u32[]{:S(2)}) copy-start(f32[256,128]{1,0:T(8,128)} %get-tuple-element.49.decay_ref) | copy-start | bytes 393220 | tf_op jit(solution)/shard_map/cond
  45.3 18.5 %copy-start.13 = (s32[8,2048]{1,0:T(8,128)S(1)}, s32[8,2048]{1,0:T(8,128)}, u32[]{:S(2)}) copy-start(s32[8,2048]{1,0:T(8,128)} %get-tuple-element.47.dest_ref) | copy-start | bytes 196612 | tf_op jit(solution)/shard_map/cond

commit v4 on v3

--- a/solution.py
+++ b/solution.py
@@ -187,6 +187,12 @@
 
 def hot(flags):
     return jnp.where(flags, 1.0, 0.0).astype(BF16)
+
+
+def hot_at(rows, wanted):
+    row = iota((rows, wanted.shape[1]), 0).astype(F32).astype(BF16)
+    one = jnp.ones((), BF16)
+    return jnp.where(row == wanted.astype(F32).astype(BF16), one, jnp.zeros((), BF16))
 
 
 def dot(left, right):
@@ -325,13 +331,15 @@
     value_hbm,
     cot_hbm,
     query_hbm,
-    out_ref,
+    out_hbm,
     dest_ref,
     place_ref,
     group_ref,
     inputs,
     data,
+    outgoing,
     arrived,
+    left,
 ):
     moves = [(group_hbm, group_ref), (place_hbm, place_ref)]
     for at, source in enumerate((key_hbm, value_hbm, cot_hbm, query_hbm)):
@@ -366,20 +374,31 @@
     first = lax.shift_right_logical(place_ref[0], shift)
     second = lax.shift_right_logical(place_ref[sizes.run], shift)
     run_row = jnp.where(iota((1, 1, 2 * LANES), 2) < LANES, first, second).astype(F32)
-    part = 16
+    part = 8
     spare = iota((part, sizes.cap, 1), 1) == sizes.cap - 1
+    copies = []
     for start in range(0, sizes.peers, part):
         base = start * sizes.cap
         chosen = hot(iota((part * sizes.cap, sizes.channels), 0) == dest_ref[0:1, :] - base)
         rows = dot(chosen, data[...]).reshape(part, sizes.cap, 2 * LANES)
-        out_ref[start : start + part] = jnp.where(spare, run_row, rows).astype(BF16)
+        at = pl.ds(start, part)
+        outgoing[at] = jnp.where(spare, run_row, rows).astype(BF16)
+        copies.append(
+            pltpu.make_async_copy(outgoing.at[at], out_hbm.at[at], left.at[start // part])
+        )
+        copies[-1].start()
+    for copy in copies:
+        copy.wait()
 
 
 def pack(sizes, positions, groups, key_proj, value_proj, cotangent, query_proj):
     return pl.pallas_call(
         functools.partial(pack_kernel, sizes),
-        in_specs=[pl.BlockSpec(memory_space=pl.ANY)] * 6,
-        out_specs=[pl.BlockSpec(memory_space=pltpu.VMEM)] * 2,
+        in_specs=[pl.BlockSpec(memory_space=pltpu.HBM)] * 6,
+        out_specs=[
+            pl.BlockSpec(memory_space=pltpu.HBM),
+            pl.BlockSpec(memory_space=pltpu.VMEM),
+        ],
         out_shape=[
             jax.ShapeDtypeStruct((sizes.peers, sizes.cap, 2 * LANES), BF16),
             jax.ShapeDtypeStruct((8, sizes.channels), I32),
@@ -389,7 +408,9 @@
             pltpu.VMEM(groups.shape, I32),
             pltpu.VMEM((4, sizes.channels, sizes.tokens), BF16),
             pltpu.VMEM((sizes.channels, 2 * LANES), BF16),
+            pltpu.VMEM((sizes.peers, sizes.cap, 2 * LANES), BF16),
             pltpu.SemaphoreType.DMA((6,)),
+            pltpu.SemaphoreType.DMA((sizes.peers // 8,)),
         ],
         compiler_params=pltpu.CompilerParams(vmem_limit_bytes=VMEM_LIMIT),
         name="pack_rows",
@@ -433,18 +454,9 @@
         row = jnp.where(mine, where * sizes.size + nth, -1)
         column = jnp.where(mine & (slot < sizes.cap - 1), slot, -1)
         to_row = hot(iota((256, sizes.channels), 0) == row)
-        in_front = (column >= 0) & (column < sizes.rest)
-        columns = (
-            column,
-            jnp.where(in_front, column + sizes.cap, -1),
-            jnp.where(column >= sizes.rest, column + sizes.cap - sizes.rest, -1),
-        )
-        for at, wanted in enumerate(columns):
-            to_column = hot(iota((LANES, sizes.channels), 0) == wanted)
-            back_ref[at, :, source * LANES : (source + 1) * LANES] = dot_lanes(
-                to_row, to_column
-            ).astype(BF16)
-        found = back_ref[0, :, source * LANES : (source + 1) * LANES]
+        to_column = hot(iota((LANES, sizes.channels), 0) == column)
+        found = dot_lanes(to_row, to_column).astype(BF16)
+        back_ref[:, source * LANES : (source + 1) * LANES] = found
         shape = (LANES, sizes.ch * sizes.cap)
         moved = hot(
             (iota(shape, 1) == iota(shape, 0) + source * sizes.cap)
@@ -491,7 +503,7 @@
         + [pl.BlockSpec(memory_space=pltpu.VMEM)] * 3,
         out_shape=[
             jax.ShapeDtypeStruct((256, sizes.ch * sizes.cap), BF16),
-            jax.ShapeDtypeStruct((3, 256, sizes.ch * LANES), BF16),
+            jax.ShapeDtypeStruct((256, sizes.ch * LANES), BF16),
             jax.ShapeDtypeStruct((8, LANES), I32),
             jax.ShapeDtypeStruct((256, 2 * sizes.run), BF16),
             jax.ShapeDtypeStruct((modes, 256), F32),
@@ -603,12 +615,13 @@
     for source in range(sizes.ctx):
         block = recv_ref[source * sizes.ch : (source + 1) * sizes.ch]
         found = dot(into_ref[...], block.reshape(sizes.ch * sizes.cap, 2 * LANES))
+        found = found.astype(BF16)
         value = found[:, :LANES]
         turned = pltpu.roll(value, run, 1)
-        merged[source, 0] = jnp.where(lane < run, value, turned).astype(BF16)
-        merged[source, 1] = jnp.where(lane < run, turned, value).astype(BF16)
-        merged[source, 2] = found[:, LANES:].astype(BF16)
-        merged[source, 3] = pltpu.roll(found[:, LANES:], run, 1).astype(BF16)
+        merged[source, 0] = jnp.where(lane < run, value, turned)
+        merged[source, 1] = jnp.where(lane < run, turned, value)
+        merged[source, 2] = found[:, LANES:]
+        merged[source, 3] = pltpu.roll(found[:, LANES:], run, 1)
     for source in range(sizes.ctx):
         first, second = run_at[2 * source], run_at[2 * source + 1]
         gated[first] = merged[source, 0]
@@ -626,10 +639,10 @@
         states[at] = carried
         if at + 1 < runs:
             ends = dot_lanes(table_ref[...], gated[at])
-            total = jnp.zeros((modes, rows), F32)
-            for group in range(own):
+            total = ends[:modes]
+            for group in range(1, own):
                 piece = ends[group * modes : (group + 1) * modes]
-                total = total + jnp.where(group_lane == group, piece, 0.0)
+                total = jnp.where(group_lane == group, piece, total)
             carried = carried * leap + total
 
     seq = run * runs
@@ -658,9 +671,7 @@
         jnp.concatenate([states[run_at[2 * target]], states[run_at[2 * target + 1]]], axis=0)
         for target in range(sizes.ctx)
     ]
-    front = dot(jnp.concatenate(pairs, axis=0).astype(BF16), back_ref[0])
-    last = jnp.concatenate([pair[wide:] for pair in pairs], axis=0).astype(BF16)
-    second, third = dot(last, back_ref[1]), dot(last, back_ref[2])
+    front = dot(jnp.concatenate(pairs, axis=0).astype(BF16), back_ref[...])
     out_lane = iota((8, LANES), 1)
     for target in range(sizes.ctx):
         lags = sums[:, target * LANES : (target + 1) * LANES]
@@ -671,10 +682,11 @@
             mine = slice(chan * each, (chan + 1) * each)
             most, few = [jnp.concatenate([part[mine] for part in pair], axis=0) for pair in moved]
             head = front[target * 2 * modes : target * 2 * modes + wide, at]
-            tail = slice(target * 8, (target + 1) * 8)
+            last = front[target * 2 * modes + wide : (target + 1) * 2 * modes, at]
+            third = pltpu.roll(last, cap - rest, 1)
             beside = [
-                second[tail, at],
-                jnp.where(out_lane < LANES - few_lags, third[tail, at], few),
+                pltpu.roll(last, cap, 1),
+                jnp.where(out_lane < LANES - few_lags, third, few),
                 most,
             ]
             out_ref[target * sizes.ch + chan] = jnp.concatenate(
@@ -707,8 +719,21 @@
 
 
 def finish_kernel(
-    sizes, recv_ref, dest_ref, conv_ref, decay_ref, query_ref, out_ref, grad_ref, found, total
+    sizes,
+    recv_ref,
+    dest_ref,
+    conv_ref,
+    decay_ref,
+    query_hbm,
+    out_ref,
+    grad_ref,
+    found,
+    total,
+    query_ref,
+    arrived,
 ):
+    copy = pltpu.make_async_copy(query_hbm, query_ref, arrived)
+    copy.start()
     blocks = sizes.channels // LANES
     wide = recv_ref.shape[1]
     rows = wide + 8
@@ -725,11 +750,10 @@
         at = pl.ds(part * 256, 256)
         owner, slot = dest_ref[1:2, at], dest_ref[2:3, at]
         half, offset = lax.shift_right_logical(owner, 1), (owner & 1) * LANES
-        lane = iota((2 * LANES, 256), 0)
         in_second = jnp.where(slot < rest, slot + cap + offset, -1)
         in_third = jnp.where(slot >= rest, slot + cap - rest + offset, -1)
-        most = dot(front, hot(lane == slot + offset))
-        few = dot(second, hot(lane == in_second)) + dot(third, hot(lane == in_third))
+        most = dot(front, hot_at(2 * LANES, slot + offset))
+        few = dot(second, hot_at(2 * LANES, in_second)) + dot(third, hot_at(2 * LANES, in_third))
         mine = [jnp.zeros((wide, 256), F32), jnp.zeros((8, 256), F32)]
         for peer in range(halves):
             mine[0] = mine[0] + jnp.where(half == peer, most[peer * wide : (peer + 1) * wide], 0.0)
@@ -767,6 +791,8 @@
                 return states
 
             lax.fori_loop(0, sizes.run, step, states, unroll=True)
+        if first == 0:
+            copy.wait()
         for block in range(first, first + 8):
             turn(block)
 
@@ -793,7 +819,8 @@
     blocks = sizes.channels // LANES
     return pl.pallas_call(
         functools.partial(finish_kernel, sizes),
-        in_specs=[pl.BlockSpec(memory_space=pltpu.VMEM)] * 5,
+        in_specs=[pl.BlockSpec(memory_space=pltpu.VMEM)] * 4
+        + [pl.BlockSpec(memory_space=pltpu.HBM)],
         out_shape=[
             jax.ShapeDtypeStruct((sizes.channels, sizes.tokens), BF16),
             jax.ShapeDtypeStruct((sizes.block, LANES), F32),
@@ -801,6 +828,8 @@
         scratch_shapes=[
             pltpu.VMEM((blocks * (recv.shape[1] + 8), LANES), F32),
             pltpu.VMEM((sizes.tokens * blocks, LANES), F32),
+            pltpu.VMEM(query_proj.shape, BF16),
+            pltpu.SemaphoreType.DMA,
         ],
         compiler_params=pltpu.CompilerParams(vmem_limit_bytes=VMEM_LIMIT),
         name="finish_rows",
@@ -823,27 +852,18 @@
     conv, decay = local(sizes, me, groups, params, key_proj, value_proj)
     into, back, most, table, leap = index(sizes, me, groups, dest, params)
 
-    def fast(recv, into, back, table, leap, dest, conv, decay, *args):
-        returned = exchange(owner(sizes, recv, into, back, table, leap))
-        return tuple(finish(sizes, returned, dest, conv, decay, args[0]))
-
-    def slow(recv, into, back, table, leap, dest, conv, decay, *args):
-        return general_way(*args)
-
-    return lax.cond(
-        most[0, 0] <= sizes.cap - 1,
-        fast,
-        slow,
-        recv,
-        into,
-        back,
-        table,
-        leap,
-        dest,
-        conv,
-        decay,
-        *args,
-    )
+    into, conv, decay = lax.optimization_barrier((into, conv, decay))
+    returned = exchange(owner(sizes, recv, into, back, table, leap))
+    output, filter_grad = finish(sizes, returned, dest, conv, decay, query_proj)
+
+    def again(state):
+        return (jnp.zeros((), jnp.bool_), *general_way(*args))
+
+    over = most[0, 0] > sizes.cap - 1
+    _, output, filter_grad = lax.while_loop(
+        lambda state: state[0], again, (over, output, filter_grad)
+    )
+    return (output, filter_grad)
 
 
 def shards(*args):

time: 67.6 us -> 67.3 us (level)
  blocking collectives: 13.5 us -> 0 us
  waiting for transfers between devices: 17.2 us -> 28.7 us
  starting transfers between devices: 7.1 us -> 11.6 us
  Pallas kernels: 27.3 us -> 24 us
    all_to_all x1 -> x0, blocking collectives: 13.5 us -> none  [exchange(): lax.all_to_all(blocks, ('ctx', 'ch'), split_axis=0, concat_axis=0, tiled=...]
    all_to_all x1 -> x2, waiting for transfers between devices: 17.2 us -> 28.7 us  [exchange(): lax.all_to_all(blocks, ('ctx', 'ch'), split_axis=0, concat_axis=0, tiled=...]
    all_to_all x1 -> x2, starting transfers between devices: 7.1 us -> 11.6 us  [exchange(): lax.all_to_all(blocks, ('ctx', 'ch'), split_axis=0, concat_axis=0, tiled=...]
    pallas_call x1, Pallas kernels: 5.78 us -> 4.26 us  [index(): pl.pallas_call(functools.partial(index_kernel, sizes), in_specs=[pl.Block...]
    pallas_call x1, Pallas kernels: 6.72 us -> 5.69 us  [local(): pl.pallas_call(functools.partial(local_kernel, sizes), in_specs=[pl.Block...]
  transfers between devices with their start and end apart: 1 -> 2, of which waited for: 1 -> 2; matrix products, arithmetic and copies ran while one was open for 1% -> 1% of each run, Pallas kernels for 19% -> 15%
where the time goes in v4:
time: 67.3 us; the launch traced here: 67 us
  waiting for transfers between devices  28.7 us (43%)
  Pallas kernels  24 us (36%)
  starting transfers between devices  11.6 us (17%)
  between operations  1.65 us (2%)
  local copies, waits for them, and re-layouts  0.8 us (1%)
    all_to_all x2, waiting for transfers between devices, exchange(): lax.all_to_all(blocks, ('ctx', 'ch'), split_axis=0, concat_axis=0, tiled=...  28.7 us
    all_to_all x2, starting transfers between devices, exchange(): lax.all_to_all(blocks, ('ctx', 'ch'), split_axis=0, concat_axis=0, tiled=...  11.6 us
    pallas_call x1, Pallas kernels, pack(): pl.pallas_call(functools.partial(pack_kernel, sizes), in_specs=[pl.BlockS...  6.18 us
    pallas_call x1, Pallas kernels, local(): pl.pallas_call(functools.partial(local_kernel, sizes), in_specs=[pl.Block...  5.69 us
    pallas_call x1, Pallas kernels, owner(): pl.pallas_call(functools.partial(owner_kernel, sizes), in_specs=[pl.Block...  4.34 us
    pallas_call x1, Pallas kernels, index(): pl.pallas_call(functools.partial(index_kernel, sizes), in_specs=[pl.Block...  4.26 us
    pallas_call x1, Pallas kernels, finish(): pl.pallas_call(functools.partial(finish_kernel, sizes), in_specs=[pl.Bloc...  3.49 us
  transfers between devices with their start and end apart: 2, of which 2 were waited for; matrix products, arithmetic and copies ran while one was open for 1% of the time, Pallas kernels for 15%

profile of v4, /device:TPU:1, one launch (start us, length us, event | category | flops | bytes accessed | tf_op | source)
XLA Modules:
  0.0 67.0 jit_solution(3609556878971871822)
XLA Ops:
  0.6 0.0 copy-start.11
  0.6 0.0 copy-start.13
  0.7 0.0 copy-start.12
  0.7 6.2 %pack_rows.1 = (bf16[32,80,256]{2,1,0:T(8,128)(2,1)}, s32[8,2048]{1,0:T(8,128)S(1)}) custom-call(s32[128]{0:T(128)} %place_hbm.1, s32[1,8192]{1,0:T(1,128)} %bitcast.173, bf16[2048,128]{1,0:T(8,128)(2,1)} %key_ref.1, bf16[2048,128]{1,0:T(8,128)(2,1)} %value_ref.1, bf16[2048,128]{1,0:T(8,128)(2,1)} %cot_hbm.1, bf16[2048,128]{1,0:T(8,128)(2,1)} %query_hbm.3), custom_call_target="tpu_custom_call" | custom-call | tf_op jit(solution)/shard_map/pack_rows/pallas_call | solution.py:395
  6.9 7.1 %all-to-all-start.6 = ((bf16[32,80,256]{2,1,0:T(8,128)(2,1)}), bf16[32,80,256]{2,1,0:T(8,128)(2,1)S(1)}, u32[]{:S(2)}, u32[]{:S(2)}) async-start(bf16[32,80,256]{2,1,0:T(8,128)(2,1)} %get-tuple-element.73), calls=%async_computation.6 | async-start | bytes 2621440 | tf_op jit(solution)/shard_map/all_to_all | solution.py:840
  14.0 0.0 copy-done.11
  14.0 0.0 copy-done.13
  14.0 0.0 copy-done.12
  14.0 0.0 copy-start.7
  14.0 0.0 copy-start.9
  14.1 4.3 %index_rows.1 = (bf16[256,320]{1,0:T(8,128)(2,1)S(1)}, bf16[256,512]{1,0:T(8,128)(2,1)S(1)}, s32[8,128]{1,0:T(8,128)S(1)}, bf16[256,128]{1,0:T(8,128)(2,1)S(1)}, f32[16,256]{1,0:T(8,128)S(1)}) custom-call(s32[1]{0:T(128)} %bitcast.46.me_ref, s32[1,8192]{1,0:T(1,128)S(1)} %bitcast.174, s32[8,2048]{1,0:T(8,128)S(1)} %get-tuple-element.71.dest_ref, ...), custom_call_target="tpu_custom_call" | custom-call | flops 2000000000 | bytes 1000000 | tf_op jit(solution)/shard_map/index_rows/pallas_call | solution.py:500
  18.3 0.0 copy-done.7
  18.3 0.0 copy-done.9
  18.3 5.7 %local_runs.1 = (f32[2048,128]{1,0:T(8,128)S(1)}, f32[256,128]{1,0:T(8,128)S(1)}) custom-call(s32[1]{0:T(128)} %bitcast.46.me_ref, s32[1,8192]{1,0:T(1,128)S(1)} %bitcast.175, f32[32,512]{1,0:T(8,128)S(1)} %maximum_bitcast_fusion.param_ref, bf16[2048,128]{1,0:T(8,128)(2,1)S(1)} %copy-done.7, bf16[2048,128]{1,0:T(8,128)(2,1)S(1)} %copy-done.9), custom_call_target="tpu_custom_call" | custom-call | flops 4000000000 | bytes 3000000 | tf_op jit(solution)/shard_map/local_runs/pallas_call | solution.py:574
  24.0 20.9 %all-to-all-done.6.recv_ref = bf16[32,80,256]{2,1,0:T(8,128)(2,1)S(1)} async-done(((bf16[32,80,256]{2,1,0:T(8,128)(2,1)}), bf16[32,80,256]{2,1,0:T(8,128)(2,1)S(1)}, u32[]{:S(2)}, u32[]{:S(2)}) %all-to-all-start.6) | async-done | bytes 1310752 | tf_op jit(solution)/shard_map/all_to_all | solution.py:840
  45.0 0.0 copy-start.14
  45.0 4.3 %owner_sums.1 = bf16[32,24,128]{2,1,0:T(8,128)(2,1)} custom-call(bf16[32,80,256]{2,1,0:T(8,128)(2,1)S(1)} %all-to-all-done.6.recv_ref, bf16[256,320]{1,0:T(8,128)(2,1)S(1)} %get-tuple-element.77.into_ref, bf16[256,512]{1,0:T(8,128)(2,1)S(1)} %get-tuple-element.78.back_ref, bf16[256,128]{1,0:T(8,128)(2,1)S(1)} %get-tuple-element.79.table_ref, ...), custom_call_target="tpu_custom_call" | custom-call | tf_op jit(solution)/shard_map/owner_sums/pallas_call | solution.py:704
  49.3 4.5 %all-to-all-start.7 = ((bf16[32,24,128]{2,1,0:T(8,128)(2,1)}), bf16[32,24,128]{2,1,0:T(8,128)(2,1)S(1)}, u32[]{:S(2)}, u32[]{:S(2)}) async-start(bf16[32,24,128]{2,1,0:T(8,128)(2,1)} %owner_sums.1), calls=%async_computation.7 | async-start | bytes 393216 | tf_op jit(solution)/shard_map/all_to_all | solution.py:840
  53.8 0.1 copy.244
  53.9 0.1 copy.245
  54.1 0.5 slice.39
  55.2 7.8 %all-to-all-done.7.recv_ref = bf16[32,24,128]{2,1,0:T(8,128)(2,1)S(1)} async-done(((bf16[32,24,128]{2,1,0:T(8,128)(2,1)}), bf16[32,24,128]{2,1,0:T(8,128)(2,1)S(1)}, u32[]{:S(2)}, u32[]{:S(2)}) %all-to-all-start.7) | async-done | bytes 196640 | tf_op jit(solution)/shard_map/all_to_all | solution.py:840
  63.0 3.5 %finish_rows.1 = (bf16[2048,128]{1,0:T(8,128)(2,1)}, f32[128,128]{1,0:T(8,128)}) custom-call(bf16[32,24,128]{2,1,0:T(8,128)(2,1)S(1)} %all-to-all-done.7.recv_ref, s32[8,2048]{1,0:T(8,128)S(1)} %get-tuple-element.71.dest_ref, f32[2048,128]{1,0:T(8,128)S(1)} %get-tuple-element.81.conv_ref, f32[256,128]{1,0:T(8,128)S(1)} %get-tuple-element.82.decay_ref, ...), custom_call_target="tpu_custom_call" | custom-call | tf_op jit(solution)/shard_map/finish_rows/pallas_call | solution.py:820
  66.5 0.0 copy-done.14
  66.5 0.3 while.11
  (2 shorter events, 0.0 us)
Async XLA Ops:
  0.6 13.3 %copy-start.11 = (f32[512,16]{0,1:T(8,128)S(1)}, f32[512,16]{0,1:T(8,128)}, u32[]{:S(2)}) copy-start(f32[512,16]{0,1:T(8,128)} %param.16) | copy-start | bytes 98308
  0.6 13.3 %copy-start.13 = (f32[512,16]{0,1:T(8,128)S(1)}, f32[512,16]{0,1:T(8,128)}, u32[]{:S(2)}) copy-start(f32[512,16]{0,1:T(8,128)} %param.17) | copy-start | bytes 98308
  0.7 13.4 %copy-start.12 = (s32[8192]{0:T(1024)S(1)}, s32[8192]{0:T(1024)}, u32[]{:S(2)}) copy-start(s32[8192]{0:T(1024)} %param.15) | copy-start | bytes 98308
  6.9 38.1 %all-to-all-start.6 = ((bf16[32,80,256]{2,1,0:T(8,128)(2,1)}), bf16[32,80,256]{2,1,0:T(8,128)(2,1)S(1)}, u32[]{:S(2)}, u32[]{:S(2)}) async-start(bf16[32,80,256]{2,1,0:T(8,128)(2,1)} %get-tuple-element.73), calls=%async_computation.6 | async-start | bytes 2621440 | tf_op jit(solution)/shard_map/all_to_all | solution.py:840
  14.0 4.3 %copy-start.7 = (bf16[2048,128]{1,0:T(8,128)(2,1)S(1)}, bf16[2048,128]{1,0:T(8,128)(2,1)}, u32[]{:S(2)}) copy-start(bf16[2048,128]{1,0:T(8,128)(2,1)} %key_ref.1) | copy-start | bytes 1572868
  14.0 4.3 %copy-start.9 = (bf16[2048,128]{1,0:T(8,128)(2,1)S(1)}, bf16[2048,128]{1,0:T(8,128)(2,1)}, u32[]{:S(2)}) copy-start(bf16[2048,128]{1,0:T(8,128)(2,1)} %value_ref.1) | copy-start | bytes 1572868
  45.0 21.6 %copy-start.14 = (s32[128]{0:T(128)S(1)}, s32[128]{0:T(128)}, u32[]{:S(2)}) copy-start(s32[128]{0:T(128)} %place_hbm.1) | copy-start | bytes 1540
  49.3 13.7 %all-to-all-start.7 = ((bf16[32,24,128]{2,1,0:T(8,128)(2,1)}), bf16[32,24,128]{2,1,0:T(8,128)(2,1)S(1)}, u32[]{:S(2)}, u32[]{:S(2)}) async-start(bf16[32,24,128]{2,1,0:T(8,128)(2,1)} %owner_sums.1), calls=%async_computation.7 | async-start | bytes 393216 | tf_op jit(solution)/shard_map/all_to_all | solution.py:840

commit v5 on v3

--- a/solution.py
+++ b/solution.py
@@ -187,6 +187,12 @@
 
 def hot(flags):
     return jnp.where(flags, 1.0, 0.0).astype(BF16)
+
+
+def hot_at(rows, wanted):
+    row = iota((rows, wanted.shape[1]), 0).astype(F32).astype(BF16)
+    one = jnp.ones((), BF16)
+    return jnp.where(row == wanted.astype(F32).astype(BF16), one, jnp.zeros((), BF16))
 
 
 def dot(left, right):
@@ -433,18 +439,9 @@
         row = jnp.where(mine, where * sizes.size + nth, -1)
         column = jnp.where(mine & (slot < sizes.cap - 1), slot, -1)
         to_row = hot(iota((256, sizes.channels), 0) == row)
-        in_front = (column >= 0) & (column < sizes.rest)
-        columns = (
-            column,
-            jnp.where(in_front, column + sizes.cap, -1),
-            jnp.where(column >= sizes.rest, column + sizes.cap - sizes.rest, -1),
-        )
-        for at, wanted in enumerate(columns):
-            to_column = hot(iota((LANES, sizes.channels), 0) == wanted)
-            back_ref[at, :, source * LANES : (source + 1) * LANES] = dot_lanes(
-                to_row, to_column
-            ).astype(BF16)
-        found = back_ref[0, :, source * LANES : (source + 1) * LANES]
+        to_column = hot(iota((LANES, sizes.channels), 0) == column)
+        found = dot_lanes(to_row, to_column).astype(BF16)
+        back_ref[:, source * LANES : (source + 1) * LANES] = found
         shape = (LANES, sizes.ch * sizes.cap)
         moved = hot(
             (iota(shape, 1) == iota(shape, 0) + source * sizes.cap)
@@ -491,7 +488,7 @@
         + [pl.BlockSpec(memory_space=pltpu.VMEM)] * 3,
         out_shape=[
             jax.ShapeDtypeStruct((256, sizes.ch * sizes.cap), BF16),
-            jax.ShapeDtypeStruct((3, 256, sizes.ch * LANES), BF16),
+            jax.ShapeDtypeStruct((256, sizes.ch * LANES), BF16),
             jax.ShapeDtypeStruct((8, LANES), I32),
             jax.ShapeDtypeStruct((256, 2 * sizes.run), BF16),
             jax.ShapeDtypeStruct((modes, 256), F32),
@@ -568,8 +565,8 @@
             jax.ShapeDtypeStruct((modes * blocks, LANES), F32),
         ],
         scratch_shapes=[
-            pltpu.VMEM((blocks * 2 * modes, LANES), F32),
-            pltpu.VMEM((sizes.tokens * blocks, LANES), F32),
+            pltpu.VMEM(((blocks + 1) * 2 * modes, LANES), F32),
+            pltpu.VMEM(((sizes.tokens + 1) * blocks, LANES), F32),
         ],
         compiler_params=pltpu.CompilerParams(vmem_limit_bytes=VMEM_LIMIT),
         cost_estimate=pl.CostEstimate(flops=4 * 10**9, bytes_accessed=3 * 10**6, transcendentals=0),
@@ -603,12 +600,13 @@
     for source in range(sizes.ctx):
         block = recv_ref[source * sizes.ch : (source + 1) * sizes.ch]
         found = dot(into_ref[...], block.reshape(sizes.ch * sizes.cap, 2 * LANES))
+        found = found.astype(BF16)
         value = found[:, :LANES]
         turned = pltpu.roll(value, run, 1)
-        merged[source, 0] = jnp.where(lane < run, value, turned).astype(BF16)
-        merged[source, 1] = jnp.where(lane < run, turned, value).astype(BF16)
-        merged[source, 2] = found[:, LANES:].astype(BF16)
-        merged[source, 3] = pltpu.roll(found[:, LANES:], run, 1).astype(BF16)
+        merged[source, 0] = jnp.where(lane < run, value, turned)
+        merged[source, 1] = jnp.where(lane < run, turned, value)
+        merged[source, 2] = found[:, LANES:]
+        merged[source, 3] = pltpu.roll(found[:, LANES:], run, 1)
     for source in range(sizes.ctx):
         first, second = run_at[2 * source], run_at[2 * source + 1]
         gated[first] = merged[source, 0]
@@ -626,10 +624,10 @@
         states[at] = carried
         if at + 1 < runs:
             ends = dot_lanes(table_ref[...], gated[at])
-            total = jnp.zeros((modes, rows), F32)
-            for group in range(own):
+            total = ends[:modes]
+            for group in range(1, own):
                 piece = ends[group * modes : (group + 1) * modes]
-                total = total + jnp.where(group_lane == group, piece, 0.0)
+                total = jnp.where(group_lane == group, piece, total)
             carried = carried * leap + total
 
     seq = run * runs
@@ -658,9 +656,7 @@
         jnp.concatenate([states[run_at[2 * target]], states[run_at[2 * target + 1]]], axis=0)
         for target in range(sizes.ctx)
     ]
-    front = dot(jnp.concatenate(pairs, axis=0).astype(BF16), back_ref[0])
-    last = jnp.concatenate([pair[wide:] for pair in pairs], axis=0).astype(BF16)
-    second, third = dot(last, back_ref[1]), dot(last, back_ref[2])
+    front = dot(jnp.concatenate(pairs, axis=0).astype(BF16), back_ref[...])
     out_lane = iota((8, LANES), 1)
     for target in range(sizes.ctx):
         lags = sums[:, target * LANES : (target + 1) * LANES]
@@ -671,10 +667,11 @@
             mine = slice(chan * each, (chan + 1) * each)
             most, few = [jnp.concatenate([part[mine] for part in pair], axis=0) for pair in moved]
             head = front[target * 2 * modes : target * 2 * modes + wide, at]
-            tail = slice(target * 8, (target + 1) * 8)
+            last = front[target * 2 * modes + wide : (target + 1) * 2 * modes, at]
+            third = pltpu.roll(last, cap - rest, 1)
             beside = [
-                second[tail, at],
-                jnp.where(out_lane < LANES - few_lags, third[tail, at], few),
+                pltpu.roll(last, cap, 1),
+                jnp.where(out_lane < LANES - few_lags, third, few),
                 most,
             ]
             out_ref[target * sizes.ch + chan] = jnp.concatenate(
@@ -725,11 +722,10 @@
         at = pl.ds(part * 256, 256)
         owner, slot = dest_ref[1:2, at], dest_ref[2:3, at]
         half, offset = lax.shift_right_logical(owner, 1), (owner & 1) * LANES
-        lane = iota((2 * LANES, 256), 0)
         in_second = jnp.where(slot < rest, slot + cap + offset, -1)
         in_third = jnp.where(slot >= rest, slot + cap - rest + offset, -1)
-        most = dot(front, hot(lane == slot + offset))
-        few = dot(second, hot(lane == in_second)) + dot(third, hot(lane == in_third))
+        most = dot(front, hot_at(2 * LANES, slot + offset))
+        few = dot(second, hot_at(2 * LANES, in_second)) + dot(third, hot_at(2 * LANES, in_third))
         mine = [jnp.zeros((wide, 256), F32), jnp.zeros((8, 256), F32)]
         for peer in range(halves):
             mine[0] = mine[0] + jnp.where(half == peer, most[peer * wide : (peer + 1) * wide], 0.0)
@@ -799,8 +795,8 @@
             jax.ShapeDtypeStruct((sizes.block, LANES), F32),
         ],
         scratch_shapes=[
-            pltpu.VMEM((blocks * (recv.shape[1] + 8), LANES), F32),
-            pltpu.VMEM((sizes.tokens * blocks, LANES), F32),
+            pltpu.VMEM(((blocks + 1) * (recv.shape[1] + 8), LANES), F32),
+            pltpu.VMEM(((sizes.tokens + 1) * blocks, LANES), F32),
         ],
         compiler_params=pltpu.CompilerParams(vmem_limit_bytes=VMEM_LIMIT),
         name="finish_rows",

time: 67.6 us -> 67.3 us (level)
  Pallas kernels: 27.3 us -> 26.1 us
  waiting for transfers between devices: 17.2 us -> 18.1 us
    all_to_all x1, waiting for transfers between devices: 17.2 us -> 18.1 us  [exchange(): lax.all_to_all(blocks, ('ctx', 'ch'), split_axis=0, concat_axis=0, tiled=...]
    pallas_call x1, Pallas kernels: 5.78 us -> 4.88 us  [index(): pl.pallas_call(functools.partial(index_kernel, sizes), in_specs=[pl.Block...]
  transfers between devices with their start and end apart: 1 -> 1, of which waited for: 1 -> 1; matrix products, arithmetic and copies ran while one was open for 1% -> 1% of each run, Pallas kernels for 19% -> 17%
where the time goes in v5:
time: 67.3 us; the launch traced here: 67.1 us
  Pallas kernels  26.1 us (39%)
  waiting for transfers between devices  18.1 us (27%)
  blocking collectives  13.5 us (20%)
  starting transfers between devices  7.1 us (11%)
  between operations  1.44 us (2%)
    all_to_all x1, waiting for transfers between devices, exchange(): lax.all_to_all(blocks, ('ctx', 'ch'), split_axis=0, concat_axis=0, tiled=...  18.1 us
    all_to_all x1, blocking collectives, exchange(): lax.all_to_all(blocks, ('ctx', 'ch'), split_axis=0, concat_axis=0, tiled=...  13.5 us
    all_to_all x1, starting transfers between devices, exchange(): lax.all_to_all(blocks, ('ctx', 'ch'), split_axis=0, concat_axis=0, tiled=...  7.1 us
    pallas_call x1, Pallas kernels, local(): pl.pallas_call(functools.partial(local_kernel, sizes), in_specs=[pl.Block...  6.72 us
    pallas_call x1, Pallas kernels, pack(): pl.pallas_call(functools.partial(pack_kernel, sizes), in_specs=[pl.BlockS...  6.3 us
    pallas_call x1, Pallas kernels, index(): pl.pallas_call(functools.partial(index_kernel, sizes), in_specs=[pl.Block...  4.88 us
    pallas_call x1, Pallas kernels, owner(): pl.pallas_call(functools.partial(owner_kernel, sizes), in_specs=[pl.Block...  4.78 us
    pallas_call x1, Pallas kernels, finish(): pl.pallas_call(functools.partial(finish_kernel, sizes), in_specs=[pl.Bloc...  3.38 us
  transfers between devices with their start and end apart: 1, of which 1 were waited for; matrix products, arithmetic and copies ran while one was open for 1% of the time, Pallas kernels for 17%

profile of v5, /device:TPU:1, one launch (start us, length us, event | category | flops | bytes accessed | tf_op | source)
XLA Modules:
  0.0 67.1 jit_solution(93401832769459002)
XLA Ops:
  0.6 0.0 copy-start.9
  0.6 0.0 copy-start.10
  0.7 0.0 copy-start.14
  0.7 6.3 %pack_rows.1 = (bf16[32,80,256]{2,1,0:T(8,128)(2,1)}, s32[8,2048]{1,0:T(8,128)S(1)}) custom-call(s32[128]{0:T(128)} %place_hbm.1, s32[1,8192]{1,0:T(1,128)} %bitcast.172, bf16[2048,128]{1,0:T(8,128)(2,1)} %key_ref.1, bf16[2048,128]{1,0:T(8,128)(2,1)} %value_ref.1, bf16[2048,128]{1,0:T(8,128)(2,1)} %cot_hbm.1, bf16[2048,128]{1,0:T(8,128)(2,1)} %query_hbm.1), custom_call_target="tpu_custom_call" | custom-call | tf_op jit(solution)/shard_map/pack_rows/pallas_call | solution.py:385
  7.0 0.0 copy-start.12
  7.0 7.1 %all-to-all-start.7 = ((bf16[32,80,256]{2,1,0:T(8,128)(2,1)}), bf16[32,80,256]{2,1,0:T(8,128)(2,1)S(1)}, u32[]{:S(2)}, u32[]{:S(2)}) async-start(bf16[32,80,256]{2,1,0:T(8,128)(2,1)} %get-tuple-element.64), calls=%async_computation.7 | async-start | bytes 2621440 | tf_op jit(solution)/shard_map/all_to_all | solution.py:807
  14.1 0.0 copy-done.9
  14.1 0.0 copy-done.10
  14.1 0.0 copy-done.14
  14.2 0.0 copy-start.5
  14.2 0.0 copy-start.6
  14.2 4.9 %index_rows.1 = (bf16[256,320]{1,0:T(8,128)(2,1)}, bf16[256,512]{1,0:T(8,128)(2,1)}, s32[8,128]{1,0:T(8,128)S(1)}, bf16[256,128]{1,0:T(8,128)(2,1)}, f32[16,256]{1,0:T(8,128)S(1)}) custom-call(s32[1]{0:T(128)} %bitcast.46.me_ref, s32[1,8192]{1,0:T(1,128)S(1)} %bitcast.173, s32[8,2048]{1,0:T(8,128)S(1)} %get-tuple-element.62.dest_ref, ...), custom_call_target="tpu_custom_call" | custom-call | flops 2000000000 | bytes 1000000 | tf_op jit(solution)/shard_map/index_rows/pallas_call | solution.py:485
  19.1 0.0 copy-done.12
  19.1 0.5 slice.39
  20.2 0.0 copy-done.5
  20.2 0.0 copy-done.6
  20.3 0.0 copy-start.3
  20.3 0.0 copy-start.7
  20.3 0.0 copy-start.16
  20.3 6.7 %local_runs.1 = (f32[2048,128]{1,0:T(8,128)}, f32[256,128]{1,0:T(8,128)}) custom-call(s32[1]{0:T(128)} %bitcast.46.me_ref, s32[1,8192]{1,0:T(1,128)S(1)} %bitcast.174, f32[32,512]{1,0:T(8,128)S(1)} %maximum_bitcast_fusion.param_ref, bf16[2048,128]{1,0:T(8,128)(2,1)S(1)} %copy-done.5, bf16[2048,128]{1,0:T(8,128)(2,1)S(1)} %copy-done.6), custom_call_target="tpu_custom_call" | custom-call | flops 4000000000 | bytes 3000000 | tf_op jit(solution)/shard_map/local_runs/pallas_call | solution.py:559
  27.0 18.1 %all-to-all-done.7 = bf16[32,80,256]{2,1,0:T(8,128)(2,1)S(1)} async-done(((bf16[32,80,256]{2,1,0:T(8,128)(2,1)}), bf16[32,80,256]{2,1,0:T(8,128)(2,1)S(1)}, u32[]{:S(2)}, u32[]{:S(2)}) %all-to-all-start.7) | async-done | bytes 1310752 | tf_op jit(solution)/shard_map/all_to_all | solution.py:807
  45.1 0.0 copy-done.3
  45.1 0.0 copy-done.7
  45.1 0.0 copy-done.16
  45.1 22.0 %conditional.1 = ((bf16[2048,128]{1,0:T(8,128)(2,1)}, f32[128,128]{1,0:T(8,128)})) conditional(s32[]{:T(128)} %bitcast.49, (bf16[2048,128]{1,0:T(8,128)(2,1)S(1)}, s32[8192]{0:T(1024)S(1)}, f32[512,16]{0,1:T(8,128)S(1)}, f32[512,16]{0,1:T(8,128)S(1)}, bf16[2048,128]{1,0:T(8,128)(2,1)S(1)}, /*index=5*/bf16[2048,128]{1,0:T(8,128)(2,1)S(1)}, ...), branch_computations={%region_0.4_spmd, %region_4.5_spmd} | conditional | flops 10720338944 | bytes 257407616 | solution.py:829
  45.3 0.0 copy-start.8
  45.3 0.0 copy-start.11
  45.3 0.0 copy-start.13
  45.4 4.8 %owner_sums.1 = bf16[32,24,128]{2,1,0:T(8,128)(2,1)S(1)} custom-call(bf16[32,80,256]{2,1,0:T(8,128)(2,1)S(1)} %get-tuple-element.42.recv_ref, bf16[256,320]{1,0:T(8,128)(2,1)} %get-tuple-element.43.into_ref, bf16[256,512]{1,0:T(8,128)(2,1)} %get-tuple-element.44.back_ref, bf16[256,128]{1,0:T(8,128)(2,1)} %get-tuple-element.45.table_ref, ...), custom_call_target="tpu_custom_call" | custom-call | tf_op jit(solution)/shard_map/cond/branch_1_fun/owner_sums/pallas_call | solution.py:689
  50.1 13.5 %all_to_all.68.recv_ref = bf16[32,24,128]{2,1,0:T(8,128)(2,1)S(1)} all-to-all(bf16[32,24,128]{2,1,0:T(8,128)(2,1)S(1)} %owner_sums.1), channel_id=1, replica_groups=mesh['ctx'=8,'ch'=4] {'ctx','ch'}, dimensions={0} | all-to-all | bytes 393216 | tf_op jit(solution)/shard_map/cond/branch_1_fun/all_to_all | solution.py:807
  63.7 0.0 copy-done.11
  63.7 3.4 %finish_rows.1 = (bf16[2048,128]{1,0:T(8,128)(2,1)}, f32[128,128]{1,0:T(8,128)}) custom-call(bf16[32,24,128]{2,1,0:T(8,128)(2,1)S(1)} %all_to_all.68.recv_ref, s32[8,2048]{1,0:T(8,128)S(1)} %copy-done.13, f32[2048,128]{1,0:T(8,128)S(1)} %copy-done.8, f32[256,128]{1,0:T(8,128)S(1)} %copy-done.11, bf16[2048,128]{1,0:T(8,128)(2,1)S(1)} %get-tuple-element.50.query_ref), custom_call_target="tpu_custom_call" | custom-call | tf_op jit(solution)/shard_map/cond/branch_1_fun/finish_rows/pallas_call | solution.py:790
  (4 shorter events, 0.0 us)
Async XLA Ops:
  0.6 13.5 %copy-start.9 = (f32[512,16]{0,1:T(8,128)S(1)}, f32[512,16]{0,1:T(8,128)}, u32[]{:S(2)}) copy-start(f32[512,16]{0,1:T(8,128)} %param.16) | copy-start | bytes 98308
  0.6 13.5 %copy-start.10 = (f32[512,16]{0,1:T(8,128)S(1)}, f32[512,16]{0,1:T(8,128)}, u32[]{:S(2)}) copy-start(f32[512,16]{0,1:T(8,128)} %param.17) | copy-start | bytes 98308
  0.7 13.5 %copy-start.14 = (s32[8192]{0:T(1024)S(1)}, s32[8192]{0:T(1024)}, u32[]{:S(2)}) copy-start(s32[8192]{0:T(1024)} %param.15) | copy-start | bytes 98308
  7.0 12.1 %copy-start.12 = (s32[8,2048]{1,0:T(8,128)}, s32[8,2048]{1,0:T(8,128)S(1)}, u32[]{:S(2)}) copy-start(s32[8,2048]{1,0:T(8,128)S(1)} %get-tuple-element.62.dest_ref) | copy-start | bytes 196612
  7.0 38.1 %all-to-all-start.7 = ((bf16[32,80,256]{2,1,0:T(8,128)(2,1)}), bf16[32,80,256]{2,1,0:T(8,128)(2,1)S(1)}, u32[]{:S(2)}, u32[]{:S(2)}) async-start(bf16[32,80,256]{2,1,0:T(8,128)(2,1)} %get-tuple-element.64), calls=%async_computation.7 | async-start | bytes 2621440 | tf_op jit(solution)/shard_map/all_to_all | solution.py:807
  14.2 6.1 %copy-start.5 = (bf16[2048,128]{1,0:T(8,128)(2,1)S(1)}, bf16[2048,128]{1,0:T(8,128)(2,1)}, u32[]{:S(2)}) copy-start(bf16[2048,128]{1,0:T(8,128)(2,1)} %key_ref.1) | copy-start | bytes 1572868
  14.2 6.1 %copy-start.6 = (bf16[2048,128]{1,0:T(8,128)(2,1)S(1)}, bf16[2048,128]{1,0:T(8,128)(2,1)}, u32[]{:S(2)}) copy-start(bf16[2048,128]{1,0:T(8,128)(2,1)} %value_ref.1) | copy-start | bytes 1572868
  20.3 24.8 %copy-start.3 = (bf16[2048,128]{1,0:T(8,128)(2,1)S(1)}, bf16[2048,128]{1,0:T(8,128)(2,1)}, u32[]{:S(2)}) copy-start(bf16[2048,128]{1,0:T(8,128)(2,1)} %query_hbm.1) | copy-start | bytes 1572868
  20.3 24.8 %copy-start.7 = (bf16[2048,128]{1,0:T(8,128)(2,1)S(1)}, bf16[2048,128]{1,0:T(8,128)(2,1)}, u32[]{:S(2)}) copy-start(bf16[2048,128]{1,0:T(8,128)(2,1)} %cot_hbm.1) | copy-start | bytes 1572868
  20.3 24.8 %copy-start.16 = (s32[128]{0:T(128)S(1)}, s32[128]{0:T(128)}, u32[]{:S(2)}) copy-start(s32[128]{0:T(128)} %place_hbm.1) | copy-start | bytes 1540
  45.3 18.3 %copy-start.8 = (f32[2048,128]{1,0:T(8,128)S(1)}, f32[2048,128]{1,0:T(8,128)}, u32[]{:S(2)}) copy-start(f32[2048,128]{1,0:T(8,128)} %get-tuple-element.48.conv_ref) | copy-start | bytes 3145732 | tf_op jit(solution)/shard_map/cond
  45.3 18.3 %copy-start.11 = (f32[256,128]{1,0:T(8,128)S(1)}, f32[256,128]{1,0:T(8,128)}, u32[]{:S(2)}) copy-start(f32[256,128]{1,0:T(8,128)} %get-tuple-element.49.decay_ref) | copy-start | bytes 393220 | tf_op jit(solution)/shard_map/cond
  45.3 18.3 %copy-start.13 = (s32[8,2048]{1,0:T(8,128)S(1)}, s32[8,2048]{1,0:T(8,128)}, u32[]{:S(2)}) copy-start(s32[8,2048]{1,0:T(8,128)} %get-tuple-element.47.dest_ref) | copy-start | bytes 196612 | tf_op jit(solution)/shard_map/cond

commit v6 on v5

--- a/solution.py
+++ b/solution.py
@@ -408,7 +408,6 @@
     group_ref,
     dest_ref,
     param_ref,
-    into_ref,
     back_ref,
     over_ref,
     table_ref,
@@ -427,7 +426,6 @@
     over_ref[...] = jnp.broadcast_to(jnp.max(most, axis=0, keepdims=True), (8, LANES)).astype(I32)
 
     earlier = jnp.zeros((sizes.own, 1), F32)
-    into = jnp.zeros((256, sizes.ch * sizes.cap), F32)
     for source in range(sizes.ch):
         mine = owner[source] == me
         where = jnp.where(mine, place[source], -1)
@@ -440,15 +438,8 @@
         column = jnp.where(mine & (slot < sizes.cap - 1), slot, -1)
         to_row = hot(iota((256, sizes.channels), 0) == row)
         to_column = hot(iota((LANES, sizes.channels), 0) == column)
-        found = dot_lanes(to_row, to_column).astype(BF16)
-        back_ref[:, source * LANES : (source + 1) * LANES] = found
-        shape = (LANES, sizes.ch * sizes.cap)
-        moved = hot(
-            (iota(shape, 1) == iota(shape, 0) + source * sizes.cap)
-            & (iota(shape, 0) < sizes.cap)
-        )
-        into = into + dot(found, moved)
-    into_ref[...] = into.astype(BF16)
+        at = slice(source * LANES, (source + 1) * LANES)
+        back_ref[:, at] = dot_lanes(to_row, to_column).astype(BF16)
 
     modes = leap_ref.shape[0]
     terms = three_terms(param_ref[...])
@@ -487,7 +478,6 @@
         in_specs=[pl.BlockSpec(memory_space=pltpu.SMEM)]
         + [pl.BlockSpec(memory_space=pltpu.VMEM)] * 3,
         out_shape=[
-            jax.ShapeDtypeStruct((256, sizes.ch * sizes.cap), BF16),
             jax.ShapeDtypeStruct((256, sizes.ch * LANES), BF16),
             jax.ShapeDtypeStruct((8, LANES), I32),
             jax.ShapeDtypeStruct((256, 2 * sizes.run), BF16),
@@ -577,7 +567,6 @@
 def owner_kernel(
     sizes,
     recv_ref,
-    into_ref,
     back_ref,
     table_ref,
     leap_ref,
@@ -597,9 +586,12 @@
         run_at[2 * source] = tail[15, 0].astype(I32)
         run_at[2 * source + 1] = tail[15, LANES].astype(I32)
     lane = iota((rows, LANES), 1)
+    nothing = jnp.zeros((sizes.rest, 2 * LANES), BF16)
     for source in range(sizes.ctx):
-        block = recv_ref[source * sizes.ch : (source + 1) * sizes.ch]
-        found = dot(into_ref[...], block.reshape(sizes.ch * sizes.cap, 2 * LANES))
+        block = []
+        for peer in range(source * sizes.ch, (source + 1) * sizes.ch):
+            block += [recv_ref[peer], nothing]
+        found = dot(back_ref[...], jnp.concatenate(block, axis=0))
         found = found.astype(BF16)
         value = found[:, :LANES]
         turned = pltpu.roll(value, run, 1)
@@ -683,12 +675,12 @@
             ).astype(BF16)
 
 
-def owner(sizes, recv, into, back, table, leap):
+def owner(sizes, recv, back, table, leap):
     rows = sizes.own * sizes.size
     modes = leap.shape[0]
     return pl.pallas_call(
         functools.partial(owner_kernel, sizes),
-        in_specs=[pl.BlockSpec(memory_space=pltpu.VMEM)] * 5,
+        in_specs=[pl.BlockSpec(memory_space=pltpu.VMEM)] * 4,
         out_shape=jax.ShapeDtypeStruct((sizes.peers, 2 * modes - 8, LANES), BF16),
         scratch_shapes=[
             pltpu.VMEM((sizes.ctx, 4, rows, LANES), BF16),
@@ -700,7 +692,7 @@
         ],
         compiler_params=pltpu.CompilerParams(vmem_limit_bytes=VMEM_LIMIT),
         name="owner_sums",
-    )(recv, into, back, table, leap)
+    )(recv, back, table, leap)
 
 
 def finish_kernel(
@@ -817,13 +809,13 @@
     gains = residues * jnp.sqrt(2.0 * decay_rates)
     params = jnp.concatenate([decay_rates, gains], axis=1).T
     conv, decay = local(sizes, me, groups, params, key_proj, value_proj)
-    into, back, most, table, leap = index(sizes, me, groups, dest, params)
-
-    def fast(recv, into, back, table, leap, dest, conv, decay, *args):
-        returned = exchange(owner(sizes, recv, into, back, table, leap))
+    back, most, table, leap = index(sizes, me, groups, dest, params)
+
+    def fast(recv, back, table, leap, dest, conv, decay, *args):
+        returned = exchange(owner(sizes, recv, back, table, leap))
         return tuple(finish(sizes, returned, dest, conv, decay, args[0]))
 
-    def slow(recv, into, back, table, leap, dest, conv, decay, *args):
+    def slow(recv, back, table, leap, dest, conv, decay, *args):
         return general_way(*args)
 
     return lax.cond(
@@ -831,7 +823,6 @@
         fast,
         slow,
         recv,
-        into,
         back,
         table,
         leap,

time: 67.3 us -> 67.3 us (level)
  Pallas kernels: 26.1 us -> 24.1 us
  waiting for transfers between devices: 18.1 us -> 20 us
    all_to_all x1, waiting for transfers between devices: 18.1 us -> 20 us  [exchange(): lax.all_to_all(blocks, ('ctx', 'ch'), split_axis=0, concat_axis=0, tiled=...]
    pallas_call x1, Pallas kernels: 4.88 us -> 2.99 us  [index(): pl.pallas_call(functools.partial(index_kernel, sizes), in_specs=[pl.Block...]
  transfers between devices with their start and end apart: 1 -> 1, of which waited for: 1 -> 1; matrix products, arithmetic and copies ran while one was open for 1% -> 1% of each run, Pallas kernels for 17% -> 14%
where the time goes in v6:
time: 67.3 us; the launch traced here: 67 us
  Pallas kernels  24.1 us (36%)
  waiting for transfers between devices  20 us (30%)
  blocking collectives  13.5 us (20%)
  starting transfers between devices  7.1 us (11%)
  between operations  1.44 us (2%)
    all_to_all x1, waiting for transfers between devices, exchange(): lax.all_to_all(blocks, ('ctx', 'ch'), split_axis=0, concat_axis=0, tiled=...  20 us
    all_to_all x1, blocking collectives, exchange(): lax.all_to_all(blocks, ('ctx', 'ch'), split_axis=0, concat_axis=0, tiled=...  13.5 us
    all_to_all x1, starting transfers between devices, exchange(): lax.all_to_all(blocks, ('ctx', 'ch'), split_axis=0, concat_axis=0, tiled=...  7.1 us
    pallas_call x1, Pallas kernels, local(): pl.pallas_call(functools.partial(local_kernel, sizes), in_specs=[pl.Block...  6.72 us
    pallas_call x1, Pallas kernels, pack(): pl.pallas_call(functools.partial(pack_kernel, sizes), in_specs=[pl.BlockS...  6.3 us
    pallas_call x1, Pallas kernels, owner(): pl.pallas_call(functools.partial(owner_kernel, sizes), in_specs=[pl.Block...  4.72 us
    pallas_call x1, Pallas kernels, finish(): pl.pallas_call(functools.partial(finish_kernel, sizes), in_specs=[pl.Bloc...  3.38 us
    pallas_call x1, Pallas kernels, index(): pl.pallas_call(functools.partial(index_kernel, sizes), in_specs=[pl.Block...  2.99 us
  transfers between devices with their start and end apart: 1, of which 1 were waited for; matrix products, arithmetic and copies ran while one was open for 1% of the time, Pallas kernels for 14%

profile of v6, /device:TPU:1, one launch (start us, length us, event | category | flops | bytes accessed | tf_op | source)
XLA Modules:
  0.0 67.0 jit_solution(4829493251244910820)
XLA Ops:
  0.6 0.0 copy-start.9
  0.6 0.0 copy-start.10
  0.7 0.0 copy-start.14
  0.7 6.3 %pack_rows.1 = (bf16[32,80,256]{2,1,0:T(8,128)(2,1)}, s32[8,2048]{1,0:T(8,128)S(1)}) custom-call(s32[128]{0:T(128)} %place_hbm.1, s32[1,8192]{1,0:T(1,128)} %bitcast.172, bf16[2048,128]{1,0:T(8,128)(2,1)} %key_ref.1, bf16[2048,128]{1,0:T(8,128)(2,1)} %value_ref.1, bf16[2048,128]{1,0:T(8,128)(2,1)} %cot_hbm.1, bf16[2048,128]{1,0:T(8,128)(2,1)} %query_hbm.1), custom_call_target="tpu_custom_call" | custom-call | tf_op jit(solution)/shard_map/pack_rows/pallas_call | solution.py:385
  7.0 0.0 copy-start.12
  7.0 7.1 %all-to-all-start.7 = ((bf16[32,80,256]{2,1,0:T(8,128)(2,1)}), bf16[32,80,256]{2,1,0:T(8,128)(2,1)S(1)}, u32[]{:S(2)}, u32[]{:S(2)}) async-start(bf16[32,80,256]{2,1,0:T(8,128)(2,1)} %get-tuple-element.60), calls=%async_computation.7 | async-start | bytes 2621440 | tf_op jit(solution)/shard_map/all_to_all | solution.py:799
  14.1 0.0 copy-done.9
  14.1 0.0 copy-done.10
  14.1 0.0 copy-done.14
  14.2 0.0 copy-start.5
  14.2 0.0 copy-start.6
  14.2 3.0 %index_rows.1 = (bf16[256,512]{1,0:T(8,128)(2,1)}, s32[8,128]{1,0:T(8,128)S(1)}, bf16[256,128]{1,0:T(8,128)(2,1)}, f32[16,256]{1,0:T(8,128)S(1)}) custom-call(s32[1]{0:T(128)} %bitcast.46.me_ref, s32[1,8192]{1,0:T(1,128)S(1)} %bitcast.173, s32[8,2048]{1,0:T(8,128)S(1)} %get-tuple-element.58.dest_ref, f32[32,512]{1,0:T(8,128)S(1)} %maximum_bitcast_fusion.param_ref), custom_call_target="tpu_custom_call" | custom-call | flops 2000000000 | bytes 1000000 | tf_op jit(solution)/shard_map/index_rows/pallas_call | solution.py:476
  17.2 0.0 copy-done.12
  17.2 0.5 slice.39
  18.3 0.0 copy-done.5
  18.3 0.0 copy-done.6
  18.4 0.0 copy-start.3
  18.4 0.0 copy-start.7
  18.4 0.0 copy-start.16
  18.4 6.7 %local_runs.1 = (f32[2048,128]{1,0:T(8,128)}, f32[256,128]{1,0:T(8,128)}) custom-call(s32[1]{0:T(128)} %bitcast.46.me_ref, s32[1,8192]{1,0:T(1,128)S(1)} %bitcast.174, f32[32,512]{1,0:T(8,128)S(1)} %maximum_bitcast_fusion.param_ref, bf16[2048,128]{1,0:T(8,128)(2,1)S(1)} %copy-done.5, bf16[2048,128]{1,0:T(8,128)(2,1)S(1)} %copy-done.6), custom_call_target="tpu_custom_call" | custom-call | flops 4000000000 | bytes 3000000 | tf_op jit(solution)/shard_map/local_runs/pallas_call | solution.py:549
  25.1 20.0 %all-to-all-done.7 = bf16[32,80,256]{2,1,0:T(8,128)(2,1)S(1)} async-done(((bf16[32,80,256]{2,1,0:T(8,128)(2,1)}), bf16[32,80,256]{2,1,0:T(8,128)(2,1)S(1)}, u32[]{:S(2)}, u32[]{:S(2)}) %all-to-all-start.7) | async-done | bytes 1310752 | tf_op jit(solution)/shard_map/all_to_all | solution.py:799
  45.1 0.0 copy-done.3
  45.1 0.0 copy-done.7
  45.1 21.9 %conditional.1 = ((bf16[2048,128]{1,0:T(8,128)(2,1)}, f32[128,128]{1,0:T(8,128)})) conditional(s32[]{:T(128)} %bitcast.49, (bf16[2048,128]{1,0:T(8,128)(2,1)S(1)}, s32[8192]{0:T(1024)S(1)}, f32[512,16]{0,1:T(8,128)S(1)}, f32[512,16]{0,1:T(8,128)S(1)}, bf16[2048,128]{1,0:T(8,128)(2,1)S(1)}, /*index=5*/bf16[2048,128]{1,0:T(8,128)(2,1)S(1)}, ...), branch_computations={%region_0.4_spmd, %region_4.5_spmd} | conditional | flops 10720338944 | bytes 257407616 | solution.py:821
  45.3 0.0 copy-start.8
  45.3 0.0 copy-start.11
  45.3 0.0 copy-start.13
  45.4 4.7 %owner_sums.1 = bf16[32,24,128]{2,1,0:T(8,128)(2,1)S(1)} custom-call(bf16[32,80,256]{2,1,0:T(8,128)(2,1)S(1)} %get-tuple-element.40.recv_ref, bf16[256,512]{1,0:T(8,128)(2,1)} %get-tuple-element.41.back_ref, bf16[256,128]{1,0:T(8,128)(2,1)} %get-tuple-element.42.table_ref, f32[16,256]{1,0:T(8,128)S(1)} %get-tuple-element.43.leap_ref), custom_call_target="tpu_custom_call" | custom-call | tf_op jit(solution)/shard_map/cond/branch_1_fun/owner_sums/pallas_call | solution.py:681
  50.1 13.5 %all_to_all.68.recv_ref = bf16[32,24,128]{2,1,0:T(8,128)(2,1)S(1)} all-to-all(bf16[32,24,128]{2,1,0:T(8,128)(2,1)S(1)} %owner_sums.1), channel_id=1, replica_groups=mesh['ctx'=8,'ch'=4] {'ctx','ch'}, dimensions={0} | all-to-all | bytes 393216 | tf_op jit(solution)/shard_map/cond/branch_1_fun/all_to_all | solution.py:799
  63.6 0.0 copy-done.8
  63.6 0.0 copy-done.13
  63.6 3.4 %finish_rows.1 = (bf16[2048,128]{1,0:T(8,128)(2,1)}, f32[128,128]{1,0:T(8,128)}) custom-call(bf16[32,24,128]{2,1,0:T(8,128)(2,1)S(1)} %all_to_all.68.recv_ref, s32[8,2048]{1,0:T(8,128)S(1)} %copy-done.13, f32[2048,128]{1,0:T(8,128)S(1)} %copy-done.8, f32[256,128]{1,0:T(8,128)S(1)} %copy-done.11, bf16[2048,128]{1,0:T(8,128)(2,1)S(1)} %get-tuple-element.47.query_ref), custom_call_target="tpu_custom_call" | custom-call | tf_op jit(solution)/shard_map/cond/branch_1_fun/finish_rows/pallas_call | solution.py:782
  (4 shorter events, 0.0 us)
Async XLA Ops:
  0.6 13.5 %copy-start.9 = (f32[512,16]{0,1:T(8,128)S(1)}, f32[512,16]{0,1:T(8,128)}, u32[]{:S(2)}) copy-start(f32[512,16]{0,1:T(8,128)} %param.16) | copy-start | bytes 98308
  0.6 13.5 %copy-start.10 = (f32[512,16]{0,1:T(8,128)S(1)}, f32[512,16]{0,1:T(8,128)}, u32[]{:S(2)}) copy-start(f32[512,16]{0,1:T(8,128)} %param.17) | copy-start | bytes 98308
  0.7 13.5 %copy-start.14 = (s32[8192]{0:T(1024)S(1)}, s32[8192]{0:T(1024)}, u32[]{:S(2)}) copy-start(s32[8192]{0:T(1024)} %param.15) | copy-start | bytes 98308
  7.0 10.2 %copy-start.12 = (s32[8,2048]{1,0:T(8,128)}, s32[8,2048]{1,0:T(8,128)S(1)}, u32[]{:S(2)}) copy-start(s32[8,2048]{1,0:T(8,128)S(1)} %get-tuple-element.58.dest_ref) | copy-start | bytes 196612
  7.0 38.1 %all-to-all-start.7 = ((bf16[32,80,256]{2,1,0:T(8,128)(2,1)}), bf16[32,80,256]{2,1,0:T(8,128)(2,1)S(1)}, u32[]{:S(2)}, u32[]{:S(2)}) async-start(bf16[32,80,256]{2,1,0:T(8,128)(2,1)} %get-tuple-element.60), calls=%async_computation.7 | async-start | bytes 2621440 | tf_op jit(solution)/shard_map/all_to_all | solution.py:799
  14.2 4.2 %copy-start.5 = (bf16[2048,128]{1,0:T(8,128)(2,1)S(1)}, bf16[2048,128]{1,0:T(8,128)(2,1)}, u32[]{:S(2)}) copy-start(bf16[2048,128]{1,0:T(8,128)(2,1)} %key_ref.1) | copy-start | bytes 1572868
  14.2 4.2 %copy-start.6 = (bf16[2048,128]{1,0:T(8,128)(2,1)S(1)}, bf16[2048,128]{1,0:T(8,128)(2,1)}, u32[]{:S(2)}) copy-start(bf16[2048,128]{1,0:T(8,128)(2,1)} %value_ref.1) | copy-start | bytes 1572868
  18.4 26.7 %copy-start.3 = (bf16[2048,128]{1,0:T(8,128)(2,1)S(1)}, bf16[2048,128]{1,0:T(8,128)(2,1)}, u32[]{:S(2)}) copy-start(bf16[2048,128]{1,0:T(8,128)(2,1)} %query_hbm.1) | copy-start | bytes 1572868
  18.4 26.7 %copy-start.7 = (bf16[2048,128]{1,0:T(8,128)(2,1)S(1)}, bf16[2048,128]{1,0:T(8,128)(2,1)}, u32[]{:S(2)}) copy-start(bf16[2048,128]{1,0:T(8,128)(2,1)} %cot_hbm.1) | copy-start | bytes 1572868
  18.4 26.7 %copy-start.16 = (s32[128]{0:T(128)S(1)}, s32[128]{0:T(128)}, u32[]{:S(2)}) copy-start(s32[128]{0:T(128)} %place_hbm.1) | copy-start | bytes 1540
  45.3 18.3 %copy-start.8 = (f32[2048,128]{1,0:T(8,128)S(1)}, f32[2048,128]{1,0:T(8,128)}, u32[]{:S(2)}) copy-start(f32[2048,128]{1,0:T(8,128)} %get-tuple-element.45.conv_ref) | copy-start | bytes 3145732 | tf_op jit(solution)/shard_map/cond
  45.3 18.3 %copy-start.11 = (f32[256,128]{1,0:T(8,128)S(1)}, f32[256,128]{1,0:T(8,128)}, u32[]{:S(2)}) copy-start(f32[256,128]{1,0:T(8,128)} %get-tuple-element.46.decay_ref) | copy-start | bytes 393220 | tf_op jit(solution)/shard_map/cond
  45.3 18.3 %copy-start.13 = (s32[8,2048]{1,0:T(8,128)S(1)}, s32[8,2048]{1,0:T(8,128)}, u32[]{:S(2)}) copy-start(s32[8,2048]{1,0:T(8,128)} %get-tuple-element.44.dest_ref) | copy-start | bytes 196612 | tf_op jit(solution)/shard_map/cond

commit v7 on v6

--- a/solution.py
+++ b/solution.py
@@ -696,7 +696,18 @@
 
 
 def finish_kernel(
-    sizes, recv_ref, dest_ref, conv_ref, decay_ref, query_ref, out_ref, grad_ref, found, total
+    sizes,
+    recv_ref,
+    dest_ref,
+    conv_ref,
+    decay_ref,
+    query_ref,
+    out_hbm,
+    grad_ref,
+    found,
+    total,
+    out_ref,
+    left,
 ):
     blocks = sizes.channels // LANES
     wide = recv_ref.shape[1]
@@ -734,6 +745,7 @@
         conv = total[pl.ds(block, sizes.tokens, stride=blocks), :].astype(BF16).T
         out_ref[at, :] = (query_ref[at, :].astype(F32) * conv.astype(F32)).astype(BF16)
 
+    copies = []
     for first in range(0, blocks, 8):
         for part in range(first // 2, first // 2 + 4):
             fetch(part)
@@ -757,6 +769,11 @@
             lax.fori_loop(0, sizes.run, step, states, unroll=True)
         for block in range(first, first + 8):
             turn(block)
+        at = pl.ds(first * LANES, 8 * LANES)
+        copies.append(
+            pltpu.make_async_copy(out_ref.at[at], out_hbm.at[at], left.at[first // 8])
+        )
+        copies[-1].start()
 
     each, few_lags = sizes.each, LANES // 2 - rest
     shape = (sizes.peers * 8, LANES)
@@ -775,6 +792,8 @@
     wanted = sizes.group_at(seat, way_of(dest_ref))
     chosen = hot(iota((sizes.block, sizes.peers * 8), 0) == wanted)
     grad_ref[...] = dot(chosen, placed.astype(BF16))
+    for copy in copies:
+        copy.wait()
 
 
 def finish(sizes, recv, dest, conv, decay, query_proj):
@@ -782,6 +801,10 @@
     return pl.pallas_call(
         functools.partial(finish_kernel, sizes),
         in_specs=[pl.BlockSpec(memory_space=pltpu.VMEM)] * 5,
+        out_specs=[
+            pl.BlockSpec(memory_space=pltpu.HBM),
+            pl.BlockSpec(memory_space=pltpu.VMEM),
+        ],
         out_shape=[
             jax.ShapeDtypeStruct((sizes.channels, sizes.tokens), BF16),
             jax.ShapeDtypeStruct((sizes.block, LANES), F32),
@@ -789,6 +812,8 @@
         scratch_shapes=[
             pltpu.VMEM(((blocks + 1) * (recv.shape[1] + 8), LANES), F32),
             pltpu.VMEM(((sizes.tokens + 1) * blocks, LANES), F32),
+            pltpu.VMEM(query_proj.shape, BF16),
+            pltpu.SemaphoreType.DMA((blocks // 8,)),
         ],
         compiler_params=pltpu.CompilerParams(vmem_limit_bytes=VMEM_LIMIT),
         name="finish_rows",

time: 67.3 us -> 68 us (1.010)
  no operation moved by 1% of the time
where the time goes in v7:
time: 68 us; the launch traced here: 67.7 us
  Pallas kernels  24.7 us (36%)
  waiting for transfers between devices  20 us (29%)
  blocking collectives  13.5 us (20%)
  starting transfers between devices  7.1 us (10%)
  between operations  1.62 us (2%)
    all_to_all x1, waiting for transfers between devices, exchange(): lax.all_to_all(blocks, ('ctx', 'ch'), split_axis=0, concat_axis=0, tiled=...  20 us
    all_to_all x1, blocking collectives, exchange(): lax.all_to_all(blocks, ('ctx', 'ch'), split_axis=0, concat_axis=0, tiled=...  13.5 us
    all_to_all x1, starting transfers between devices, exchange(): lax.all_to_all(blocks, ('ctx', 'ch'), split_axis=0, concat_axis=0, tiled=...  7.1 us
    pallas_call x1, Pallas kernels, local(): pl.pallas_call(functools.partial(local_kernel, sizes), in_specs=[pl.Block...  6.72 us
    pallas_call x1, Pallas kernels, pack(): pl.pallas_call(functools.partial(pack_kernel, sizes), in_specs=[pl.BlockS...  6.3 us
    pallas_call x1, Pallas kernels, owner(): pl.pallas_call(functools.partial(owner_kernel, sizes), in_specs=[pl.Block...  4.72 us
    pallas_call x1, Pallas kernels, finish(): pl.pallas_call(functools.partial(finish_kernel, sizes), in_specs=[pl.Bloc...  3.94 us
    pallas_call x1, Pallas kernels, index(): pl.pallas_call(functools.partial(index_kernel, sizes), in_specs=[pl.Block...  2.99 us
  transfers between devices with their start and end apart: 1, of which 1 were waited for; matrix products, arithmetic and copies ran while one was open for 1% of the time, Pallas kernels for 14%

profile of v7, /device:TPU:1, one launch (start us, length us, event | category | flops | bytes accessed | tf_op | source)
XLA Modules:
  0.0 67.7 jit_solution(1110004047294726062)
XLA Ops:
  0.6 0.0 copy-start.9
  0.6 0.0 copy-start.10
  0.7 0.0 copy-start.14
  0.7 6.3 %pack_rows.1 = (bf16[32,80,256]{2,1,0:T(8,128)(2,1)}, s32[8,2048]{1,0:T(8,128)S(1)}) custom-call(s32[128]{0:T(128)} %place_hbm.1, s32[1,8192]{1,0:T(1,128)} %bitcast.172, bf16[2048,128]{1,0:T(8,128)(2,1)} %key_ref.1, bf16[2048,128]{1,0:T(8,128)(2,1)} %value_ref.1, bf16[2048,128]{1,0:T(8,128)(2,1)} %cot_hbm.1, bf16[2048,128]{1,0:T(8,128)(2,1)} %query_hbm.1), custom_call_target="tpu_custom_call" | custom-call | tf_op jit(solution)/shard_map/pack_rows/pallas_call | solution.py:385
  7.0 0.0 copy-start.12
  7.0 7.1 %all-to-all-start.7 = ((bf16[32,80,256]{2,1,0:T(8,128)(2,1)}), bf16[32,80,256]{2,1,0:T(8,128)(2,1)S(1)}, u32[]{:S(2)}, u32[]{:S(2)}) async-start(bf16[32,80,256]{2,1,0:T(8,128)(2,1)} %get-tuple-element.60), calls=%async_computation.7 | async-start | bytes 2621440 | tf_op jit(solution)/shard_map/all_to_all | solution.py:824
  14.1 0.0 copy-done.9
  14.1 0.0 copy-done.10
  14.1 0.0 copy-done.14
  14.2 0.0 copy-start.5
  14.2 0.0 copy-start.6
  14.2 3.0 %index_rows.1 = (bf16[256,512]{1,0:T(8,128)(2,1)}, s32[8,128]{1,0:T(8,128)S(1)}, bf16[256,128]{1,0:T(8,128)(2,1)}, f32[16,256]{1,0:T(8,128)S(1)}) custom-call(s32[1]{0:T(128)} %bitcast.46.me_ref, s32[1,8192]{1,0:T(1,128)S(1)} %bitcast.173, s32[8,2048]{1,0:T(8,128)S(1)} %get-tuple-element.58.dest_ref, f32[32,512]{1,0:T(8,128)S(1)} %maximum_bitcast_fusion.param_ref), custom_call_target="tpu_custom_call" | custom-call | flops 2000000000 | bytes 1000000 | tf_op jit(solution)/shard_map/index_rows/pallas_call | solution.py:476
  17.2 0.0 copy-done.12
  17.2 0.5 slice.39
  18.3 0.0 copy-done.5
  18.3 0.0 copy-done.6
  18.4 0.0 copy-start.3
  18.4 0.0 copy-start.7
  18.4 0.0 copy-start.16
  18.4 6.7 %local_runs.1 = (f32[2048,128]{1,0:T(8,128)}, f32[256,128]{1,0:T(8,128)}) custom-call(s32[1]{0:T(128)} %bitcast.46.me_ref, s32[1,8192]{1,0:T(1,128)S(1)} %bitcast.174, f32[32,512]{1,0:T(8,128)S(1)} %maximum_bitcast_fusion.param_ref, bf16[2048,128]{1,0:T(8,128)(2,1)S(1)} %copy-done.5, bf16[2048,128]{1,0:T(8,128)(2,1)S(1)} %copy-done.6), custom_call_target="tpu_custom_call" | custom-call | flops 4000000000 | bytes 3000000 | tf_op jit(solution)/shard_map/local_runs/pallas_call | solution.py:549
  25.1 20.0 %all-to-all-done.7 = bf16[32,80,256]{2,1,0:T(8,128)(2,1)S(1)} async-done(((bf16[32,80,256]{2,1,0:T(8,128)(2,1)}), bf16[32,80,256]{2,1,0:T(8,128)(2,1)S(1)}, u32[]{:S(2)}, u32[]{:S(2)}) %all-to-all-start.7) | async-done | bytes 1310752 | tf_op jit(solution)/shard_map/all_to_all | solution.py:824
  45.1 0.0 copy-done.3
  45.1 0.0 copy-done.7
  45.1 0.0 copy-done.16
  45.1 22.5 %conditional.1 = ((bf16[2048,128]{1,0:T(8,128)(2,1)}, f32[128,128]{1,0:T(8,128)})) conditional(s32[]{:T(128)} %bitcast.49, (bf16[2048,128]{1,0:T(8,128)(2,1)S(1)}, s32[8192]{0:T(1024)S(1)}, f32[512,16]{0,1:T(8,128)S(1)}, f32[512,16]{0,1:T(8,128)S(1)}, bf16[2048,128]{1,0:T(8,128)(2,1)S(1)}, /*index=5*/bf16[2048,128]{1,0:T(8,128)(2,1)S(1)}, ...), branch_computations={%region_0.4_spmd, %region_4.5_spmd} | conditional | flops 10720338944 | bytes 257407616 | solution.py:846
  45.3 0.0 copy-start.8
  45.3 0.0 copy-start.11
  45.3 0.0 copy-start.13
  45.4 4.7 %owner_sums.1 = bf16[32,24,128]{2,1,0:T(8,128)(2,1)S(1)} custom-call(bf16[32,80,256]{2,1,0:T(8,128)(2,1)S(1)} %get-tuple-element.40.recv_ref, bf16[256,512]{1,0:T(8,128)(2,1)} %get-tuple-element.41.back_ref, bf16[256,128]{1,0:T(8,128)(2,1)} %get-tuple-element.42.table_ref, f32[16,256]{1,0:T(8,128)S(1)} %get-tuple-element.43.leap_ref), custom_call_target="tpu_custom_call" | custom-call | tf_op jit(solution)/shard_map/cond/branch_1_fun/owner_sums/pallas_call | solution.py:681
  50.1 13.5 %all_to_all.68.recv_ref = bf16[32,24,128]{2,1,0:T(8,128)(2,1)S(1)} all-to-all(bf16[32,24,128]{2,1,0:T(8,128)(2,1)S(1)} %owner_sums.1), channel_id=1, replica_groups=mesh['ctx'=8,'ch'=4] {'ctx','ch'}, dimensions={0} | all-to-all | bytes 393216 | tf_op jit(solution)/shard_map/cond/branch_1_fun/all_to_all | solution.py:824
  63.6 0.0 copy-done.8
  63.6 3.9 %finish_rows.1 = (bf16[2048,128]{1,0:T(8,128)(2,1)}, f32[128,128]{1,0:T(8,128)}) custom-call(bf16[32,24,128]{2,1,0:T(8,128)(2,1)S(1)} %all_to_all.68.recv_ref, s32[8,2048]{1,0:T(8,128)S(1)} %copy-done.13, f32[2048,128]{1,0:T(8,128)S(1)} %copy-done.8, f32[256,128]{1,0:T(8,128)S(1)} %copy-done.11, bf16[2048,128]{1,0:T(8,128)(2,1)S(1)} %get-tuple-element.47.query_ref), custom_call_target="tpu_custom_call" | custom-call | tf_op jit(solution)/shard_map/cond/branch_1_fun/finish_rows/pallas_call | solution.py:801
  (4 shorter events, 0.0 us)
Async XLA Ops:
  0.6 13.5 %copy-start.9 = (f32[512,16]{0,1:T(8,128)S(1)}, f32[512,16]{0,1:T(8,128)}, u32[]{:S(2)}) copy-start(f32[512,16]{0,1:T(8,128)} %param.16) | copy-start | bytes 98308
  0.6 13.5 %copy-start.10 = (f32[512,16]{0,1:T(8,128)S(1)}, f32[512,16]{0,1:T(8,128)}, u32[]{:S(2)}) copy-start(f32[512,16]{0,1:T(8,128)} %param.17) | copy-start | bytes 98308
  0.7 13.5 %copy-start.14 = (s32[8192]{0:T(1024)S(1)}, s32[8192]{0:T(1024)}, u32[]{:S(2)}) copy-start(s32[8192]{0:T(1024)} %param.15) | copy-start | bytes 98308
  7.0 10.2 %copy-start.12 = (s32[8,2048]{1,0:T(8,128)}, s32[8,2048]{1,0:T(8,128)S(1)}, u32[]{:S(2)}) copy-start(s32[8,2048]{1,0:T(8,128)S(1)} %get-tuple-element.58.dest_ref) | copy-start | bytes 196612
  7.0 38.1 %all-to-all-start.7 = ((bf16[32,80,256]{2,1,0:T(8,128)(2,1)}), bf16[32,80,256]{2,1,0:T(8,128)(2,1)S(1)}, u32[]{:S(2)}, u32[]{:S(2)}) async-start(bf16[32,80,256]{2,1,0:T(8,128)(2,1)} %get-tuple-element.60), calls=%async_computation.7 | async-start | bytes 2621440 | tf_op jit(solution)/shard_map/all_to_all | solution.py:824
  14.2 4.2 %copy-start.5 = (bf16[2048,128]{1,0:T(8,128)(2,1)S(1)}, bf16[2048,128]{1,0:T(8,128)(2,1)}, u32[]{:S(2)}) copy-start(bf16[2048,128]{1,0:T(8,128)(2,1)} %key_ref.1) | copy-start | bytes 1572868
  14.2 4.2 %copy-start.6 = (bf16[2048,128]{1,0:T(8,128)(2,1)S(1)}, bf16[2048,128]{1,0:T(8,128)(2,1)}, u32[]{:S(2)}) copy-start(bf16[2048,128]{1,0:T(8,128)(2,1)} %value_ref.1) | copy-start | bytes 1572868
  18.4 26.7 %copy-start.3 = (bf16[2048,128]{1,0:T(8,128)(2,1)S(1)}, bf16[2048,128]{1,0:T(8,128)(2,1)}, u32[]{:S(2)}) copy-start(bf16[2048,128]{1,0:T(8,128)(2,1)} %query_hbm.1) | copy-start | bytes 1572868
  18.4 26.7 %copy-start.7 = (bf16[2048,128]{1,0:T(8,128)(2,1)S(1)}, bf16[2048,128]{1,0:T(8,128)(2,1)}, u32[]{:S(2)}) copy-start(bf16[2048,128]{1,0:T(8,128)(2,1)} %cot_hbm.1) | copy-start | bytes 1572868
  18.4 26.7 %copy-start.16 = (s32[128]{0:T(128)S(1)}, s32[128]{0:T(128)}, u32[]{:S(2)}) copy-start(s32[128]{0:T(128)} %place_hbm.1) | copy-start | bytes 1540
  45.3 18.3 %copy-start.8 = (f32[2048,128]{1,0:T(8,128)S(1)}, f32[2048,128]{1,0:T(8,128)}, u32[]{:S(2)}) copy-start(f32[2048,128]{1,0:T(8,128)} %get-tuple-element.45.conv_ref) | copy-start | bytes 3145732 | tf_op jit(solution)/shard_map/cond
  45.3 18.3 %copy-start.11 = (f32[256,128]{1,0:T(8,128)S(1)}, f32[256,128]{1,0:T(8,128)}, u32[]{:S(2)}) copy-start(f32[256,128]{1,0:T(8,128)} %get-tuple-element.46.decay_ref) | copy-start | bytes 393220 | tf_op jit(solution)/shard_map/cond
  45.3 18.3 %copy-start.13 = (s32[8,2048]{1,0:T(8,128)S(1)}, s32[8,2048]{1,0:T(8,128)}, u32[]{:S(2)}) copy-start(s32[8,2048]{1,0:T(8,128)} %get-tuple-element.44.dest_ref) | copy-start | bytes 196612 | tf_op jit(solution)/shard_map/cond
